TPU v7x, 768 devices: a whole 4x8x12 slice. The times are simulated.
768 devices in a mesh: row: 24 (over x_hi, z), col: 32 (over y, x_lo, core).
Axes of the slice: x: 4 (x_hi: 2, x_lo: 2; x = x_hi * 2 + x_lo), y: 8, z: 12, core: 2. Of those that a mesh axis runs over, the one named last changes fastest.
Arguments:
- amplitudes: bfloat16 [2, 4608, 16384], P(None, 'row', 'col'), may hold values from -6 to 6
- integrals: bfloat16 [2, 16384, 6144], P(None, 'col', 'row'), may hold values from -0.03125 to 0.03125
- amp_mask: int32 [2, 72, 256], P(None, 'row', 'col'), may hold values 0 or 1
- int_mask: int32 [2, 256, 96], P(None, 'col', 'row'), may hold values 0 or 1
- owners: int32 [72], replicated, may hold values from 0 to 31, as said below
Outputs:
- residual_tiles: float32 [32, 3, 64, 6144], P('col', None, None, 'row')
Inputs may be any that keep to these rules, and one draw needn't show every extreme that they name: `owners`: each index of col owns at most 3 tiles, and some index owns exactly 3; indices 0 and 31 own at least one tile.
All inputs are finite; a program needn't handle non-finite values. No bound on the sum of `amp_mask` or of `int_mask` on one device may be relied on, other than what follows from the above.
Results may differ from a plain program's by a relative error of at most 0.015.
Values may be sent and summed in bfloat16 or wider, within the bound.
No kernel may reach another device: no remote copies, remote signals or barrier semaphores. Data moves between devices by JAX's collectives and lax.ppermute only.
A program may use at most 64 MiB of HBM per device.

v0:
```python
import jax
import jax.numpy as jnp
from jax import lax
from jax.sharding import PartitionSpec as P


def expand(mask, tile_edge, dtype):
    grown = jnp.repeat(jnp.repeat(mask, tile_edge, axis=-2), tile_edge, axis=-1)
    return grown.astype(dtype)


def body(amplitudes, integrals, amp_mask, int_mask, owners):
    tile_edge = amplitudes.shape[1] // amp_mask.shape[1]
    col_count = lax.axis_size("col")
    amp_used = amplitudes * expand(amp_mask, tile_edge, amplitudes.dtype)
    int_used = integrals * expand(int_mask, tile_edge, integrals.dtype)
    panels = amplitudes.shape[0]
    local_cols = integrals.shape[2]
    partial_value = None
    for panel_index in range(panels):
        int_panel = int_used[panel_index]
        term = jnp.dot(
            lax.all_gather(amp_used[panel_index], "row", axis=0, tiled=True),
            int_panel,
            preferred_element_type=jnp.float32,
        )
        partial_value = term if partial_value is None else partial_value + term
    tile_data = partial_value.astype(jnp.bfloat16)
    tile_total = owners.shape[0]
    capacity = tile_total // col_count + 1
    positions = jnp.arange(tile_total, dtype=jnp.int32)
    same_owner = owners[:, None] == owners[None, :]
    earlier = positions[:, None] > positions[None, :]
    slot_index = jnp.sum((same_owner & earlier).astype(jnp.int32), axis=1)
    destination = owners * capacity + slot_index
    targets = jnp.arange(col_count * capacity, dtype=jnp.int32)
    selector = (targets[:, None] == destination[None, :]).astype(jnp.bfloat16)
    tile_rows = tile_data.reshape(tile_total, tile_edge, local_cols)
    send_buffer = jnp.einsum(
        "dt,tiw->diw", selector, tile_rows, preferred_element_type=jnp.bfloat16
    )
    received = lax.all_to_all(send_buffer, "col", split_axis=0, concat_axis=0, tiled=True)
    summed = jnp.sum(
        received.astype(jnp.float32).reshape(col_count, capacity, tile_edge, local_cols), axis=0
    )
    return summed.reshape(1, capacity, tile_edge, local_cols)


def solution(mesh):
    in_specs = (
        P(None, "row", "col"),
        P(None, "col", "row"),
        P(None, "row", "col"),
        P(None, "col", "row"),
        P(),
    )
    out_specs = P("col", None, None, "row")
    return jax.shard_map(body, mesh=mesh, in_specs=in_specs, out_specs=out_specs, check_vma=False)
```

profile of v0, /device:TPU:1, one launch (start us, length us, event | category | flops | bytes accessed | tf_op | source)
XLA Modules:
  0.0 403.6 jit_solution(4471260027905137144)
XLA Ops:
  6.5 0.0 copy-start
  6.5 0.0 copy-start.1
  6.5 0.0 copy-start.2
  6.5 0.0 all-gather.5.cloned.1.call-start
  6.5 1.3 copy.27
  7.8 0.7 convert_element_type.31
  8.5 0.1 copy.26
  8.6 0.1 broadcast_in_dim.8
  8.7 0.1 convert_element_type.32
  8.9 0.8 copy.28
  9.7 0.0 all-gather.5.cloned.1.call-update
  9.7 0.0 all-gather.7.cloned.1.call-start
  9.7 0.8 copy.30
  10.5 0.0 all-gather.7.cloned.1.call-update
  10.6 0.0 copy-done
  10.6 0.2 copy.29
  10.8 0.0 copy-done.1
  10.8 0.1 broadcast_in_dim.20
  10.9 0.1 convert_element_type.35
  11.0 0.0 copy-done.2
  11.0 0.2 convert_reduce_fusion.1
  11.2 144.9 %all-gather.5.cloned.1.call-done = bf16[1,4608,512]{2,1,0:T(8,128)(2,1)} async-done(((bf16[1,192,512]{2,1,0:T(8,128)(2,1)}), bf16[1,4608,512]{2,1,0:T(8,128)(2,1)}) %all-gather.5.cloned.1.call-update) | async-done | bytes 4718608 | tf_op jit(solution)/shard_map/all_gather | solution.py:23
  156.1 6.0 %fusion.2 = f32[4608,256]{1,0:T(8,128)} fusion(bf16[1,4608,512]{2,1,0:T(8,128)(2,1)} %all-gather.5.cloned.1.call-done, bf16[2,512,256]{1,2,0:T(8,128)(2,1)S(1)} %bitcast_multiply_fusion), kind=kOutput, calls=%fused_computation.4 | convolution fusion | flops 1207959552 | bytes 9699328 | tf_op jit(solution)/shard_map/dot_general | solution.py:22
  162.1 137.5 %all-gather.7.cloned.1.call-done = bf16[1,4608,512]{2,1,0:T(8,128)(2,1)} async-done(((bf16[1,192,512]{2,1,0:T(8,128)(2,1)}), bf16[1,4608,512]{2,1,0:T(8,128)(2,1)}) %all-gather.7.cloned.1.call-update) | async-done | bytes 4718608 | tf_op jit(solution)/shard_map/all_gather | solution.py:23
  299.6 5.2 %fusion = bf16[4608,256]{1,0:T(8,128)(2,1)S(1)} fusion(f32[4608,256]{1,0:T(8,128)} %fusion.2, bf16[1,4608,512]{2,1,0:T(8,128)(2,1)} %all-gather.7.cloned.1.call-done, bf16[2,512,256]{1,2,0:T(8,128)(2,1)S(1)} %bitcast_multiply_fusion), kind=kOutput, calls=%fused_computation.1 | convolution fusion | flops 1210318848 | bytes 12058624 | tf_op jit(solution)/shard_map/dot_general | solution.py:22
  304.8 2.0 fusion.4
  306.8 1.8 copy.32
  308.6 86.9 %all_to_all.5 = bf16[96,64,256]{2,1,0:T(8,128)(2,1)S(1)} all-to-all(bf16[96,64,256]{2,1,0:T(8,128)(2,1)S(1)} %copy.32), channel_id=1, replica_groups=mesh['row'=24,'col'=32] {'col'}, dimensions={0} | all-to-all | bytes 6291456 | tf_op jit(solution)/shard_map/all_to_all | solution.py:42
  395.5 1.3 convert_reduce_fusion
  (5 shorter events, 0.1 us)
Async XLA Ops:
  6.5 4.0 %copy-start = (bf16[2,512,256]{2,1,0:T(8,128)(2,1)S(1)}, bf16[2,512,256]{2,1,0:T(8,128)(2,1)}, u32[]{:S(2)}) copy-start(bf16[2,512,256]{2,1,0:T(8,128)(2,1)} %param.6) | copy-start | bytes 1572868
  6.5 4.3 %copy-start.1 = (s32[2,8,4]{1,2,0:T(4,128)S(1)}, s32[2,8,4]{1,2,0:T(4,128)}, u32[]{:S(2)}) copy-start(s32[2,8,4]{1,2,0:T(4,128)} %param.8) | copy-start | bytes 772
  6.5 4.5 %copy-start.2 = (s32[72]{0:T(128)S(1)}, s32[72]{0:T(128)}, u32[]{:S(2)}) copy-start(s32[72]{0:T(128)} %param.9) | copy-start | bytes 868
  6.5 149.5 %all-gather.5.cloned.1.call-start = ((), (), s32[]{:S(2)}) async-start(), calls=%async_computation.1 | async-start | bytes 4915200 | tf_op jit(solution)/shard_map/all_gather | solution.py:23
  9.7 289.9 %all-gather.7.cloned.1.call-start = ((), (), s32[]{:S(2)}) async-start(), calls=%async_computation.2 | async-start | bytes 4915200 | tf_op jit(solution)/shard_map/all_gather | solution.py:23
Sparse Core Ops, SparseCore 0:
  11.0 145.0 all-gather.4
  159.7 139.7 all-gather.6
where the time goes:
time: 404 us
  waiting for transfers between devices  282 us (70%)
  blocking collectives  86.9 us (22%)
  between operations  13.5 us (3%)
  matrix products  13.2 us (3%)
  local copies, waits for them, and re-layouts  5.32 us (1%)
    all_gather x2, waiting for transfers between devices, body(): lax.all_gather(amp_used[panel_index], 'row', axis=0, tiled=True)  282 us
    all_to_all x1, blocking collectives, body(): lax.all_to_all(send_buffer, 'col', split_axis=0, concat_axis=0, tiled=True)  86.9 us
    dot_general x2, matrix products, body(): jnp.dot(lax.all_gather(amp_used[panel_index], 'row', axis=0, tiled=True),...  11.2 us
  transfers between devices with their start and end apart: 2, of which 2 were waited for; matrix products, arithmetic and copies ran while one was open for 2% of the time, Pallas kernels for 0%

commit v1 on v0

v1 whole, which is shorter than its diff:
```python
import jax
import jax.numpy as jnp
from jax import lax
from jax.sharding import Mesh, PartitionSpec as P

SIZES = {"xh": 2, "z": 12, "y": 8, "xl": 2, "core": 2}
GROUP = ("xh", "xl", "core")
EDGE = 64
CAP = 3
PARTS = 8
PART_ROWS = EDGE // PARTS
SWAP = [(0, 1), (1, 0)]


def expand(mask, dtype):
    grown = jnp.repeat(jnp.repeat(mask, EDGE, axis=-2), EDGE, axis=-1)
    return grown.astype(dtype)


def pair(value, axis, dim):
    other = lax.ppermute(value, axis, SWAP)
    first = lax.axis_index(axis) == 0
    low = jnp.where(first, value, other)
    high = jnp.where(first, other, value)
    return jnp.concatenate([low, high], axis=dim)


def body(amplitudes, integrals, amp_mask, int_mask, owners):
    panels, rows, depth = amplitudes.shape
    local_tiles = rows // EDGE
    width = integrals.shape[2]
    tile_total = owners.shape[0]
    col_count = SIZES["y"] * SIZES["xl"] * SIZES["core"]

    amp_used = amplitudes * expand(amp_mask, amplitudes.dtype)
    parts = amp_used.reshape(panels, local_tiles, PARTS, PART_ROWS, depth)
    parts = parts.transpose(2, 0, 1, 3, 4).reshape(PARTS, panels * local_tiles * PART_ROWS, depth)
    traded = lax.all_to_all(parts, GROUP, split_axis=0, concat_axis=0, tiled=True)
    traded = traded.reshape(2, 4, panels, local_tiles * PART_ROWS, depth)
    traded = traded.transpose(0, 3, 1, 2, 4).reshape(2 * local_tiles * PART_ROWS, 4 * panels * depth)
    left = lax.all_gather(traded, "z", axis=0, tiled=True)

    int_used = integrals * expand(int_mask, integrals.dtype)
    right = pair(int_used, "xh", 2)
    right = pair(right[None], "xl", 0)
    right = pair(right[:, None], "core", 1)
    right = right.reshape(4 * panels * depth, 2 * width)

    partial_value = jnp.dot(left, right, preferred_element_type=jnp.float32).astype(jnp.bfloat16)

    positions = jnp.arange(tile_total, dtype=jnp.int32)
    same_owner = owners[:, None] == owners[None, :]
    earlier = positions[:, None] > positions[None, :]
    slot_index = jnp.sum((same_owner & earlier).astype(jnp.int32), axis=1)
    destination = owners * CAP + slot_index
    held = destination.reshape(2, SIZES["z"], local_tiles).transpose(1, 0, 2).reshape(tile_total)
    source_row = (held[:, None] * PART_ROWS + jnp.arange(PART_ROWS, dtype=jnp.int32)).reshape(-1)
    slot_rows = jnp.arange(col_count * CAP * PART_ROWS, dtype=jnp.int32)
    selector = (slot_rows[:, None] == source_row[None, :]).astype(jnp.bfloat16)
    slots = jnp.dot(selector, partial_value, preferred_element_type=jnp.float32).astype(jnp.bfloat16)

    send = slots.reshape(SIZES["y"], 4 * CAP * PART_ROWS, 2 * width)
    received = lax.all_to_all(send, "y", split_axis=0, concat_axis=0, tiled=True)
    summed = jnp.sum(received.astype(jnp.float32), axis=0)
    summed = summed.reshape(4, CAP * PART_ROWS, 2, width).transpose(2, 0, 1, 3)
    summed = summed.reshape(PARTS, CAP * PART_ROWS, width)
    gathered = lax.all_to_all(summed, GROUP, split_axis=0, concat_axis=0, tiled=True)
    gathered = gathered.reshape(PARTS, CAP, PART_ROWS, width).transpose(1, 0, 2, 3)
    return gathered.reshape(1, CAP, EDGE, width)


def solution(mesh):
    fine = Mesh(mesh.devices.reshape(tuple(SIZES.values())), tuple(SIZES))
    row, col = ("xh", "z"), ("y", "xl", "core")
    in_specs = (
        P(None, row, col),
        P(None, col, row),
        P(None, row, col),
        P(None, col, row),
        P(),
    )
    out_specs = P(col, None, None, row)
    return jax.shard_map(body, mesh=fine, in_specs=in_specs, out_specs=out_specs, check_vma=False)
```

time: 404 us -> 153 us (0.38)
  waiting for transfers between devices: 282 us -> 40.7 us
  blocking collectives: 86.9 us -> 61.3 us
  starting transfers between devices: 0.04 us -> 9.28 us
  other arithmetic: 2.22 us -> 9.8 us
  matrix products: 13.2 us -> 6.88 us
  local copies, waits for them, and re-layouts: 5.32 us -> 10.8 us
    all_gather x2 -> x1, waiting for transfers between devices: 282 us -> 1.03 us  [body(): left = lax.all_gather(traded, 'z', axis=0, tiled=True)]
    ppermute x0 -> x3, waiting for transfers between devices: none -> 39.6 us  [pair(): other = lax.ppermute(value, axis, SWAP)]
    all_to_all x1 -> x3, blocking collectives: 86.9 us -> 61.3 us  [the longest x1 26.4 us: body(): lax.all_to_all(send, 'y', split_axis=0, concat_axis=0, tiled=True)]
    ppermute x0 -> x3, starting transfers between devices: none -> 9.28 us  [pair(): other = lax.ppermute(value, axis, SWAP)]
    concatenate x0 -> x1, local copies, waits for them, and re-layouts: none -> 7.34 us  [pair(): return jnp.concatenate([low, high], axis=dim)]
    dot_general x3 -> x1, matrix products: 13.2 us -> 6.88 us  [body(): jnp.dot(selector, partial_value, preferred_element_type=jnp.float32)]
  transfers between devices with their start and end apart: 2 -> 4, of which waited for: 2 -> 4; matrix products, arithmetic and copies ran while one was open for 2% -> 10% of each run, Pallas kernels for 0% -> 0%
where the time goes in v1:
time: 153 us; the launch traced here: 152 us
  blocking collectives  61.3 us (40%)
  waiting for transfers between devices  40.7 us (27%)
  between operations  13.6 us (9%)
  local copies, waits for them, and re-layouts  10.8 us (7%)
  other arithmetic  9.8 us (6%)
  starting transfers between devices  9.28 us (6%)
  matrix products  6.88 us (4%)
    ppermute x3, waiting for transfers between devices, pair(): other = lax.ppermute(value, axis, SWAP)  39.6 us
    all_to_all x1, blocking collectives, body(): lax.all_to_all(send, 'y', split_axis=0, concat_axis=0, tiled=True)  26.4 us
    all_to_all x1, blocking collectives, body(): lax.all_to_all(parts, GROUP, split_axis=0, concat_axis=0, tiled=True)  21 us
    all_to_all x1, blocking collectives, body(): lax.all_to_all(summed, GROUP, split_axis=0, concat_axis=0, tiled=True)  13.9 us
    ppermute x3, starting transfers between devices, pair(): other = lax.ppermute(value, axis, SWAP)  9.28 us
    concatenate x1, local copies, waits for them, and re-layouts, pair(): return jnp.concatenate([low, high], axis=dim)  7.34 us
    dot_general x1, matrix products, body(): jnp.dot(selector, partial_value, preferred_element_type=jnp.float32)  6.88 us
    select_n x3, other arithmetic, pair(): low = jnp.where(first, value, other)  3.58 us
  transfers between devices with their start and end apart: 4, of which 4 were waited for; matrix products, arithmetic and copies ran while one was open for 10% of the time, Pallas kernels for 0%

profile of v1, /device:TPU:1, one launch (start us, length us, event | category | flops | bytes accessed | tf_op | source)
XLA Modules:
  0.0 152.3 jit_solution(8991950427019537046)
XLA Ops:
  6.5 0.7 convert_element_type.36
  7.2 0.1 copy.37
  7.4 0.1 convert_element_type.37
  7.6 0.2 copy.38
  7.8 1.2 mul.39
  9.0 21.0 %all_to_all.15 = bf16[8,48,512]{2,1,0:T(8,128)(2,1)S(1)} all-to-all(bf16[8,48,512]{2,1,0:T(8,128)(2,1)S(1)} %bitcast.45), channel_id=1, replica_groups=mesh['xh'=2,'z'=12,'y'=8,'xl'=2,'core'=2] {'xh','xl','core'}, dimensions={0} | all-to-all | bytes 786432 | tf_op jit(solution)/shard_map/all_to_all | solution.py:38
  30.0 0.3 copy.47
  30.3 1.1 reshape.69
  31.4 0.2 copy.41
  31.7 0.1 convert_element_type.40
  31.8 2.5 %collective-permute-start = (bf16[2,512,256]{1,2,0:T(8,128)(2,1)S(1)}, bf16[2,512,256]{1,2,0:T(8,128)(2,1)S(1)}, u32[]{:S(2)}, u32[]{:S(2)}) collective-permute-start(bf16[2,512,256]{1,2,0:T(8,128)(2,1)S(1)} %bitcast_multiply_fusion), channel_id=1, source_target_pairs={{0,384},{384,0},{1,385},{385,1},{2,386},{386,2},{3,387},{387,3},{4... | collective-permute-start | bytes 1572872 | tf_op jit(solution)/shard_map/ppermute | solution.py:21
  34.3 13.5 %collective-permute-done = bf16[2,512,256]{1,2,0:T(8,128)(2,1)S(1)} collective-permute-done((bf16[2,512,256]{1,2,0:T(8,128)(2,1)S(1)}, bf16[2,512,256]{1,2,0:T(8,128)(2,1)S(1)}, u32[]{:S(2)}, u32[]{:S(2)}) %collective-permute-start) | collective-permute-done | bytes 524320 | tf_op jit(solution)/shard_map/ppermute | solution.py:21
  47.9 2.2 %collective-permute-start.1 = (bf16[1,2,512,512]{2,3,1,0:T(8,128)(2,1)S(1)}, bf16[1,2,512,512]{2,3,1,0:T(8,128)(2,1)}, u32[]{:S(2)}, u32[]{:S(2)}) collective-permute-start(bf16[1,2,512,512]{2,3,1,0:T(8,128)(2,1)S(1)} %maximum_bitcast_fusion.1), channel_id=1, source_target_pairs={{0,2},{2,0},{1,3},{3,1},{4,6},{6,4},{5,7},{7,5},{8,10},{10,8},{9,1... | collective-permute-start | bytes 3145736 | tf_op jit(solution)/shard_map/ppermute | solution.py:21
  50.2 22.7 %collective-permute-done.1 = bf16[1,2,512,512]{2,3,1,0:T(8,128)(2,1)} collective-permute-done((bf16[1,2,512,512]{2,3,1,0:T(8,128)(2,1)S(1)}, bf16[1,2,512,512]{2,3,1,0:T(8,128)(2,1)}, u32[]{:S(2)}, u32[]{:S(2)}) %collective-permute-start.1) | collective-permute-done | bytes 1048608 | tf_op jit(solution)/shard_map/ppermute | solution.py:21
  72.8 1.6 %broadcast_select_fusion.3 = (bf16[1,2,512,512]{2,3,1,0:T(8,128)(2,1)S(1)}, bf16[1,2,512,512]{2,3,1,0:T(8,128)(2,1)S(1)}) fusion(bf16[1,2,512,512]{2,3,1,0:T(8,128)(2,1)} %collective-permute-done.1, pred[]{:T(512)S(6)} %eq.42, bf16[2,512,256]{1,2,0:T(8,128)(2,1)S(1)} %get-tuple-element.10, bf16[2,512,256]{1,2,0:T(8,128)(2,1)S(1)} %get-tuple-element.9), kind=kLoop, calls=%fused_computation.11 | loop fusion | flops 3145728 | bytes 4194305 | tf_op jit(solution)/shard_map/jit(_where)/select_n | solution.py:23
  74.5 1.6 %maximum_bitcast_fusion = bf16[2,1,2,512,512]{3,4,2,0,1:T(8,128)(2,1)} fusion(bf16[1,2,512,512]{2,3,1,0:T(8,128)(2,1)S(1)} %get-tuple-element.8, bf16[1,2,512,512]{2,3,1,0:T(8,128)(2,1)S(1)} %get-tuple-element.7), kind=kLoop, calls=%fused_computation.1 | loop fusion | flops 1048576 | bytes 4194304 | tf_op jit(solution)/shard_map/broadcast_in_dim | solution.py:46
  76.0 4.6 %collective-permute-start.2 = (bf16[2,1,2,512,512]{3,4,2,0,1:T(8,128)(2,1)}, bf16[2,1,2,512,512]{3,4,2,0,1:T(8,128)(2,1)}, u32[]{:S(2)}, u32[]{:S(2)}) collective-permute-start(bf16[2,1,2,512,512]{3,4,2,0,1:T(8,128)(2,1)} %maximum_bitcast_fusion), channel_id=1, source_target_pairs={{0,1},{1,0},{2,3},{3,2},{4,5},{5,4},{6,7},{7,6},{8,9},{9,8},{10,11... | collective-permute-start | bytes 6291464 | tf_op jit(solution)/shard_map/ppermute | solution.py:21
  80.6 0.2 convert_reduce_fusion.1
  80.8 0.1 mul.36
  80.9 0.1 mul.38
  81.1 0.1 add.27
  81.2 3.5 %collective-permute-done.2 = bf16[2,1,2,512,512]{3,4,2,0,1:T(8,128)(2,1)} collective-permute-done((bf16[2,1,2,512,512]{3,4,2,0,1:T(8,128)(2,1)}, bf16[2,1,2,512,512]{3,4,2,0,1:T(8,128)(2,1)}, u32[]{:S(2)}, u32[]{:S(2)}) %collective-permute-start.2) | collective-permute-done | bytes 2097184 | tf_op jit(solution)/shard_map/ppermute | solution.py:21
  84.7 1.9 %broadcast_select_fusion.1 = (bf16[2,1,2,512,512]{3,4,2,0,1:T(8,128)(2,1)S(1)}, bf16[2,1,2,512,512]{3,4,2,0,1:T(8,128)(2,1)S(1)}) fusion(bf16[2,1,2,512,512]{3,4,2,0,1:T(8,128)(2,1)} %collective-permute-done.2, pred[]{:T(512)S(6)} %eq.41, bf16[1,2,512,512]{2,3,1,0:T(8,128)(2,1)S(1)} %get-tuple-element.8, bf16[1,2,512,512]{2,3,1,0:T(8,128)(2,1)S(1)} %get-tuple-element.7), kind=kLoop, calls=%fused_computation.3 | loop fusion | flops 3145728 | bytes 8388609 | tf_op jit(solution)/shard_map/jit(_where)/select_n | solution.py:23
  86.6 2.4 %pad_maximum_fusion = bf16[2,2,2,512,512]{3,4,2,0,1:T(8,128)(2,1)} fusion(bf16[2,1,2,512,512]{3,4,2,0,1:T(8,128)(2,1)S(1)} %get-tuple-element.6, bf16[2,1,2,512,512]{3,4,2,0,1:T(8,128)(2,1)S(1)} %get-tuple-element.5), kind=kLoop, calls=%fused_computation | loop fusion | flops 2097152 | bytes 8388608 | tf_op jit(solution)/shard_map/concatenate | solution.py:25
  89.0 7.3 %copy.42 = bf16[2,2,2,512,512]{4,3,2,1,0:T(8,128)(2,1)} copy(bf16[2,2,2,512,512]{3,4,2,0,1:T(8,128)(2,1)} %pad_maximum_fusion) | data formatting | bytes 8388608 | tf_op jit(solution)/shard_map/concatenate | solution.py:25
  96.3 1.0 all-gather.2.cloned.1.call-done
  97.3 6.9 %fusion.1 = bf16[768,512]{1,0:T(8,128)(2,1)S(1)} fusion(s32[576]{0:T(1024)S(1)} %add.27, bf16[576,4096]{1,0:T(8,128)(2,1)} %all-gather.2.cloned.1.call-done, bf16[4096,512]{1,0:T(8,128)(2,1)} %bitcast.43), kind=kOutput, calls=%fused_computation.7 | convolution fusion | flops 2870034432 | bytes 9701632 | tf_op jit(solution)/shard_map/dot_general | solution.py:60
  104.2 26.4 %all_to_all.16 = bf16[8,96,512]{2,1,0:T(8,128)(2,1)S(1)} all-to-all(bf16[8,96,512]{2,1,0:T(8,128)(2,1)S(1)} %bitcast.49), channel_id=1, replica_groups=mesh['xh'=2,'z'=12,'y'=8,'xl'=2,'core'=2] {'y'}, dimensions={0} | all-to-all | bytes 1572864 | tf_op jit(solution)/shard_map/all_to_all | solution.py:63
  130.7 0.1 convert_reduce_fusion
  130.8 0.1 reshape.72
  130.9 13.9 %all_to_all.17 = f32[8,24,256]{2,1,0:T(8,128)S(1)} all-to-all(f32[8,24,256]{2,1,0:T(8,128)S(1)} %bitcast.51), channel_id=1, replica_groups=mesh['xh'=2,'z'=12,'y'=8,'xl'=2,'core'=2] {'xh','xl','core'}, dimensions={0} | all-to-all | bytes 393216 | tf_op jit(solution)/shard_map/all_to_all | solution.py:67
  144.8 0.7 copy_bitcast_fusion.1
  (20 shorter events, 0.6 us)
Async XLA Ops:
  6.5 90.8 %all-gather.2.cloned.1.call-start = ((), (), s32[]{:S(2)}) async-start(), calls=%async_computation.3 | async-start | bytes 5111808 | tf_op jit(solution)/shard_map/all_gather | solution.py:41
  7.8 23.6 %copy-start = (bf16[2,512,256]{2,1,0:T(8,128)(2,1)S(1)}, bf16[2,512,256]{2,1,0:T(8,128)(2,1)}, u32[]{:S(2)}) copy-start(bf16[2,512,256]{2,1,0:T(8,128)(2,1)} %param.6) | copy-start | bytes 1572868
  9.0 22.6 %copy-start.1 = (s32[2,8,4]{1,2,0:T(4,128)S(1)}, s32[2,8,4]{1,2,0:T(4,128)}, u32[]{:S(2)}) copy-start(s32[2,8,4]{1,2,0:T(4,128)} %param.8) | copy-start | bytes 772
  31.8 16.0 %collective-permute-start = (bf16[2,512,256]{1,2,0:T(8,128)(2,1)S(1)}, bf16[2,512,256]{1,2,0:T(8,128)(2,1)S(1)}, u32[]{:S(2)}, u32[]{:S(2)}) collective-permute-start(bf16[2,512,256]{1,2,0:T(8,128)(2,1)S(1)} %bitcast_multiply_fusion), channel_id=1, source_target_pairs={{0,384},{384,0},{1,385},{385,1},{2,386},{386,2},{3,387},{387,3},{4... | collective-permute-start | bytes 1572872 | tf_op jit(solution)/shard_map/ppermute | solution.py:21
  47.9 24.9 %collective-permute-start.1 = (bf16[1,2,512,512]{2,3,1,0:T(8,128)(2,1)S(1)}, bf16[1,2,512,512]{2,3,1,0:T(8,128)(2,1)}, u32[]{:S(2)}, u32[]{:S(2)}) collective-permute-start(bf16[1,2,512,512]{2,3,1,0:T(8,128)(2,1)S(1)} %maximum_bitcast_fusion.1), channel_id=1, source_target_pairs={{0,2},{2,0},{1,3},{3,1},{4,6},{6,4},{5,7},{7,5},{8,10},{10,8},{9,1... | collective-permute-start | bytes 3145736 | tf_op jit(solution)/shard_map/ppermute | solution.py:21
  74.5 6.2 %copy-start.2 = (s32[72]{0:T(128)S(1)}, s32[72]{0:T(128)}, u32[]{:S(2)}) copy-start(s32[72]{0:T(128)} %param.9) | copy-start | bytes 868
  76.0 8.7 %collective-permute-start.2 = (bf16[2,1,2,512,512]{3,4,2,0,1:T(8,128)(2,1)}, bf16[2,1,2,512,512]{3,4,2,0,1:T(8,128)(2,1)}, u32[]{:S(2)}, u32[]{:S(2)}) collective-permute-start(bf16[2,1,2,512,512]{3,4,2,0,1:T(8,128)(2,1)} %maximum_bitcast_fusion), channel_id=1, source_target_pairs={{0,1},{1,0},{2,3},{3,2},{4,5},{5,4},{6,7},{7,6},{8,9},{9,8},{10,11... | collective-permute-start | bytes 6291464 | tf_op jit(solution)/shard_map/ppermute | solution.py:21
Sparse Core Ops, SparseCore 0:
  31.5 65.8 all-gather.1

commit v2 on v1

v2 whole, which is shorter than its diff:
```python
import jax
import jax.numpy as jnp
from jax import lax
from jax.experimental import pallas as pl
from jax.experimental.pallas import tpu as pltpu
from jax.sharding import Mesh, PartitionSpec as P

SIZES = {"xh": 2, "z": 12, "yq": 4, "yb": 2, "xl": 2, "core": 2}
GROUP = ("xh", "yb", "xl", "core")
OWNERS = ("xh", "yq", "yb", "xl", "core")
RING = ("xh", "xl")
EDGE = 64
CAP = 3
LANES = 128
PARTS = 16
PART_ROWS = EDGE // PARTS
SLICES = 8
SWAP = [(0, 1), (1, 0)]
MIB = 1 << 20


def expand(mask, dtype):
    grown = jnp.repeat(jnp.repeat(mask, EDGE, axis=-2), EDGE, axis=-1)
    return grown.astype(dtype)


def turn(value, step):
    return lax.ppermute(value, RING, [(i, (i + step) % 4) for i in range(4)])


def contract(place_ref, left_ref, select_ref, *rest):
    pieces, (out_ref, slab_ref, total_ref, sems) = rest[:-4], rest[-4:]
    depth, width = pieces[0].shape
    copies = []
    for number in range(SLICES):
        begin = pl.multiple_of(place_ref[number, 0] * depth, depth)
        copy = pltpu.make_async_copy(
            left_ref.at[:, pl.ds(begin, depth)], slab_ref.at[number], sems.at[number]
        )
        copy.start()
        copies.append(copy)
    for number in range(SLICES):
        copies[number].wait()
        for side in range(2):
            term = jnp.dot(
                slab_ref[number], pieces[2 * number + side][...], preferred_element_type=jnp.float32
            )
            half = place_ref[number, 1 + side]
            if number == 0:
                total_ref[half] = term
            else:
                total_ref[half] += term
    rows = select_ref.shape[0]
    for half in range(2):
        rounded = total_ref[half].astype(jnp.bfloat16)
        stacked = jnp.concatenate([rounded[:, :LANES], rounded[:, LANES:]], axis=0)
        placed = jnp.dot(select_ref[...], stacked, preferred_element_type=jnp.float32)
        out_ref[half * rows:(half + 1) * rows, :] = placed.astype(jnp.bfloat16)


def body(amplitudes, integrals, amp_mask, int_mask, owners):
    panels, rows, depth = amplitudes.shape
    local_tiles = rows // EDGE
    width = integrals.shape[2]
    tile_total = owners.shape[0]
    slot_total = SIZES["yq"] * SLICES * CAP
    xh, yb, xl, core = (lax.axis_index(name) for name in GROUP)

    int_used = integrals * expand(int_mask, integrals.dtype)
    own = int_used.reshape(panels * depth, width)
    across = lax.ppermute(own, "yb", SWAP)
    low = [turn(own, 1), turn(across, 1)]
    high = [turn(own, -1), turn(across, -1)]
    far = [turn(low[0], 1), turn(high[1], -1)]
    here = []
    for near, beyond in (((own, across), far), (low, high)):
        for side in range(2):
            here += [near[side], beyond[side]]
    there = [lax.ppermute(value, "core", SWAP) for value in here]
    chip = xh * 2 + xl
    place = []
    for core_at in (core, 1 - core):
        for first, second in ((0, 2), (3, 1)):
            for side in (yb, 1 - yb):
                one, other = (chip + first) % 4, (chip + second) % 4
                place.append(jnp.stack([side * 4 + (one % 2) * 2 + core_at, one // 2, other // 2]))
    place = jnp.stack(place).astype(jnp.int32)

    amp_used = amplitudes * expand(amp_mask, amplitudes.dtype)
    parts = amp_used.reshape(panels, local_tiles, PARTS, PART_ROWS, depth)
    parts = parts.transpose(2, 0, 1, 3, 4).reshape(PARTS, panels * local_tiles * PART_ROWS, depth)
    traded = lax.all_to_all(parts, GROUP, split_axis=0, concat_axis=0, tiled=True)
    traded = traded.reshape(2, SLICES, panels, local_tiles * PART_ROWS, depth)
    traded = traded.transpose(0, 3, 1, 2, 4).reshape(2 * local_tiles * PART_ROWS, SLICES * panels * depth)
    left = lax.all_gather(traded, "z", axis=0, tiled=True)

    positions = jnp.arange(tile_total, dtype=jnp.int32)
    same_owner = owners[:, None] == owners[None, :]
    earlier = positions[:, None] > positions[None, :]
    slot_index = jnp.sum((same_owner & earlier).astype(jnp.int32), axis=1)
    destination = owners * CAP + slot_index
    held = destination.reshape(2, SIZES["z"], local_tiles).transpose(1, 0, 2).reshape(tile_total)
    source_row = (held[:, None] * PART_ROWS + jnp.arange(PART_ROWS, dtype=jnp.int32)).reshape(-1)
    owner_rows = CAP * PART_ROWS
    source_row = source_row // owner_rows * (2 * owner_rows) + source_row % owner_rows
    source_row = jnp.concatenate([source_row, source_row + owner_rows])
    slot_rows = jnp.arange(2 * slot_total * PART_ROWS, dtype=jnp.int32)
    selector = (slot_rows[:, None] == source_row[None, :]).astype(jnp.bfloat16)

    vmem = pl.BlockSpec(memory_space=pltpu.VMEM)
    slots = pl.pallas_call(
        contract,
        out_shape=jax.ShapeDtypeStruct((2 * selector.shape[0], LANES), jnp.bfloat16),
        in_specs=[pl.BlockSpec(memory_space=pltpu.SMEM), pl.BlockSpec(memory_space=pl.ANY)] + [vmem] * 17,
        out_specs=vmem,
        scratch_shapes=[
            pltpu.VMEM((SLICES, left.shape[0], panels * depth), jnp.bfloat16),
            pltpu.VMEM((2, left.shape[0], width), jnp.float32),
            pltpu.SemaphoreType.DMA((SLICES,)),
        ],
        compiler_params=pltpu.CompilerParams(vmem_limit_bytes=40 * MIB),
        cost_estimate=pl.CostEstimate(
            flops=2 * left.size * 2 * width, bytes_accessed=4 * left.size, transcendentals=0
        ),
    )(place, left, selector, *here, *there)

    received = lax.all_to_all(slots, OWNERS, split_axis=0, concat_axis=0, tiled=True)
    received = received.reshape(2, SIZES["yq"], SLICES, 2, CAP, PART_ROWS, LANES).astype(jnp.float32)
    summed = jnp.sum(received, axis=1).transpose(3, 0, 1, 4, 2, 5)
    return summed.reshape(1, CAP, EDGE, width)


def solution(mesh):
    fine = Mesh(mesh.devices.reshape(tuple(SIZES.values())), tuple(SIZES))
    row, col = ("xh", "z"), ("yq", "yb", "xl", "core")
    in_specs = (
        P(None, row, col),
        P(None, col, row),
        P(None, row, col),
        P(None, col, row),
        P(),
    )
    out_specs = P(col, None, None, row)
    return jax.shard_map(body, mesh=fine, in_specs=in_specs, out_specs=out_specs, check_vma=False)
```

time: 153 us -> 151 us (0.987)
  starting transfers between devices: 9.28 us -> 40.2 us
  waiting for transfers between devices: 40.7 us -> 18.1 us
  blocking collectives: 61.3 us -> 49.3 us
  local copies, waits for them, and re-layouts: 10.8 us -> 18.4 us
  Pallas kernels: 0 us -> 7.02 us
  matrix products: 6.88 us -> 0 us
  other arithmetic: 9.8 us -> 3.09 us
    ppermute x3 -> x15, starting transfers between devices: 9.28 us -> 40.2 us  [the longest x8 19.5 us: body(): there = [lax.ppermute(value, 'core', SWAP) for value in here]]
    ppermute x3 -> x15, waiting for transfers between devices: 39.6 us -> 12 us  [the longest x6 8.15 us: turn(): return lax.ppermute(value, RING, [(i, (i + step) % 4) for i in range(4)])]
    unnamed x7 -> x33, local copies, waits for them, and re-layouts: 0.23 us -> 13.7 us
    all_to_all x2 -> x1, blocking collectives: 40.3 us -> 27.7 us  [body(): lax.all_to_all(slots, OWNERS, split_axis=0, concat_axis=0, tiled=True)]
    concatenate x1 -> x0, local copies, waits for them, and re-layouts: 7.34 us -> none  [pair(): return jnp.concatenate([low, high], axis=dim)]
    pallas_call x0 -> x1, Pallas kernels: none -> 7.02 us  [body(): pl.pallas_call(contract, out_shape=jax.ShapeDtypeStruct((2 * selector.sha...]
    dot_general x1 -> x0, matrix products: 6.88 us -> none  [body(): jnp.dot(selector, partial_value, preferred_element_type=jnp.float32)]
    all_gather x1, waiting for transfers between devices: 1.03 us -> 6.15 us  [body(): left = lax.all_gather(traded, 'z', axis=0, tiled=True)]
  transfers between devices with their start and end apart: 4 -> 16, of which waited for: 4 -> 4; matrix products, arithmetic and copies ran while one was open for 10% -> 2% of each run, Pallas kernels for 0% -> 0%
where the time goes in v2:
time: 151 us; the launch traced here: 150 us
  blocking collectives  49.3 us (33%)
  starting transfers between devices  40.2 us (27%)
  local copies, waits for them, and re-layouts  18.4 us (12%)
  waiting for transfers between devices  18.1 us (12%)
  between operations  14 us (9%)
  Pallas kernels  7.02 us (5%)
  other arithmetic  3.09 us (2%)
    all_to_all x1, blocking collectives, body(): lax.all_to_all(slots, OWNERS, split_axis=0, concat_axis=0, tiled=True)  27.7 us
    all_to_all x1, blocking collectives, body(): lax.all_to_all(parts, GROUP, split_axis=0, concat_axis=0, tiled=True)  21.5 us
    ppermute x8, starting transfers between devices, body(): there = [lax.ppermute(value, 'core', SWAP) for value in here]  19.5 us
    ppermute x6, starting transfers between devices, turn(): return lax.ppermute(value, RING, [(i, (i + step) % 4) for i in range(4)])  18 us
    unnamed x33, local copies, waits for them, and re-layouts  13.7 us
    ppermute x6, waiting for transfers between devices, turn(): return lax.ppermute(value, RING, [(i, (i + step) % 4) for i in range(4)])  8.15 us
    pallas_call x1, Pallas kernels, body(): pl.pallas_call(contract, out_shape=jax.ShapeDtypeStruct((2 * selector.sha...  7.02 us
    all_gather x1, waiting for transfers between devices, body(): left = lax.all_gather(traded, 'z', axis=0, tiled=True)  6.15 us
  transfers between devices with their start and end apart: 16, of which 4 were waited for; matrix products, arithmetic and copies ran while one was open for 2% of the time, Pallas kernels for 0%

profile of v2, /device:TPU:1, one launch (start us, length us, event | category | flops | bytes accessed | tf_op | source)
XLA Modules:
  0.0 150.0 jit_solution(4885025123305767957)
XLA Ops:
  7.8 1.1 mul.70
  9.6 21.5 %all_to_all.14 = bf16[16,24,512]{2,1,0:T(8,128)(2,1)S(1)} all-to-all(bf16[16,24,512]{2,1,0:T(8,128)(2,1)S(1)} %copy.60), channel_id=1, replica_groups=mesh['xh'=2,'z'=12,'yq'=4,'yb'=2,'xl'=2,'core'=2] {'xh','yb','xl','core'}, dimensions={0} | all-to-all | bytes 786432 | tf_op jit(solution)/shard_map/all_to_all | solution.py:92
  31.7 1.0 reshape.61
  33.5 2.7 %collective-permute-start.2 = (bf16[1024,256]{1,0:T(8,128)(2,1)S(1)}, bf16[1024,256]{1,0:T(8,128)(2,1)S(1)}, u32[]{:S(2)}, u32[]{:S(2)}) collective-permute-start(bf16[1024,256]{1,0:T(8,128)(2,1)S(1)} %bitcast.50), channel_id=1, source_target_pairs={{0,4},{4,0},{1,5},{5,1},{2,6},{6,2},{3,7},{7,3},{8,12},{12,8},{9,1... | collective-permute-start | bytes 1572872 | tf_op jit(solution)/shard_map/ppermute | solution.py:71
  36.2 2.3 %collective-permute-start.7 = (bf16[1024,256]{1,0:T(8,128)(2,1)S(1)}, bf16[1024,256]{1,0:T(8,128)(2,1)S(1)}, u32[]{:S(2)}, u32[]{:S(2)}) collective-permute-start(bf16[1024,256]{1,0:T(8,128)(2,1)S(1)} %bitcast.51), channel_id=1, source_target_pairs={{0,1},{1,0},{2,3},{3,2},{4,5},{5,4},{6,7},{7,6},{8,9},{9,8},{10,11... | collective-permute-start | bytes 1572872 | tf_op jit(solution)/shard_map/ppermute | solution.py:79
  38.5 3.0 %collective-permute-start.5 = (bf16[1024,256]{1,0:T(8,128)(2,1)S(1)}, bf16[1024,256]{1,0:T(8,128)(2,1)S(1)}, u32[]{:S(2)}, u32[]{:S(2)}) collective-permute-start(bf16[1024,256]{1,0:T(8,128)(2,1)S(1)} %bitcast.52), channel_id=1, source_target_pairs={{0,386},{2,0},{384,2},{386,384},{1,387},{3,1},{385,3},{387,385},{4... | collective-permute-start | bytes 1572872 | tf_op jit(solution)/shard_map/ppermute | solution.py:28
  41.5 2.3 %collective-permute-start = (bf16[1024,256]{1,0:T(8,128)(2,1)S(1)}, bf16[1024,256]{1,0:T(8,128)(2,1)}, u32[]{:S(2)}, u32[]{:S(2)}) collective-permute-start(bf16[1024,256]{1,0:T(8,128)(2,1)S(1)} %bitcast.53), channel_id=1, source_target_pairs={{0,2},{2,384},{384,386},{386,0},{1,3},{3,385},{385,387},{387,1},{4... | collective-permute-start | bytes 1572872 | tf_op jit(solution)/shard_map/ppermute | solution.py:28
  43.8 3.8 %collective-permute-done.2.rest_2_ = bf16[1024,256]{1,0:T(8,128)(2,1)S(1)} collective-permute-done((bf16[1024,256]{1,0:T(8,128)(2,1)S(1)}, bf16[1024,256]{1,0:T(8,128)(2,1)S(1)}, u32[]{:S(2)}, u32[]{:S(2)}) %collective-permute-start.2) | collective-permute-done | bytes 524320 | tf_op jit(solution)/shard_map/ppermute | solution.py:71
  47.6 4.1 %collective-permute-start.3 = (bf16[1024,256]{1,0:T(8,128)(2,1)S(1)}, bf16[1024,256]{1,0:T(8,128)(2,1)}, u32[]{:S(2)}, u32[]{:S(2)}) collective-permute-start(bf16[1024,256]{1,0:T(8,128)(2,1)S(1)} %collective-permute-done.2.rest_2_), channel_id=1, source_target_pairs={{0,386},{2,0},{384,2},{386,384},{1,387},{3,1},{385,3},{387,385},{4... | collective-permute-start | bytes 1572872 | tf_op jit(solution)/shard_map/ppermute | solution.py:28
  52.3 3.1 %collective-permute-start.9 = (bf16[1024,256]{1,0:T(8,128)(2,1)S(1)}, bf16[1024,256]{1,0:T(8,128)(2,1)S(1)}, u32[]{:S(2)}, u32[]{:S(2)}) collective-permute-start(bf16[1024,256]{1,0:T(8,128)(2,1)S(1)} %collective-permute-done.2.rest_2_), channel_id=1, source_target_pairs={{0,1},{1,0},{2,3},{3,2},{4,5},{5,4},{6,7},{7,6},{8,9},{9,8},{10,11... | collective-permute-start | bytes 1572872 | tf_op jit(solution)/shard_map/ppermute | solution.py:79
  55.4 2.3 %collective-permute-start.6 = (bf16[1024,256]{1,0:T(8,128)(2,1)S(1)}, bf16[1024,256]{1,0:T(8,128)(2,1)}, u32[]{:S(2)}, u32[]{:S(2)}) collective-permute-start(bf16[1024,256]{1,0:T(8,128)(2,1)S(1)} %collective-permute-done.2.rest_2_), channel_id=1, source_target_pairs={{0,2},{2,384},{384,386},{386,0},{1,3},{3,385},{385,387},{387,1},{4... | collective-permute-start | bytes 1572872 | tf_op jit(solution)/shard_map/ppermute | solution.py:28
  57.7 2.2 %collective-permute-start.12 = (bf16[1024,256]{1,0:T(8,128)(2,1)S(1)}, bf16[1024,256]{1,0:T(8,128)(2,1)}, u32[]{:S(2)}, u32[]{:S(2)}) collective-permute-start(bf16[1024,256]{1,0:T(8,128)(2,1)S(1)} %collective-permute-done.5.rest_5_), channel_id=1, source_target_pairs={{0,1},{1,0},{2,3},{3,2},{4,5},{5,4},{6,7},{7,6},{8,9},{9,8},{10,11... | collective-permute-start | bytes 1572872 | tf_op jit(solution)/shard_map/ppermute | solution.py:79
  59.9 1.9 %collective-permute-start.1 = (bf16[1024,256]{1,0:T(8,128)(2,1)}, bf16[1024,256]{1,0:T(8,128)(2,1)}, u32[]{:S(2)}, u32[]{:S(2)}) collective-permute-start(bf16[1024,256]{1,0:T(8,128)(2,1)} %collective-permute-done.rest_4_), channel_id=1, source_target_pairs={{0,2},{2,384},{384,386},{386,0},{1,3},{3,385},{385,387},{387,1},{4... | collective-permute-start | bytes 1572872 | tf_op jit(solution)/shard_map/ppermute | solution.py:28
  61.9 3.3 %collective-permute-done.3.rest_7_ = bf16[1024,256]{1,0:T(8,128)(2,1)} collective-permute-done((bf16[1024,256]{1,0:T(8,128)(2,1)S(1)}, bf16[1024,256]{1,0:T(8,128)(2,1)}, u32[]{:S(2)}, u32[]{:S(2)}) %collective-permute-start.3) | collective-permute-done | bytes 524320 | tf_op jit(solution)/shard_map/ppermute | solution.py:28
  65.2 4.3 %collective-permute-start.4 = (bf16[1024,256]{1,0:T(8,128)(2,1)}, bf16[1024,256]{1,0:T(8,128)(2,1)}, u32[]{:S(2)}, u32[]{:S(2)}) collective-permute-start(bf16[1024,256]{1,0:T(8,128)(2,1)} %collective-permute-done.3.rest_7_), channel_id=1, source_target_pairs={{0,386},{2,0},{384,2},{386,384},{1,387},{3,1},{385,3},{387,385},{4... | collective-permute-start | bytes 1572872 | tf_op jit(solution)/shard_map/ppermute | solution.py:28
  70.4 3.0 %collective-permute-start.11 = (bf16[1024,256]{1,0:T(8,128)(2,1)}, bf16[1024,256]{1,0:T(8,128)(2,1)S(1)}, u32[]{:S(2)}, u32[]{:S(2)}) collective-permute-start(bf16[1024,256]{1,0:T(8,128)(2,1)} %collective-permute-done.rest_4_), channel_id=1, source_target_pairs={{0,1},{1,0},{2,3},{3,2},{4,5},{5,4},{6,7},{7,6},{8,9},{9,8},{10,11... | collective-permute-start | bytes 1572872 | tf_op jit(solution)/shard_map/ppermute | solution.py:79
  74.2 1.9 %collective-permute-start.14 = (bf16[1024,256]{1,0:T(8,128)(2,1)}, bf16[1024,256]{1,0:T(8,128)(2,1)S(1)}, u32[]{:S(2)}, u32[]{:S(2)}) collective-permute-start(bf16[1024,256]{1,0:T(8,128)(2,1)} %collective-permute-done.3.rest_7_), channel_id=1, source_target_pairs={{0,1},{1,0},{2,3},{3,2},{4,5},{5,4},{6,7},{7,6},{8,9},{9,8},{10,11... | collective-permute-start | bytes 1572872 | tf_op jit(solution)/shard_map/ppermute | solution.py:79
  76.2 2.4 %collective-permute-start.13 = (bf16[1024,256]{1,0:T(8,128)(2,1)}, bf16[1024,256]{1,0:T(8,128)(2,1)S(1)}, u32[]{:S(2)}, u32[]{:S(2)}) collective-permute-start(bf16[1024,256]{1,0:T(8,128)(2,1)} %collective-permute-done.6.rest_6_), channel_id=1, source_target_pairs={{0,1},{1,0},{2,3},{3,2},{4,5},{5,4},{6,7},{7,6},{8,9},{9,8},{10,11... | collective-permute-start | bytes 1572872 | tf_op jit(solution)/shard_map/ppermute | solution.py:79
  78.6 4.8 %collective-permute-done.1.rest_1_ = bf16[1024,256]{1,0:T(8,128)(2,1)} collective-permute-done((bf16[1024,256]{1,0:T(8,128)(2,1)}, bf16[1024,256]{1,0:T(8,128)(2,1)}, u32[]{:S(2)}, u32[]{:S(2)}) %collective-permute-start.1) | collective-permute-done | bytes 524320 | tf_op jit(solution)/shard_map/ppermute | solution.py:28
  83.4 2.7 %collective-permute-start.8 = (bf16[1024,256]{1,0:T(8,128)(2,1)}, bf16[1024,256]{1,0:T(8,128)(2,1)S(1)}, u32[]{:S(2)}, u32[]{:S(2)}) collective-permute-start(bf16[1024,256]{1,0:T(8,128)(2,1)} %collective-permute-done.1.rest_1_), channel_id=1, source_target_pairs={{0,1},{1,0},{2,3},{3,2},{4,5},{5,4},{6,7},{7,6},{8,9},{9,8},{10,11... | collective-permute-start | bytes 1572872 | tf_op jit(solution)/shard_map/ppermute | solution.py:79
  86.1 1.9 %collective-permute-start.10 = (bf16[1024,256]{1,0:T(8,128)(2,1)}, bf16[1024,256]{1,0:T(8,128)(2,1)S(1)}, u32[]{:S(2)}, u32[]{:S(2)}) collective-permute-start(bf16[1024,256]{1,0:T(8,128)(2,1)} %collective-permute-done.4.rest_3_), channel_id=1, source_target_pairs={{0,1},{1,0},{2,3},{3,2},{4,5},{5,4},{6,7},{7,6},{8,9},{9,8},{10,11... | collective-permute-start | bytes 1572872 | tf_op jit(solution)/shard_map/ppermute | solution.py:79
  90.9 0.8 copy-done.9
  92.6 6.2 %all-gather.2.cloned.1.call-done.left_ref = bf16[288,8192]{1,0:T(8,128)(2,1)} async-done(((bf16[24,8192]{1,0:T(8,128)(2,1)}), bf16[288,8192]{1,0:T(8,128)(2,1)}) %all-gather.2.cloned.1.call-update) | async-done | bytes 4718608 | tf_op jit(solution)/shard_map/all_gather | solution.py:95
  98.7 2.3 %copy-done = bf16[288,8192]{1,0:T(8,128)(2,1)S(1)} copy-done((bf16[288,8192]{1,0:T(8,128)(2,1)S(1)}, bf16[288,8192]{1,0:T(8,128)(2,1)}, u32[]{:S(2)}) %copy-start) | copy-done | bytes 4718616
  101.0 1.0 copy-done.2
  102.1 1.0 copy-done.4
  103.1 1.0 copy-done.6
  104.2 1.0 copy-done.8
  105.2 1.0 copy-done.10
  106.3 1.0 copy-done.12
  107.3 7.0 %shard_map.55 = bf16[1536,128]{1,0:T(8,128)(2,1)S(1)} custom-call(s32[8,3]{1,0:T(8,128)S(1)} %stack.127.place_ref, bf16[288,8192]{1,0:T(8,128)(2,1)S(1)} %copy-done, bf16[768,576]{1,0:T(8,128)(2,1)S(1)} %fusion.select_ref, bf16[1024,256]{1,0:T(8,128)(2,1)S(1)} %bitcast.54, bf16[1024,256]{1,0:T(8,128)(2,1)} %collective-permute-done.1.rest_1_, ...), custom_call_target="tpu_custom_call" | custom-call | flops 2415919104 | bytes 9437184 | tf_op jit(solution)/shard_map/pallas_call | solution.py:111
  114.3 27.7 %all_to_all.15 = bf16[64,24,128]{2,1,0:T(8,128)(2,1)S(1)} all-to-all(bf16[64,24,128]{2,1,0:T(8,128)(2,1)S(1)} %bitcast.55), channel_id=1, replica_groups=mesh['xh'=2,'z'=12,'yq'=4,'yb'=2,'xl'=2,'core'=2] {'xh','yq','yb','xl','..., dimensions={0} | all-to-all | bytes 786432 | tf_op jit(solution)/shard_map/all_to_all | solution.py:127
  (76 shorter events, 10.0 us)
Async XLA Ops:
  6.5 92.2 %all-gather.2.cloned.1.call-start = ((), (), s32[]{:S(2)}) async-start(), calls=%async_computation.2 | async-start | bytes 5111808 | tf_op jit(solution)/shard_map/all_gather | solution.py:95
  9.6 23.2 %copy-start.14 = (s32[2,8,4]{1,2,0:T(4,128)S(1)}, s32[2,8,4]{1,2,0:T(4,128)}, u32[]{:S(2)}) copy-start(s32[2,8,4]{1,2,0:T(4,128)} %param.8) | copy-start | bytes 772
  9.6 23.4 %copy-start.13 = (bf16[2,512,256]{2,1,0:T(8,128)(2,1)S(1)}, bf16[2,512,256]{2,1,0:T(8,128)(2,1)}, u32[]{:S(2)}) copy-start(bf16[2,512,256]{2,1,0:T(8,128)(2,1)} %param.6) | copy-start | bytes 1572868
  32.8 19.0 %copy-start.15 = (s32[72]{0:T(128)S(1)}, s32[72]{0:T(128)}, u32[]{:S(2)}) copy-start(s32[72]{0:T(128)} %param.9) | copy-start | bytes 868
  33.5 14.1 %collective-permute-start.2 = (bf16[1024,256]{1,0:T(8,128)(2,1)S(1)}, bf16[1024,256]{1,0:T(8,128)(2,1)S(1)}, u32[]{:S(2)}, u32[]{:S(2)}) collective-permute-start(bf16[1024,256]{1,0:T(8,128)(2,1)S(1)} %bitcast.50), channel_id=1, source_target_pairs={{0,4},{4,0},{1,5},{5,1},{2,6},{6,2},{3,7},{7,3},{8,12},{12,8},{9,1... | collective-permute-start | bytes 1572872 | tf_op jit(solution)/shard_map/ppermute | solution.py:71
  36.2 19.2 %collective-permute-start.7 = (bf16[1024,256]{1,0:T(8,128)(2,1)S(1)}, bf16[1024,256]{1,0:T(8,128)(2,1)S(1)}, u32[]{:S(2)}, u32[]{:S(2)}) collective-permute-start(bf16[1024,256]{1,0:T(8,128)(2,1)S(1)} %bitcast.51), channel_id=1, source_target_pairs={{0,1},{1,0},{2,3},{3,2},{4,5},{5,4},{6,7},{7,6},{8,9},{9,8},{10,11... | collective-permute-start | bytes 1572872 | tf_op jit(solution)/shard_map/ppermute | solution.py:79
  38.5 19.2 %collective-permute-start.5 = (bf16[1024,256]{1,0:T(8,128)(2,1)S(1)}, bf16[1024,256]{1,0:T(8,128)(2,1)S(1)}, u32[]{:S(2)}, u32[]{:S(2)}) collective-permute-start(bf16[1024,256]{1,0:T(8,128)(2,1)S(1)} %bitcast.52), channel_id=1, source_target_pairs={{0,386},{2,0},{384,2},{386,384},{1,387},{3,1},{385,3},{387,385},{4... | collective-permute-start | bytes 1572872 | tf_op jit(solution)/shard_map/ppermute | solution.py:28
  41.5 18.4 %collective-permute-start = (bf16[1024,256]{1,0:T(8,128)(2,1)S(1)}, bf16[1024,256]{1,0:T(8,128)(2,1)}, u32[]{:S(2)}, u32[]{:S(2)}) collective-permute-start(bf16[1024,256]{1,0:T(8,128)(2,1)S(1)} %bitcast.53), channel_id=1, source_target_pairs={{0,2},{2,384},{384,386},{386,0},{1,3},{3,385},{385,387},{387,1},{4... | collective-permute-start | bytes 1572872 | tf_op jit(solution)/shard_map/ppermute | solution.py:28
  47.6 17.6 %collective-permute-start.3 = (bf16[1024,256]{1,0:T(8,128)(2,1)S(1)}, bf16[1024,256]{1,0:T(8,128)(2,1)}, u32[]{:S(2)}, u32[]{:S(2)}) collective-permute-start(bf16[1024,256]{1,0:T(8,128)(2,1)S(1)} %collective-permute-done.2.rest_2_), channel_id=1, source_target_pairs={{0,386},{2,0},{384,2},{386,384},{1,387},{3,1},{385,3},{387,385},{4... | collective-permute-start | bytes 1572872 | tf_op jit(solution)/shard_map/ppermute | solution.py:28
  52.3 21.2 %collective-permute-start.9 = (bf16[1024,256]{1,0:T(8,128)(2,1)S(1)}, bf16[1024,256]{1,0:T(8,128)(2,1)S(1)}, u32[]{:S(2)}, u32[]{:S(2)}) collective-permute-start(bf16[1024,256]{1,0:T(8,128)(2,1)S(1)} %collective-permute-done.2.rest_2_), channel_id=1, source_target_pairs={{0,1},{1,0},{2,3},{3,2},{4,5},{5,4},{6,7},{7,6},{8,9},{9,8},{10,11... | collective-permute-start | bytes 1572872 | tf_op jit(solution)/shard_map/ppermute | solution.py:79
  55.4 20.8 %collective-permute-start.6 = (bf16[1024,256]{1,0:T(8,128)(2,1)S(1)}, bf16[1024,256]{1,0:T(8,128)(2,1)}, u32[]{:S(2)}, u32[]{:S(2)}) collective-permute-start(bf16[1024,256]{1,0:T(8,128)(2,1)S(1)} %collective-permute-done.2.rest_2_), channel_id=1, source_target_pairs={{0,2},{2,384},{384,386},{386,0},{1,3},{3,385},{385,387},{387,1},{4... | collective-permute-start | bytes 1572872 | tf_op jit(solution)/shard_map/ppermute | solution.py:28
  57.7 12.7 %collective-permute-start.12 = (bf16[1024,256]{1,0:T(8,128)(2,1)S(1)}, bf16[1024,256]{1,0:T(8,128)(2,1)}, u32[]{:S(2)}, u32[]{:S(2)}) collective-permute-start(bf16[1024,256]{1,0:T(8,128)(2,1)S(1)} %collective-permute-done.5.rest_5_), channel_id=1, source_target_pairs={{0,1},{1,0},{2,3},{3,2},{4,5},{5,4},{6,7},{7,6},{8,9},{9,8},{10,11... | collective-permute-start | bytes 1572872 | tf_op jit(solution)/shard_map/ppermute | solution.py:79
  59.9 23.4 %collective-permute-start.1 = (bf16[1024,256]{1,0:T(8,128)(2,1)}, bf16[1024,256]{1,0:T(8,128)(2,1)}, u32[]{:S(2)}, u32[]{:S(2)}) collective-permute-start(bf16[1024,256]{1,0:T(8,128)(2,1)} %collective-permute-done.rest_4_), channel_id=1, source_target_pairs={{0,2},{2,384},{384,386},{386,0},{1,3},{3,385},{385,387},{387,1},{4... | collective-permute-start | bytes 1572872 | tf_op jit(solution)/shard_map/ppermute | solution.py:28
  65.2 20.9 %collective-permute-start.4 = (bf16[1024,256]{1,0:T(8,128)(2,1)}, bf16[1024,256]{1,0:T(8,128)(2,1)}, u32[]{:S(2)}, u32[]{:S(2)}) collective-permute-start(bf16[1024,256]{1,0:T(8,128)(2,1)} %collective-permute-done.3.rest_7_), channel_id=1, source_target_pairs={{0,386},{2,0},{384,2},{386,384},{1,387},{3,1},{385,3},{387,385},{4... | collective-permute-start | bytes 1572872 | tf_op jit(solution)/shard_map/ppermute | solution.py:28
  70.4 18.0 %collective-permute-start.11 = (bf16[1024,256]{1,0:T(8,128)(2,1)}, bf16[1024,256]{1,0:T(8,128)(2,1)S(1)}, u32[]{:S(2)}, u32[]{:S(2)}) collective-permute-start(bf16[1024,256]{1,0:T(8,128)(2,1)} %collective-permute-done.rest_4_), channel_id=1, source_target_pairs={{0,1},{1,0},{2,3},{3,2},{4,5},{5,4},{6,7},{7,6},{8,9},{9,8},{10,11... | collective-permute-start | bytes 1572872 | tf_op jit(solution)/shard_map/ppermute | solution.py:79
  73.4 0.8 copy-start.1
  74.2 15.9 %collective-permute-start.14 = (bf16[1024,256]{1,0:T(8,128)(2,1)}, bf16[1024,256]{1,0:T(8,128)(2,1)S(1)}, u32[]{:S(2)}, u32[]{:S(2)}) collective-permute-start(bf16[1024,256]{1,0:T(8,128)(2,1)} %collective-permute-done.3.rest_7_), channel_id=1, source_target_pairs={{0,1},{1,0},{2,3},{3,2},{4,5},{5,4},{6,7},{7,6},{8,9},{9,8},{10,11... | collective-permute-start | bytes 1572872 | tf_op jit(solution)/shard_map/ppermute | solution.py:79
  76.2 13.1 %collective-permute-start.13 = (bf16[1024,256]{1,0:T(8,128)(2,1)}, bf16[1024,256]{1,0:T(8,128)(2,1)S(1)}, u32[]{:S(2)}, u32[]{:S(2)}) collective-permute-start(bf16[1024,256]{1,0:T(8,128)(2,1)} %collective-permute-done.6.rest_6_), channel_id=1, source_target_pairs={{0,1},{1,0},{2,3},{3,2},{4,5},{5,4},{6,7},{7,6},{8,9},{9,8},{10,11... | collective-permute-start | bytes 1572872 | tf_op jit(solution)/shard_map/ppermute | solution.py:79
  83.4 7.6 %collective-permute-start.8 = (bf16[1024,256]{1,0:T(8,128)(2,1)}, bf16[1024,256]{1,0:T(8,128)(2,1)S(1)}, u32[]{:S(2)}, u32[]{:S(2)}) collective-permute-start(bf16[1024,256]{1,0:T(8,128)(2,1)} %collective-permute-done.1.rest_1_), channel_id=1, source_target_pairs={{0,1},{1,0},{2,3},{3,2},{4,5},{5,4},{6,7},{7,6},{8,9},{9,8},{10,11... | collective-permute-start | bytes 1572872 | tf_op jit(solution)/shard_map/ppermute | solution.py:79
  86.1 5.7 %collective-permute-start.10 = (bf16[1024,256]{1,0:T(8,128)(2,1)}, bf16[1024,256]{1,0:T(8,128)(2,1)S(1)}, u32[]{:S(2)}, u32[]{:S(2)}) collective-permute-start(bf16[1024,256]{1,0:T(8,128)(2,1)} %collective-permute-done.4.rest_3_), channel_id=1, source_target_pairs={{0,1},{1,0},{2,3},{3,2},{4,5},{5,4},{6,7},{7,6},{8,9},{9,8},{10,11... | collective-permute-start | bytes 1572872 | tf_op jit(solution)/shard_map/ppermute | solution.py:79
  88.4 0.8 copy-start.3
  89.3 0.8 copy-start.7
  90.1 0.8 copy-start.5
  90.9 0.8 copy-start.9
  91.8 0.8 copy-start.11
  98.7 2.3 %copy-start = (bf16[288,8192]{1,0:T(8,128)(2,1)S(1)}, bf16[288,8192]{1,0:T(8,128)(2,1)}, u32[]{:S(2)}) copy-start(bf16[288,8192]{1,0:T(8,128)(2,1)} %all-gather.2.cloned.1.call-done.left_ref) | copy-start | bytes 14155780
  101.0 1.0 copy-start.2
  102.1 1.0 copy-start.4
  103.1 1.0 copy-start.6
  104.2 1.0 copy-start.8
  105.2 1.0 copy-start.10
  106.3 1.0 copy-start.12
Sparse Core Ops, SparseCore 0:
  32.9 65.7 all-gather.1

commit v3 on v2

--- a/solution.py
+++ b/solution.py
@@ -16,7 +16,7 @@
 PART_ROWS = EDGE // PARTS
 SLICES = 8
 SWAP = [(0, 1), (1, 0)]
-MIB = 1 << 20
+GRANT = 24 << 20
 
 
 def expand(mask, dtype):
@@ -28,28 +28,39 @@
     return lax.ppermute(value, RING, [(i, (i + step) % 4) for i in range(4)])
 
 
-def contract(place_ref, left_ref, select_ref, *rest):
-    pieces, (out_ref, slab_ref, total_ref, sems) = rest[:-4], rest[-4:]
-    depth, width = pieces[0].shape
+def contract(place_ref, select_hbm_ref, left_ref, *rest):
+    pieces, (out_ref, select_ref, slab_ref, right_ref, total_ref, sems, select_sem) = rest[:-7], rest[-7:]
+    depth = pieces[0].shape[0]
     copies = []
     for number in range(SLICES):
         begin = pl.multiple_of(place_ref[number, 0] * depth, depth)
-        copy = pltpu.make_async_copy(
-            left_ref.at[:, pl.ds(begin, depth)], slab_ref.at[number], sems.at[number]
-        )
-        copy.start()
-        copies.append(copy)
+        started = [
+            pltpu.make_async_copy(pieces[2 * number], right_ref.at[2 * number], sems.at[number, 0]),
+            pltpu.make_async_copy(
+                left_ref.at[:, pl.ds(begin, depth)], slab_ref.at[number], sems.at[number, 1]
+            ),
+            pltpu.make_async_copy(
+                pieces[2 * number + 1], right_ref.at[2 * number + 1], sems.at[number, 2]
+            ),
+        ]
+        for copy in started:
+            copy.start()
+        copies.append(started)
+    select_copy = pltpu.make_async_copy(select_hbm_ref, select_ref, select_sem)
+    select_copy.start()
     for number in range(SLICES):
-        copies[number].wait()
+        for copy in copies[number]:
+            copy.wait()
         for side in range(2):
             term = jnp.dot(
-                slab_ref[number], pieces[2 * number + side][...], preferred_element_type=jnp.float32
+                slab_ref[number], right_ref[2 * number + side], preferred_element_type=jnp.float32
             )
             half = place_ref[number, 1 + side]
             if number == 0:
                 total_ref[half] = term
             else:
                 total_ref[half] += term
+    select_copy.wait()
     rows = select_ref.shape[0]
     for half in range(2):
         rounded = total_ref[half].astype(jnp.bfloat16)
@@ -99,30 +110,34 @@
     earlier = positions[:, None] > positions[None, :]
     slot_index = jnp.sum((same_owner & earlier).astype(jnp.int32), axis=1)
     destination = owners * CAP + slot_index
-    held = destination.reshape(2, SIZES["z"], local_tiles).transpose(1, 0, 2).reshape(tile_total)
-    source_row = (held[:, None] * PART_ROWS + jnp.arange(PART_ROWS, dtype=jnp.int32)).reshape(-1)
+    order = destination.reshape(2, SIZES["z"], local_tiles).transpose(1, 0, 2).reshape(tile_total)
+    source_row = (order[:, None] * PART_ROWS + jnp.arange(PART_ROWS, dtype=jnp.int32)).reshape(-1)
     owner_rows = CAP * PART_ROWS
     source_row = source_row // owner_rows * (2 * owner_rows) + source_row % owner_rows
     source_row = jnp.concatenate([source_row, source_row + owner_rows])
     slot_rows = jnp.arange(2 * slot_total * PART_ROWS, dtype=jnp.int32)
     selector = (slot_rows[:, None] == source_row[None, :]).astype(jnp.bfloat16)
 
-    vmem = pl.BlockSpec(memory_space=pltpu.VMEM)
+    vmem, anywhere = pl.BlockSpec(memory_space=pltpu.VMEM), pl.BlockSpec(memory_space=pl.ANY)
+    held = [pltpu.with_memory_space_constraint(value, pltpu.HBM) for value in [selector, left] + here + there]
     slots = pl.pallas_call(
         contract,
         out_shape=jax.ShapeDtypeStruct((2 * selector.shape[0], LANES), jnp.bfloat16),
-        in_specs=[pl.BlockSpec(memory_space=pltpu.SMEM), pl.BlockSpec(memory_space=pl.ANY)] + [vmem] * 17,
+        in_specs=[pl.BlockSpec(memory_space=pltpu.SMEM)] + [anywhere] * 18,
         out_specs=vmem,
         scratch_shapes=[
+            pltpu.VMEM(selector.shape, jnp.bfloat16),
             pltpu.VMEM((SLICES, left.shape[0], panels * depth), jnp.bfloat16),
+            pltpu.VMEM((2 * SLICES, panels * depth, width), jnp.bfloat16),
             pltpu.VMEM((2, left.shape[0], width), jnp.float32),
-            pltpu.SemaphoreType.DMA((SLICES,)),
+            pltpu.SemaphoreType.DMA((SLICES, 3)),
+            pltpu.SemaphoreType.DMA,
         ],
-        compiler_params=pltpu.CompilerParams(vmem_limit_bytes=40 * MIB),
+        compiler_params=pltpu.CompilerParams(vmem_limit_bytes=GRANT),
         cost_estimate=pl.CostEstimate(
             flops=2 * left.size * 2 * width, bytes_accessed=4 * left.size, transcendentals=0
         ),
-    )(place, left, selector, *here, *there)
+    )(place, *held)
 
     received = lax.all_to_all(slots, OWNERS, split_axis=0, concat_axis=0, tiled=True)
     received = received.reshape(2, SIZES["yq"], SLICES, 2, CAP, PART_ROWS, LANES).astype(jnp.float32)

time: 151 us -> 142 us (0.940)
  local copies, waits for them, and re-layouts: 18.4 us -> 7.36 us
  waiting for transfers between devices: 18.1 us -> 19.7 us
    unnamed x33 -> x27, local copies, waits for them, and re-layouts: 13.7 us -> 2.66 us
where the time goes in v3:
time: 142 us; the launch traced here: 141 us
  blocking collectives  49.1 us (35%)
  starting transfers between devices  40.1 us (28%)
  waiting for transfers between devices  19.7 us (14%)
  between operations  14 us (10%)
  local copies, waits for them, and re-layouts  7.36 us (5%)
  Pallas kernels  6.88 us (5%)
  other arithmetic  4.07 us (3%)
    all_to_all x1, blocking collectives, body(): lax.all_to_all(slots, OWNERS, split_axis=0, concat_axis=0, tiled=True)  27.6 us
    all_to_all x1, blocking collectives, body(): lax.all_to_all(parts, GROUP, split_axis=0, concat_axis=0, tiled=True)  21.5 us
    ppermute x8, starting transfers between devices, body(): there = [lax.ppermute(value, 'core', SWAP) for value in here]  19.5 us
    ppermute x6, starting transfers between devices, turn(): return lax.ppermute(value, RING, [(i, (i + step) % 4) for i in range(4)])  17.8 us
    ppermute x6, waiting for transfers between devices, turn(): return lax.ppermute(value, RING, [(i, (i + step) % 4) for i in range(4)])  9.01 us
    pallas_call x1, Pallas kernels, body(): pl.pallas_call(contract, out_shape=jax.ShapeDtypeStruct((2 * selector.sha...  6.88 us
    all_gather x1, waiting for transfers between devices, body(): left = lax.all_gather(traded, 'z', axis=0, tiled=True)  6.87 us
    ppermute x1, waiting for transfers between devices, body(): across = lax.ppermute(own, 'yb', SWAP)  3.8 us
  transfers between devices with their start and end apart: 16, of which 4 were waited for; matrix products, arithmetic and copies ran while one was open for 2% of the time, Pallas kernels for 0%

profile of v3, /device:TPU:1, one launch (start us, length us, event | category | flops | bytes accessed | tf_op | source)
XLA Modules:
  0.0 141.2 jit_solution(2088798636799527826)
XLA Ops:
  6.5 0.7 convert_element_type.36
  7.8 1.1 mul.79
  8.9 0.4 copy.59
  9.6 21.5 %all_to_all.14 = bf16[16,24,512]{2,1,0:T(8,128)(2,1)S(1)} all-to-all(bf16[16,24,512]{2,1,0:T(8,128)(2,1)S(1)} %copy.61), channel_id=1, replica_groups=mesh['xh'=2,'z'=12,'yq'=4,'yb'=2,'xl'=2,'core'=2] {'xh','yb','xl','core'}, dimensions={0} | all-to-all | bytes 786432 | tf_op jit(solution)/shard_map/all_to_all | solution.py:103
  31.3 0.4 copy.63
  31.7 1.1 reshape.61
  33.5 2.7 %collective-permute-start.2 = (bf16[1024,256]{1,0:T(8,128)(2,1)S(1)}, bf16[1024,256]{1,0:T(8,128)(2,1)S(1)}, u32[]{:S(2)}, u32[]{:S(2)}) collective-permute-start(bf16[1024,256]{1,0:T(8,128)(2,1)S(1)} %bitcast.51), channel_id=1, source_target_pairs={{0,4},{4,0},{1,5},{5,1},{2,6},{6,2},{3,7},{7,3},{8,12},{12,8},{9,1... | collective-permute-start | bytes 1572872 | tf_op jit(solution)/shard_map/ppermute | solution.py:82
  36.2 2.3 %collective-permute-start.7 = (bf16[1024,256]{1,0:T(8,128)(2,1)S(1)}, bf16[1024,256]{1,0:T(8,128)(2,1)S(1)}, u32[]{:S(2)}, u32[]{:S(2)}) collective-permute-start(bf16[1024,256]{1,0:T(8,128)(2,1)S(1)} %bitcast.52), channel_id=1, source_target_pairs={{0,1},{1,0},{2,3},{3,2},{4,5},{5,4},{6,7},{7,6},{8,9},{9,8},{10,11... | collective-permute-start | bytes 1572872 | tf_op jit(solution)/shard_map/ppermute | solution.py:90
  38.5 3.0 %collective-permute-start.5 = (bf16[1024,256]{1,0:T(8,128)(2,1)S(1)}, bf16[1024,256]{1,0:T(8,128)(2,1)S(1)}, u32[]{:S(2)}, u32[]{:S(2)}) collective-permute-start(bf16[1024,256]{1,0:T(8,128)(2,1)S(1)} %bitcast.53), channel_id=1, source_target_pairs={{0,386},{2,0},{384,2},{386,384},{1,387},{3,1},{385,3},{387,385},{4... | collective-permute-start | bytes 1572872 | tf_op jit(solution)/shard_map/ppermute | solution.py:28
  41.5 2.3 %collective-permute-start = (bf16[1024,256]{1,0:T(8,128)(2,1)S(1)}, bf16[1024,256]{1,0:T(8,128)(2,1)S(1)}, u32[]{:S(2)}, u32[]{:S(2)}) collective-permute-start(bf16[1024,256]{1,0:T(8,128)(2,1)S(1)} %bitcast.54), channel_id=1, source_target_pairs={{0,2},{2,384},{384,386},{386,0},{1,3},{3,385},{385,387},{387,1},{4... | collective-permute-start | bytes 1572872 | tf_op jit(solution)/shard_map/ppermute | solution.py:28
  43.8 3.8 %collective-permute-done.2.rest_2_ = bf16[1024,256]{1,0:T(8,128)(2,1)S(1)} collective-permute-done((bf16[1024,256]{1,0:T(8,128)(2,1)S(1)}, bf16[1024,256]{1,0:T(8,128)(2,1)S(1)}, u32[]{:S(2)}, u32[]{:S(2)}) %collective-permute-start.2) | collective-permute-done | bytes 524320 | tf_op jit(solution)/shard_map/ppermute | solution.py:82
  47.6 4.0 %collective-permute-start.3 = (bf16[1024,256]{1,0:T(8,128)(2,1)S(1)}, bf16[1024,256]{1,0:T(8,128)(2,1)S(1)}, u32[]{:S(2)}, u32[]{:S(2)}) collective-permute-start(bf16[1024,256]{1,0:T(8,128)(2,1)S(1)} %collective-permute-done.2.rest_2_), channel_id=1, source_target_pairs={{0,386},{2,0},{384,2},{386,384},{1,387},{3,1},{385,3},{387,385},{4... | collective-permute-start | bytes 1572872 | tf_op jit(solution)/shard_map/ppermute | solution.py:28
  52.2 3.2 %collective-permute-start.9 = (bf16[1024,256]{1,0:T(8,128)(2,1)S(1)}, bf16[1024,256]{1,0:T(8,128)(2,1)}, u32[]{:S(2)}, u32[]{:S(2)}) collective-permute-start(bf16[1024,256]{1,0:T(8,128)(2,1)S(1)} %collective-permute-done.2.rest_2_), channel_id=1, source_target_pairs={{0,1},{1,0},{2,3},{3,2},{4,5},{5,4},{6,7},{7,6},{8,9},{9,8},{10,11... | collective-permute-start | bytes 1572872 | tf_op jit(solution)/shard_map/ppermute | solution.py:90
  55.4 2.3 %collective-permute-start.6 = (bf16[1024,256]{1,0:T(8,128)(2,1)S(1)}, bf16[1024,256]{1,0:T(8,128)(2,1)}, u32[]{:S(2)}, u32[]{:S(2)}) collective-permute-start(bf16[1024,256]{1,0:T(8,128)(2,1)S(1)} %collective-permute-done.2.rest_2_), channel_id=1, source_target_pairs={{0,2},{2,384},{384,386},{386,0},{1,3},{3,385},{385,387},{387,1},{4... | collective-permute-start | bytes 1572872 | tf_op jit(solution)/shard_map/ppermute | solution.py:28
  57.8 2.2 %collective-permute-start.12 = (bf16[1024,256]{1,0:T(8,128)(2,1)S(1)}, bf16[1024,256]{1,0:T(8,128)(2,1)}, u32[]{:S(2)}, u32[]{:S(2)}) collective-permute-start(bf16[1024,256]{1,0:T(8,128)(2,1)S(1)} %collective-permute-done.5.rest_5_), channel_id=1, source_target_pairs={{0,1},{1,0},{2,3},{3,2},{4,5},{5,4},{6,7},{7,6},{8,9},{9,8},{10,11... | collective-permute-start | bytes 1572872 | tf_op jit(solution)/shard_map/ppermute | solution.py:90
  60.0 1.9 %collective-permute-start.1 = (bf16[1024,256]{1,0:T(8,128)(2,1)S(1)}, bf16[1024,256]{1,0:T(8,128)(2,1)}, u32[]{:S(2)}, u32[]{:S(2)}) collective-permute-start(bf16[1024,256]{1,0:T(8,128)(2,1)S(1)} %collective-permute-done.rest_4_), channel_id=1, source_target_pairs={{0,2},{2,384},{384,386},{386,0},{1,3},{3,385},{385,387},{387,1},{4... | collective-permute-start | bytes 1572872 | tf_op jit(solution)/shard_map/ppermute | solution.py:28
  61.9 3.3 %collective-permute-done.3.rest_7_ = bf16[1024,256]{1,0:T(8,128)(2,1)S(1)} collective-permute-done((bf16[1024,256]{1,0:T(8,128)(2,1)S(1)}, bf16[1024,256]{1,0:T(8,128)(2,1)S(1)}, u32[]{:S(2)}, u32[]{:S(2)}) %collective-permute-start.3) | collective-permute-done | bytes 524320 | tf_op jit(solution)/shard_map/ppermute | solution.py:28
  65.2 4.3 %collective-permute-start.4 = (bf16[1024,256]{1,0:T(8,128)(2,1)S(1)}, bf16[1024,256]{1,0:T(8,128)(2,1)}, u32[]{:S(2)}, u32[]{:S(2)}) collective-permute-start(bf16[1024,256]{1,0:T(8,128)(2,1)S(1)} %collective-permute-done.3.rest_7_), channel_id=1, source_target_pairs={{0,386},{2,0},{384,2},{386,384},{1,387},{3,1},{385,3},{387,385},{4... | collective-permute-start | bytes 1572872 | tf_op jit(solution)/shard_map/ppermute | solution.py:28
  70.4 2.9 %collective-permute-start.11 = (bf16[1024,256]{1,0:T(8,128)(2,1)S(1)}, bf16[1024,256]{1,0:T(8,128)(2,1)S(1)}, u32[]{:S(2)}, u32[]{:S(2)}) collective-permute-start(bf16[1024,256]{1,0:T(8,128)(2,1)S(1)} %collective-permute-done.rest_4_), channel_id=1, source_target_pairs={{0,1},{1,0},{2,3},{3,2},{4,5},{5,4},{6,7},{7,6},{8,9},{9,8},{10,11... | collective-permute-start | bytes 1572872 | tf_op jit(solution)/shard_map/ppermute | solution.py:90
  73.3 1.9 %collective-permute-start.14 = (bf16[1024,256]{1,0:T(8,128)(2,1)S(1)}, bf16[1024,256]{1,0:T(8,128)(2,1)S(1)}, u32[]{:S(2)}, u32[]{:S(2)}) collective-permute-start(bf16[1024,256]{1,0:T(8,128)(2,1)S(1)} %collective-permute-done.3.rest_7_), channel_id=1, source_target_pairs={{0,1},{1,0},{2,3},{3,2},{4,5},{5,4},{6,7},{7,6},{8,9},{9,8},{10,11... | collective-permute-start | bytes 1572872 | tf_op jit(solution)/shard_map/ppermute | solution.py:90
  75.3 2.4 %collective-permute-start.13 = (bf16[1024,256]{1,0:T(8,128)(2,1)}, bf16[1024,256]{1,0:T(8,128)(2,1)S(1)}, u32[]{:S(2)}, u32[]{:S(2)}) collective-permute-start(bf16[1024,256]{1,0:T(8,128)(2,1)} %collective-permute-done.6.rest_6_), channel_id=1, source_target_pairs={{0,1},{1,0},{2,3},{3,2},{4,5},{5,4},{6,7},{7,6},{8,9},{9,8},{10,11... | collective-permute-start | bytes 1572872 | tf_op jit(solution)/shard_map/ppermute | solution.py:90
  77.7 5.7 %collective-permute-done.1.rest_1_ = bf16[1024,256]{1,0:T(8,128)(2,1)} collective-permute-done((bf16[1024,256]{1,0:T(8,128)(2,1)S(1)}, bf16[1024,256]{1,0:T(8,128)(2,1)}, u32[]{:S(2)}, u32[]{:S(2)}) %collective-permute-start.1) | collective-permute-done | bytes 524320 | tf_op jit(solution)/shard_map/ppermute | solution.py:28
  83.4 2.7 %collective-permute-start.8 = (bf16[1024,256]{1,0:T(8,128)(2,1)}, bf16[1024,256]{1,0:T(8,128)(2,1)S(1)}, u32[]{:S(2)}, u32[]{:S(2)}) collective-permute-start(bf16[1024,256]{1,0:T(8,128)(2,1)} %collective-permute-done.1.rest_1_), channel_id=1, source_target_pairs={{0,1},{1,0},{2,3},{3,2},{4,5},{5,4},{6,7},{7,6},{8,9},{9,8},{10,11... | collective-permute-start | bytes 1572872 | tf_op jit(solution)/shard_map/ppermute | solution.py:90
  86.1 1.9 %collective-permute-start.10 = (bf16[1024,256]{1,0:T(8,128)(2,1)}, bf16[1024,256]{1,0:T(8,128)(2,1)}, u32[]{:S(2)}, u32[]{:S(2)}) collective-permute-start(bf16[1024,256]{1,0:T(8,128)(2,1)} %collective-permute-done.4.rest_3_), channel_id=1, source_target_pairs={{0,1},{1,0},{2,3},{3,2},{4,5},{5,4},{6,7},{7,6},{8,9},{9,8},{10,11... | collective-permute-start | bytes 1572872 | tf_op jit(solution)/shard_map/ppermute | solution.py:90
  88.1 1.3 fusion.select_hbm_ref
  89.5 0.8 copy-done.6
  90.5 0.6 copy-done.7
  91.1 0.8 copy-done.9
  91.9 6.9 %all-gather.2.cloned.1.call-done.left_ref = bf16[288,8192]{1,0:T(8,128)(2,1)} async-done(((bf16[24,8192]{1,0:T(8,128)(2,1)}), bf16[288,8192]{1,0:T(8,128)(2,1)}) %all-gather.2.cloned.1.call-update) | async-done | bytes 4718608 | tf_op jit(solution)/shard_map/all_gather | solution.py:106
  98.8 6.9 %shard_map.55 = bf16[1536,128]{1,0:T(8,128)(2,1)S(1)} custom-call(s32[8,3]{1,0:T(8,128)S(1)} %stack.127.place_ref, bf16[768,576]{1,0:T(8,128)(2,1)} %fusion.select_hbm_ref, bf16[288,8192]{1,0:T(8,128)(2,1)} %all-gather.2.cloned.1.call-done.left_ref, bf16[1024,256]{1,0:T(8,128)(2,1)} %bitcast.55, bf16[1024,256]{1,0:T(8,128)(2,1)} %collective-permute-done.1.rest_1_, ...), custom_call_target="tpu_custom_call" | custom-call | flops 2415919104 | bytes 9437184 | tf_op jit(solution)/shard_map/pallas_call | solution.py:123
  105.7 27.6 %all_to_all.15 = bf16[64,24,128]{2,1,0:T(8,128)(2,1)S(1)} all-to-all(bf16[64,24,128]{2,1,0:T(8,128)(2,1)S(1)} %bitcast.50), channel_id=1, replica_groups=mesh['xh'=2,'z'=12,'yq'=4,'yb'=2,'xl'=2,'core'=2] {'xh','yq','yb','xl','..., dimensions={0} | all-to-all | bytes 786432 | tf_op jit(solution)/shard_map/all_to_all | solution.py:142
  133.6 0.8 reshape.63
  (70 shorter events, 3.5 us)
Async XLA Ops:
  6.5 92.2 %all-gather.2.cloned.1.call-start = ((), (), s32[]{:S(2)}) async-start(), calls=%async_computation.2 | async-start | bytes 5111808 | tf_op jit(solution)/shard_map/all_gather | solution.py:106
  9.6 23.2 %copy-start.11 = (s32[2,8,4]{1,2,0:T(4,128)S(1)}, s32[2,8,4]{1,2,0:T(4,128)}, u32[]{:S(2)}) copy-start(s32[2,8,4]{1,2,0:T(4,128)} %param.8) | copy-start | bytes 772
  9.6 23.4 %copy-start.10 = (bf16[2,512,256]{2,1,0:T(8,128)(2,1)S(1)}, bf16[2,512,256]{2,1,0:T(8,128)(2,1)}, u32[]{:S(2)}) copy-start(bf16[2,512,256]{2,1,0:T(8,128)(2,1)} %param.6) | copy-start | bytes 1572868
  32.8 18.9 %copy-start.12 = (s32[72]{0:T(128)S(1)}, s32[72]{0:T(128)}, u32[]{:S(2)}) copy-start(s32[72]{0:T(128)} %param.9) | copy-start | bytes 868
  33.5 65.3 %copy-start = (bf16[2,512,256]{2,1,0:T(8,128)(2,1)}, bf16[2,512,256]{2,1,0:T(8,128)(2,1)S(1)}, u32[]{:S(2)}) copy-start(bf16[2,512,256]{2,1,0:T(8,128)(2,1)S(1)} %copy.65) | copy-start | bytes 1572868
  33.5 14.1 %collective-permute-start.2 = (bf16[1024,256]{1,0:T(8,128)(2,1)S(1)}, bf16[1024,256]{1,0:T(8,128)(2,1)S(1)}, u32[]{:S(2)}, u32[]{:S(2)}) collective-permute-start(bf16[1024,256]{1,0:T(8,128)(2,1)S(1)} %bitcast.51), channel_id=1, source_target_pairs={{0,4},{4,0},{1,5},{5,1},{2,6},{6,2},{3,7},{7,3},{8,12},{12,8},{9,1... | collective-permute-start | bytes 1572872 | tf_op jit(solution)/shard_map/ppermute | solution.py:82
  36.2 19.2 %collective-permute-start.7 = (bf16[1024,256]{1,0:T(8,128)(2,1)S(1)}, bf16[1024,256]{1,0:T(8,128)(2,1)S(1)}, u32[]{:S(2)}, u32[]{:S(2)}) collective-permute-start(bf16[1024,256]{1,0:T(8,128)(2,1)S(1)} %bitcast.52), channel_id=1, source_target_pairs={{0,1},{1,0},{2,3},{3,2},{4,5},{5,4},{6,7},{7,6},{8,9},{9,8},{10,11... | collective-permute-start | bytes 1572872 | tf_op jit(solution)/shard_map/ppermute | solution.py:90
  38.5 19.3 %collective-permute-start.5 = (bf16[1024,256]{1,0:T(8,128)(2,1)S(1)}, bf16[1024,256]{1,0:T(8,128)(2,1)S(1)}, u32[]{:S(2)}, u32[]{:S(2)}) collective-permute-start(bf16[1024,256]{1,0:T(8,128)(2,1)S(1)} %bitcast.53), channel_id=1, source_target_pairs={{0,386},{2,0},{384,2},{386,384},{1,387},{3,1},{385,3},{387,385},{4... | collective-permute-start | bytes 1572872 | tf_op jit(solution)/shard_map/ppermute | solution.py:28
  41.5 18.4 %collective-permute-start = (bf16[1024,256]{1,0:T(8,128)(2,1)S(1)}, bf16[1024,256]{1,0:T(8,128)(2,1)S(1)}, u32[]{:S(2)}, u32[]{:S(2)}) collective-permute-start(bf16[1024,256]{1,0:T(8,128)(2,1)S(1)} %bitcast.54), channel_id=1, source_target_pairs={{0,2},{2,384},{384,386},{386,0},{1,3},{3,385},{385,387},{387,1},{4... | collective-permute-start | bytes 1572872 | tf_op jit(solution)/shard_map/ppermute | solution.py:28
  47.6 51.1 %copy-start.1 = (bf16[1024,256]{1,0:T(8,128)(2,1)}, bf16[1024,256]{1,0:T(8,128)(2,1)S(1)}, u32[]{:S(2)}) copy-start(bf16[1024,256]{1,0:T(8,128)(2,1)S(1)} %collective-permute-done.2.rest_2_) | copy-start | bytes 1572868
  47.6 17.6 %collective-permute-start.3 = (bf16[1024,256]{1,0:T(8,128)(2,1)S(1)}, bf16[1024,256]{1,0:T(8,128)(2,1)S(1)}, u32[]{:S(2)}, u32[]{:S(2)}) collective-permute-start(bf16[1024,256]{1,0:T(8,128)(2,1)S(1)} %collective-permute-done.2.rest_2_), channel_id=1, source_target_pairs={{0,386},{2,0},{384,2},{386,384},{1,387},{3,1},{385,3},{387,385},{4... | collective-permute-start | bytes 1572872 | tf_op jit(solution)/shard_map/ppermute | solution.py:28
  52.2 21.2 %collective-permute-start.9 = (bf16[1024,256]{1,0:T(8,128)(2,1)S(1)}, bf16[1024,256]{1,0:T(8,128)(2,1)}, u32[]{:S(2)}, u32[]{:S(2)}) collective-permute-start(bf16[1024,256]{1,0:T(8,128)(2,1)S(1)} %collective-permute-done.2.rest_2_), channel_id=1, source_target_pairs={{0,1},{1,0},{2,3},{3,2},{4,5},{5,4},{6,7},{7,6},{8,9},{9,8},{10,11... | collective-permute-start | bytes 1572872 | tf_op jit(solution)/shard_map/ppermute | solution.py:90
  55.4 43.4 %copy-start.2 = (bf16[1024,256]{1,0:T(8,128)(2,1)}, bf16[1024,256]{1,0:T(8,128)(2,1)S(1)}, u32[]{:S(2)}) copy-start(bf16[1024,256]{1,0:T(8,128)(2,1)S(1)} %collective-permute-done.7.rest_8_) | copy-start | bytes 1572868
  55.4 19.9 %collective-permute-start.6 = (bf16[1024,256]{1,0:T(8,128)(2,1)S(1)}, bf16[1024,256]{1,0:T(8,128)(2,1)}, u32[]{:S(2)}, u32[]{:S(2)}) collective-permute-start(bf16[1024,256]{1,0:T(8,128)(2,1)S(1)} %collective-permute-done.2.rest_2_), channel_id=1, source_target_pairs={{0,2},{2,384},{384,386},{386,0},{1,3},{3,385},{385,387},{387,1},{4... | collective-permute-start | bytes 1572872 | tf_op jit(solution)/shard_map/ppermute | solution.py:28
  57.8 41.0 %copy-start.3 = (bf16[1024,256]{1,0:T(8,128)(2,1)}, bf16[1024,256]{1,0:T(8,128)(2,1)S(1)}, u32[]{:S(2)}) copy-start(bf16[1024,256]{1,0:T(8,128)(2,1)S(1)} %collective-permute-done.5.rest_5_) | copy-start | bytes 1572868
  57.8 12.7 %collective-permute-start.12 = (bf16[1024,256]{1,0:T(8,128)(2,1)S(1)}, bf16[1024,256]{1,0:T(8,128)(2,1)}, u32[]{:S(2)}, u32[]{:S(2)}) collective-permute-start(bf16[1024,256]{1,0:T(8,128)(2,1)S(1)} %collective-permute-done.5.rest_5_), channel_id=1, source_target_pairs={{0,1},{1,0},{2,3},{3,2},{4,5},{5,4},{6,7},{7,6},{8,9},{9,8},{10,11... | collective-permute-start | bytes 1572872 | tf_op jit(solution)/shard_map/ppermute | solution.py:90
  60.0 38.8 %copy-start.4 = (bf16[1024,256]{1,0:T(8,128)(2,1)}, bf16[1024,256]{1,0:T(8,128)(2,1)S(1)}, u32[]{:S(2)}) copy-start(bf16[1024,256]{1,0:T(8,128)(2,1)S(1)} %collective-permute-done.rest_4_) | copy-start | bytes 1572868
  60.0 23.4 %collective-permute-start.1 = (bf16[1024,256]{1,0:T(8,128)(2,1)S(1)}, bf16[1024,256]{1,0:T(8,128)(2,1)}, u32[]{:S(2)}, u32[]{:S(2)}) collective-permute-start(bf16[1024,256]{1,0:T(8,128)(2,1)S(1)} %collective-permute-done.rest_4_), channel_id=1, source_target_pairs={{0,2},{2,384},{384,386},{386,0},{1,3},{3,385},{385,387},{387,1},{4... | collective-permute-start | bytes 1572872 | tf_op jit(solution)/shard_map/ppermute | solution.py:28
  65.2 33.6 %copy-start.5 = (bf16[1024,256]{1,0:T(8,128)(2,1)}, bf16[1024,256]{1,0:T(8,128)(2,1)S(1)}, u32[]{:S(2)}) copy-start(bf16[1024,256]{1,0:T(8,128)(2,1)S(1)} %collective-permute-done.3.rest_7_) | copy-start | bytes 1572868
  65.2 20.9 %collective-permute-start.4 = (bf16[1024,256]{1,0:T(8,128)(2,1)S(1)}, bf16[1024,256]{1,0:T(8,128)(2,1)}, u32[]{:S(2)}, u32[]{:S(2)}) collective-permute-start(bf16[1024,256]{1,0:T(8,128)(2,1)S(1)} %collective-permute-done.3.rest_7_), channel_id=1, source_target_pairs={{0,386},{2,0},{384,2},{386,384},{1,387},{3,1},{385,3},{387,385},{4... | collective-permute-start | bytes 1572872 | tf_op jit(solution)/shard_map/ppermute | solution.py:28
  70.4 19.0 %collective-permute-start.11 = (bf16[1024,256]{1,0:T(8,128)(2,1)S(1)}, bf16[1024,256]{1,0:T(8,128)(2,1)S(1)}, u32[]{:S(2)}, u32[]{:S(2)}) collective-permute-start(bf16[1024,256]{1,0:T(8,128)(2,1)S(1)} %collective-permute-done.rest_4_), channel_id=1, source_target_pairs={{0,1},{1,0},{2,3},{3,2},{4,5},{5,4},{6,7},{7,6},{8,9},{9,8},{10,11... | collective-permute-start | bytes 1572872 | tf_op jit(solution)/shard_map/ppermute | solution.py:90
  73.3 16.1 %collective-permute-start.14 = (bf16[1024,256]{1,0:T(8,128)(2,1)S(1)}, bf16[1024,256]{1,0:T(8,128)(2,1)S(1)}, u32[]{:S(2)}, u32[]{:S(2)}) collective-permute-start(bf16[1024,256]{1,0:T(8,128)(2,1)S(1)} %collective-permute-done.3.rest_7_), channel_id=1, source_target_pairs={{0,1},{1,0},{2,3},{3,2},{4,5},{5,4},{6,7},{7,6},{8,9},{9,8},{10,11... | collective-permute-start | bytes 1572872 | tf_op jit(solution)/shard_map/ppermute | solution.py:90
  75.3 14.2 %collective-permute-start.13 = (bf16[1024,256]{1,0:T(8,128)(2,1)}, bf16[1024,256]{1,0:T(8,128)(2,1)S(1)}, u32[]{:S(2)}, u32[]{:S(2)}) collective-permute-start(bf16[1024,256]{1,0:T(8,128)(2,1)} %collective-permute-done.6.rest_6_), channel_id=1, source_target_pairs={{0,1},{1,0},{2,3},{3,2},{4,5},{5,4},{6,7},{7,6},{8,9},{9,8},{10,11... | collective-permute-start | bytes 1572872 | tf_op jit(solution)/shard_map/ppermute | solution.py:90
  83.4 6.9 %collective-permute-start.8 = (bf16[1024,256]{1,0:T(8,128)(2,1)}, bf16[1024,256]{1,0:T(8,128)(2,1)S(1)}, u32[]{:S(2)}, u32[]{:S(2)}) collective-permute-start(bf16[1024,256]{1,0:T(8,128)(2,1)} %collective-permute-done.1.rest_1_), channel_id=1, source_target_pairs={{0,1},{1,0},{2,3},{3,2},{4,5},{5,4},{6,7},{7,6},{8,9},{9,8},{10,11... | collective-permute-start | bytes 1572872 | tf_op jit(solution)/shard_map/ppermute | solution.py:90
  86.1 5.8 %collective-permute-start.10 = (bf16[1024,256]{1,0:T(8,128)(2,1)}, bf16[1024,256]{1,0:T(8,128)(2,1)}, u32[]{:S(2)}, u32[]{:S(2)}) collective-permute-start(bf16[1024,256]{1,0:T(8,128)(2,1)} %collective-permute-done.4.rest_3_), channel_id=1, source_target_pairs={{0,1},{1,0},{2,3},{3,2},{4,5},{5,4},{6,7},{7,6},{8,9},{9,8},{10,11... | collective-permute-start | bytes 1572872 | tf_op jit(solution)/shard_map/ppermute | solution.py:90
  89.4 0.8 copy-start.6
  89.5 1.0 copy-start.8
  90.3 0.8 copy-start.7
  91.1 0.8 copy-start.9
Sparse Core Ops, SparseCore 0:
  32.9 65.7 all-gather.1

commit v4 on v3

--- a/solution.py
+++ b/solution.py
@@ -14,6 +14,7 @@
 LANES = 128
 PARTS = 16
 PART_ROWS = EDGE // PARTS
+TILE_BITS, PART_BITS = EDGE.bit_length() - 1, PART_ROWS.bit_length() - 1
 SLICES = 8
 SWAP = [(0, 1), (1, 0)]
 GRANT = 24 << 20
@@ -24,12 +25,65 @@
     return grown.astype(dtype)
 
 
+def one_hot(target):
+    size = target.shape[1]
+    return (lax.broadcasted_iota(jnp.int32, (size, size), 0) == target).astype(jnp.bfloat16)
+
+
+def masked_parts(mask_hbm_ref, amp_hbm_ref, out_ref, mask_ref, amp_ref, sems):
+    copies = [
+        pltpu.make_async_copy(mask_hbm_ref, mask_ref, sems.at[0]),
+        pltpu.make_async_copy(amp_hbm_ref, amp_ref, sems.at[1]),
+    ]
+    for copy in copies:
+        copy.start()
+    panels, rows, depth = amp_ref.shape
+    low = lax.broadcasted_iota(jnp.int32, (depth // EDGE, depth), 0) * EDGE
+    lane = lax.broadcasted_iota(jnp.int32, (depth // EDGE, depth), 1)
+    lane_of = ((lane >= low) & (lane < low + EDGE)).astype(jnp.bfloat16)
+    row = lax.broadcasted_iota(jnp.int32, (1, panels * rows), 1)
+    block, within = row >> TILE_BITS, row & (EDGE - 1)
+    part, inner = within >> PART_BITS, within & (PART_ROWS - 1)
+    order = one_hot(part * (panels * rows // PARTS) + block * PART_ROWS + inner)
+    for copy in copies:
+        copy.wait()
+    factors = []
+    for tile in range(rows // EDGE):
+        mask = mask_ref[tile].astype(jnp.float32).astype(jnp.bfloat16)
+        factors.append(jnp.dot(mask, lane_of, preferred_element_type=jnp.float32).astype(jnp.bfloat16))
+    blocks = [
+        amp_ref[panel, tile * EDGE:(tile + 1) * EDGE, :] * factors[tile][panel:panel + 1]
+        for panel in range(panels)
+        for tile in range(rows // EDGE)
+    ]
+    masked = jnp.concatenate(blocks, axis=0)
+    out_ref[...] = jnp.dot(order, masked, preferred_element_type=jnp.float32).astype(jnp.bfloat16)
+
+
+def join(traded_ref, out_ref):
+    rows, columns = out_ref.shape
+    total, depth = traded_ref.shape
+    half, run = total // 2, rows // 2
+    row = lax.broadcasted_iota(jnp.int32, (1, total), 1)
+    upper = (row >= half).astype(jnp.int32)
+    within = row - half * upper
+    block = jnp.zeros_like(row)
+    for start in range(run, half, run):
+        block += (within >= start).astype(jnp.int32)
+    order = one_hot(within + run * block + run * upper)
+    sorted_rows = jnp.dot(order, traded_ref[...], preferred_element_type=jnp.float32)
+    for index in range(columns // depth):
+        out_ref[:, index * depth:(index + 1) * depth] = sorted_rows[
+            index * rows:(index + 1) * rows
+        ].astype(jnp.bfloat16)
+
+
 def turn(value, step):
     return lax.ppermute(value, RING, [(i, (i + step) % 4) for i in range(4)])
 
 
-def contract(place_ref, select_hbm_ref, left_ref, *rest):
-    pieces, (out_ref, select_ref, slab_ref, right_ref, total_ref, sems, select_sem) = rest[:-7], rest[-7:]
+def contract(place_ref, source_ref, left_ref, *rest):
+    pieces, (out_ref, slab_ref, right_ref, total_ref, sems) = rest[:-5], rest[-5:]
     depth = pieces[0].shape[0]
     copies = []
     for number in range(SLICES):
@@ -46,8 +100,9 @@
         for copy in started:
             copy.start()
         copies.append(started)
-    select_copy = pltpu.make_async_copy(select_hbm_ref, select_ref, select_sem)
-    select_copy.start()
+    rows = out_ref.shape[0] // 2
+    slot_row = lax.broadcasted_iota(jnp.int32, (rows, source_ref.shape[1]), 0)
+    select = (slot_row == source_ref[...]).astype(jnp.bfloat16)
     for number in range(SLICES):
         for copy in copies[number]:
             copy.wait()
@@ -60,12 +115,10 @@
                 total_ref[half] = term
             else:
                 total_ref[half] += term
-    select_copy.wait()
-    rows = select_ref.shape[0]
     for half in range(2):
         rounded = total_ref[half].astype(jnp.bfloat16)
         stacked = jnp.concatenate([rounded[:, :LANES], rounded[:, LANES:]], axis=0)
-        placed = jnp.dot(select_ref[...], stacked, preferred_element_type=jnp.float32)
+        placed = jnp.dot(select, stacked, preferred_element_type=jnp.float32)
         out_ref[half * rows:(half + 1) * rows, :] = placed.astype(jnp.bfloat16)
 
 
@@ -97,12 +150,28 @@
                 place.append(jnp.stack([side * 4 + (one % 2) * 2 + core_at, one // 2, other // 2]))
     place = jnp.stack(place).astype(jnp.int32)
 
-    amp_used = amplitudes * expand(amp_mask, amplitudes.dtype)
-    parts = amp_used.reshape(panels, local_tiles, PARTS, PART_ROWS, depth)
-    parts = parts.transpose(2, 0, 1, 3, 4).reshape(PARTS, panels * local_tiles * PART_ROWS, depth)
+    vmem, anywhere = pl.BlockSpec(memory_space=pltpu.VMEM), pl.BlockSpec(memory_space=pl.ANY)
+    masks = amp_mask.transpose(1, 0, 2)
+    parts = pl.pallas_call(
+        masked_parts,
+        out_shape=jax.ShapeDtypeStruct((panels * rows, depth), jnp.bfloat16),
+        in_specs=[anywhere] * 2,
+        out_specs=vmem,
+        scratch_shapes=[
+            pltpu.VMEM(masks.shape, jnp.int32),
+            pltpu.VMEM(amplitudes.shape, jnp.bfloat16),
+            pltpu.SemaphoreType.DMA((2,)),
+        ],
+        compiler_params=pltpu.CompilerParams(vmem_limit_bytes=GRANT),
+    )(*(pltpu.with_memory_space_constraint(value, pltpu.HBM) for value in (masks, amplitudes)))
     traded = lax.all_to_all(parts, GROUP, split_axis=0, concat_axis=0, tiled=True)
-    traded = traded.reshape(2, SLICES, panels, local_tiles * PART_ROWS, depth)
-    traded = traded.transpose(0, 3, 1, 2, 4).reshape(2 * local_tiles * PART_ROWS, SLICES * panels * depth)
+    traded = pl.pallas_call(
+        join,
+        out_shape=jax.ShapeDtypeStruct((2 * local_tiles * PART_ROWS, SLICES * panels * depth), jnp.bfloat16),
+        in_specs=[vmem],
+        out_specs=vmem,
+        compiler_params=pltpu.CompilerParams(vmem_limit_bytes=GRANT),
+    )(traded)
     left = lax.all_gather(traded, "z", axis=0, tiled=True)
 
     positions = jnp.arange(tile_total, dtype=jnp.int32)
@@ -115,29 +184,24 @@
     owner_rows = CAP * PART_ROWS
     source_row = source_row // owner_rows * (2 * owner_rows) + source_row % owner_rows
     source_row = jnp.concatenate([source_row, source_row + owner_rows])
-    slot_rows = jnp.arange(2 * slot_total * PART_ROWS, dtype=jnp.int32)
-    selector = (slot_rows[:, None] == source_row[None, :]).astype(jnp.bfloat16)
-
-    vmem, anywhere = pl.BlockSpec(memory_space=pltpu.VMEM), pl.BlockSpec(memory_space=pl.ANY)
-    held = [pltpu.with_memory_space_constraint(value, pltpu.HBM) for value in [selector, left] + here + there]
+
+    held = [pltpu.with_memory_space_constraint(value, pltpu.HBM) for value in [left] + here + there]
     slots = pl.pallas_call(
         contract,
-        out_shape=jax.ShapeDtypeStruct((2 * selector.shape[0], LANES), jnp.bfloat16),
-        in_specs=[pl.BlockSpec(memory_space=pltpu.SMEM)] + [anywhere] * 18,
+        out_shape=jax.ShapeDtypeStruct((4 * slot_total * PART_ROWS, LANES), jnp.bfloat16),
+        in_specs=[pl.BlockSpec(memory_space=pltpu.SMEM), vmem] + [anywhere] * 17,
         out_specs=vmem,
         scratch_shapes=[
-            pltpu.VMEM(selector.shape, jnp.bfloat16),
             pltpu.VMEM((SLICES, left.shape[0], panels * depth), jnp.bfloat16),
             pltpu.VMEM((2 * SLICES, panels * depth, width), jnp.bfloat16),
             pltpu.VMEM((2, left.shape[0], width), jnp.float32),
             pltpu.SemaphoreType.DMA((SLICES, 3)),
-            pltpu.SemaphoreType.DMA,
         ],
         compiler_params=pltpu.CompilerParams(vmem_limit_bytes=GRANT),
         cost_estimate=pl.CostEstimate(
             flops=2 * left.size * 2 * width, bytes_accessed=4 * left.size, transcendentals=0
         ),
-    )(place, *held)
+    )(place, source_row[None, :], *held)
 
     received = lax.all_to_all(slots, OWNERS, split_axis=0, concat_axis=0, tiled=True)
     received = received.reshape(2, SIZES["yq"], SLICES, 2, CAP, PART_ROWS, LANES).astype(jnp.float32)

time: 142 us -> 140 us (0.986)
  local copies, waits for them, and re-layouts: 7.36 us -> 3.14 us
  Pallas kernels: 6.88 us -> 9.53 us
  other arithmetic: 4.07 us -> 1.66 us
  waiting for transfers between devices: 19.7 us -> 21.8 us
    pallas_call x1 -> x3, Pallas kernels: 6.88 us -> 9.53 us  [the longest x1 6.87 us: body(): pl.pallas_call(contract, out_shape=jax.ShapeDtypeStruct((4 * slot_total *...]
    ppermute x8, waiting for transfers between devices: 0.02 us -> 1.78 us  [body(): there = [lax.ppermute(value, 'core', SWAP) for value in here]]
  transfers between devices with their start and end apart: 16 -> 16, of which waited for: 4 -> 5; matrix products, arithmetic and copies ran while one was open for 2% -> 3% of each run, Pallas kernels for 0% -> 0%
where the time goes in v4:
time: 140 us; the launch traced here: 139 us
  blocking collectives  48.9 us (35%)
  starting transfers between devices  40.1 us (29%)
  waiting for transfers between devices  21.8 us (16%)
  between operations  13.9 us (10%)
  Pallas kernels  9.53 us (7%)
  local copies, waits for them, and re-layouts  3.14 us (2%)
  other arithmetic  1.66 us (1%)
    all_to_all x1, blocking collectives, body(): lax.all_to_all(slots, OWNERS, split_axis=0, concat_axis=0, tiled=True)  27.5 us
    all_to_all x1, blocking collectives, body(): lax.all_to_all(parts, GROUP, split_axis=0, concat_axis=0, tiled=True)  21.4 us
    ppermute x8, starting transfers between devices, body(): there = [lax.ppermute(value, 'core', SWAP) for value in here]  19.5 us
    ppermute x6, starting transfers between devices, turn(): return lax.ppermute(value, RING, [(i, (i + step) % 4) for i in range(4)])  17.9 us
    ppermute x6, waiting for transfers between devices, turn(): return lax.ppermute(value, RING, [(i, (i + step) % 4) for i in range(4)])  9.26 us
    all_gather x1, waiting for transfers between devices, body(): left = lax.all_gather(traded, 'z', axis=0, tiled=True)  6.94 us
    pallas_call x1, Pallas kernels, body(): pl.pallas_call(contract, out_shape=jax.ShapeDtypeStruct((4 * slot_total *...  6.87 us
    ppermute x1, waiting for transfers between devices, body(): across = lax.ppermute(own, 'yb', SWAP)  3.8 us
  transfers between devices with their start and end apart: 16, of which 5 were waited for; matrix products, arithmetic and copies ran while one was open for 3% of the time, Pallas kernels for 0%

profile of v4, /device:TPU:1, one launch (start us, length us, event | category | flops | bytes accessed | tf_op | source)
XLA Modules:
  0.0 139.1 jit_solution(6603632246782982930)
XLA Ops:
  6.5 1.5 %shard_map.55 = bf16[384,512]{1,0:T(8,128)(2,1)S(1)} custom-call(s32[3,2,8]{2,1,0:T(2,128)} %bitcast.54, bf16[2,192,512]{2,1,0:T(8,128)(2,1)} %amp_hbm_ref.1), custom_call_target="tpu_custom_call" | custom-call | tf_op jit(solution)/shard_map/pallas_call | solution.py:155
  8.1 21.4 %all_to_all.20 = bf16[16,24,512]{2,1,0:T(8,128)(2,1)S(1)} all-to-all(bf16[16,24,512]{2,1,0:T(8,128)(2,1)S(1)} %bitcast.45), channel_id=1, replica_groups=mesh['xh'=2,'z'=12,'yq'=4,'yb'=2,'xl'=2,'core'=2] {'xh','yb','xl','core'}, dimensions={0} | all-to-all | bytes 786432 | tf_op jit(solution)/shard_map/all_to_all | solution.py:167
  29.5 1.1 shard_map.56
  30.6 0.7 convert_element_type.21
  31.5 1.3 copy.19
  32.8 0.2 copy.20
  33.0 2.7 %collective-permute-start.2 = (bf16[1024,256]{1,0:T(8,128)(2,1)S(1)}, bf16[1024,256]{1,0:T(8,128)(2,1)S(1)}, u32[]{:S(2)}, u32[]{:S(2)}) collective-permute-start(bf16[1024,256]{1,0:T(8,128)(2,1)S(1)} %bitcast.46), channel_id=1, source_target_pairs={{0,4},{4,0},{1,5},{5,1},{2,6},{6,2},{3,7},{7,3},{8,12},{12,8},{9,1... | collective-permute-start | bytes 1572872 | tf_op jit(solution)/shard_map/ppermute | solution.py:135
  35.7 2.3 %collective-permute-start.7 = (bf16[1024,256]{1,0:T(8,128)(2,1)S(1)}, bf16[1024,256]{1,0:T(8,128)(2,1)S(1)}, u32[]{:S(2)}, u32[]{:S(2)}) collective-permute-start(bf16[1024,256]{1,0:T(8,128)(2,1)S(1)} %bitcast.47), channel_id=1, source_target_pairs={{0,1},{1,0},{2,3},{3,2},{4,5},{5,4},{6,7},{7,6},{8,9},{9,8},{10,11... | collective-permute-start | bytes 1572872 | tf_op jit(solution)/shard_map/ppermute | solution.py:143
  38.0 3.0 %collective-permute-start.5 = (bf16[1024,256]{1,0:T(8,128)(2,1)S(1)}, bf16[1024,256]{1,0:T(8,128)(2,1)S(1)}, u32[]{:S(2)}, u32[]{:S(2)}) collective-permute-start(bf16[1024,256]{1,0:T(8,128)(2,1)S(1)} %bitcast.48), channel_id=1, source_target_pairs={{0,386},{2,0},{384,2},{386,384},{1,387},{3,1},{385,3},{387,385},{4... | collective-permute-start | bytes 1572872 | tf_op jit(solution)/shard_map/ppermute | solution.py:82
  41.1 2.3 %collective-permute-start = (bf16[1024,256]{1,0:T(8,128)(2,1)S(1)}, bf16[1024,256]{1,0:T(8,128)(2,1)S(1)}, u32[]{:S(2)}, u32[]{:S(2)}) collective-permute-start(bf16[1024,256]{1,0:T(8,128)(2,1)S(1)} %bitcast.49), channel_id=1, source_target_pairs={{0,2},{2,384},{384,386},{386,0},{1,3},{3,385},{385,387},{387,1},{4... | collective-permute-start | bytes 1572872 | tf_op jit(solution)/shard_map/ppermute | solution.py:82
  43.4 3.8 %collective-permute-done.2.rest_2_ = bf16[1024,256]{1,0:T(8,128)(2,1)S(1)} collective-permute-done((bf16[1024,256]{1,0:T(8,128)(2,1)S(1)}, bf16[1024,256]{1,0:T(8,128)(2,1)S(1)}, u32[]{:S(2)}, u32[]{:S(2)}) %collective-permute-start.2) | collective-permute-done | bytes 524320 | tf_op jit(solution)/shard_map/ppermute | solution.py:135
  47.2 4.0 %collective-permute-start.3 = (bf16[1024,256]{1,0:T(8,128)(2,1)S(1)}, bf16[1024,256]{1,0:T(8,128)(2,1)S(1)}, u32[]{:S(2)}, u32[]{:S(2)}) collective-permute-start(bf16[1024,256]{1,0:T(8,128)(2,1)S(1)} %collective-permute-done.2.rest_2_), channel_id=1, source_target_pairs={{0,386},{2,0},{384,2},{386,384},{1,387},{3,1},{385,3},{387,385},{4... | collective-permute-start | bytes 1572872 | tf_op jit(solution)/shard_map/ppermute | solution.py:82
  51.2 0.2 convert_reduce_fusion.1
  51.6 3.2 %collective-permute-start.9 = (bf16[1024,256]{1,0:T(8,128)(2,1)S(1)}, bf16[1024,256]{1,0:T(8,128)(2,1)}, u32[]{:S(2)}, u32[]{:S(2)}) collective-permute-start(bf16[1024,256]{1,0:T(8,128)(2,1)S(1)} %collective-permute-done.2.rest_2_), channel_id=1, source_target_pairs={{0,1},{1,0},{2,3},{3,2},{4,5},{5,4},{6,7},{7,6},{8,9},{9,8},{10,11... | collective-permute-start | bytes 1572872 | tf_op jit(solution)/shard_map/ppermute | solution.py:143
  54.8 2.3 %collective-permute-start.6 = (bf16[1024,256]{1,0:T(8,128)(2,1)S(1)}, bf16[1024,256]{1,0:T(8,128)(2,1)}, u32[]{:S(2)}, u32[]{:S(2)}) collective-permute-start(bf16[1024,256]{1,0:T(8,128)(2,1)S(1)} %collective-permute-done.2.rest_2_), channel_id=1, source_target_pairs={{0,2},{2,384},{384,386},{386,0},{1,3},{3,385},{385,387},{387,1},{4... | collective-permute-start | bytes 1572872 | tf_op jit(solution)/shard_map/ppermute | solution.py:82
  57.2 2.2 %collective-permute-start.12 = (bf16[1024,256]{1,0:T(8,128)(2,1)S(1)}, bf16[1024,256]{1,0:T(8,128)(2,1)}, u32[]{:S(2)}, u32[]{:S(2)}) collective-permute-start(bf16[1024,256]{1,0:T(8,128)(2,1)S(1)} %collective-permute-done.5.rest_5_), channel_id=1, source_target_pairs={{0,1},{1,0},{2,3},{3,2},{4,5},{5,4},{6,7},{7,6},{8,9},{9,8},{10,11... | collective-permute-start | bytes 1572872 | tf_op jit(solution)/shard_map/ppermute | solution.py:143
  59.4 1.9 %collective-permute-start.1 = (bf16[1024,256]{1,0:T(8,128)(2,1)S(1)}, bf16[1024,256]{1,0:T(8,128)(2,1)}, u32[]{:S(2)}, u32[]{:S(2)}) collective-permute-start(bf16[1024,256]{1,0:T(8,128)(2,1)S(1)} %collective-permute-done.rest_4_), channel_id=1, source_target_pairs={{0,2},{2,384},{384,386},{386,0},{1,3},{3,385},{385,387},{387,1},{4... | collective-permute-start | bytes 1572872 | tf_op jit(solution)/shard_map/ppermute | solution.py:82
  61.4 3.4 %collective-permute-done.3.rest_7_ = bf16[1024,256]{1,0:T(8,128)(2,1)S(1)} collective-permute-done((bf16[1024,256]{1,0:T(8,128)(2,1)S(1)}, bf16[1024,256]{1,0:T(8,128)(2,1)S(1)}, u32[]{:S(2)}, u32[]{:S(2)}) %collective-permute-start.3) | collective-permute-done | bytes 524320 | tf_op jit(solution)/shard_map/ppermute | solution.py:82
  64.8 4.3 %collective-permute-start.4 = (bf16[1024,256]{1,0:T(8,128)(2,1)S(1)}, bf16[1024,256]{1,0:T(8,128)(2,1)}, u32[]{:S(2)}, u32[]{:S(2)}) collective-permute-start(bf16[1024,256]{1,0:T(8,128)(2,1)S(1)} %collective-permute-done.3.rest_7_), channel_id=1, source_target_pairs={{0,386},{2,0},{384,2},{386,384},{1,387},{3,1},{385,3},{387,385},{4... | collective-permute-start | bytes 1572872 | tf_op jit(solution)/shard_map/ppermute | solution.py:82
  69.3 0.1 ne.147
  69.7 2.9 %collective-permute-start.11 = (bf16[1024,256]{1,0:T(8,128)(2,1)S(1)}, bf16[1024,256]{1,0:T(8,128)(2,1)}, u32[]{:S(2)}, u32[]{:S(2)}) collective-permute-start(bf16[1024,256]{1,0:T(8,128)(2,1)S(1)} %collective-permute-done.rest_4_), channel_id=1, source_target_pairs={{0,1},{1,0},{2,3},{3,2},{4,5},{5,4},{6,7},{7,6},{8,9},{9,8},{10,11... | collective-permute-start | bytes 1572872 | tf_op jit(solution)/shard_map/ppermute | solution.py:143
  72.6 1.9 %collective-permute-start.14 = (bf16[1024,256]{1,0:T(8,128)(2,1)S(1)}, bf16[1024,256]{1,0:T(8,128)(2,1)}, u32[]{:S(2)}, u32[]{:S(2)}) collective-permute-start(bf16[1024,256]{1,0:T(8,128)(2,1)S(1)} %collective-permute-done.3.rest_7_), channel_id=1, source_target_pairs={{0,1},{1,0},{2,3},{3,2},{4,5},{5,4},{6,7},{7,6},{8,9},{9,8},{10,11... | collective-permute-start | bytes 1572872 | tf_op jit(solution)/shard_map/ppermute | solution.py:143
  74.6 2.4 %collective-permute-start.13 = (bf16[1024,256]{1,0:T(8,128)(2,1)}, bf16[1024,256]{1,0:T(8,128)(2,1)}, u32[]{:S(2)}, u32[]{:S(2)}) collective-permute-start(bf16[1024,256]{1,0:T(8,128)(2,1)} %collective-permute-done.6.rest_6_), channel_id=1, source_target_pairs={{0,1},{1,0},{2,3},{3,2},{4,5},{5,4},{6,7},{7,6},{8,9},{9,8},{10,11... | collective-permute-start | bytes 1572872 | tf_op jit(solution)/shard_map/ppermute | solution.py:143
  77.0 5.8 %collective-permute-done.1.rest_1_ = bf16[1024,256]{1,0:T(8,128)(2,1)} collective-permute-done((bf16[1024,256]{1,0:T(8,128)(2,1)S(1)}, bf16[1024,256]{1,0:T(8,128)(2,1)}, u32[]{:S(2)}, u32[]{:S(2)}) %collective-permute-start.1) | collective-permute-done | bytes 524320 | tf_op jit(solution)/shard_map/ppermute | solution.py:82
  82.8 2.7 %collective-permute-start.8 = (bf16[1024,256]{1,0:T(8,128)(2,1)}, bf16[1024,256]{1,0:T(8,128)(2,1)}, u32[]{:S(2)}, u32[]{:S(2)}) collective-permute-start(bf16[1024,256]{1,0:T(8,128)(2,1)} %collective-permute-done.1.rest_1_), channel_id=1, source_target_pairs={{0,1},{1,0},{2,3},{3,2},{4,5},{5,4},{6,7},{7,6},{8,9},{9,8},{10,11... | collective-permute-start | bytes 1572872 | tf_op jit(solution)/shard_map/ppermute | solution.py:143
  85.5 1.9 %collective-permute-start.10 = (bf16[1024,256]{1,0:T(8,128)(2,1)}, bf16[1024,256]{1,0:T(8,128)(2,1)}, u32[]{:S(2)}, u32[]{:S(2)}) collective-permute-start(bf16[1024,256]{1,0:T(8,128)(2,1)} %collective-permute-done.4.rest_3_), channel_id=1, source_target_pairs={{0,1},{1,0},{2,3},{3,2},{4,5},{5,4},{6,7},{7,6},{8,9},{9,8},{10,11... | collective-permute-start | bytes 1572872 | tf_op jit(solution)/shard_map/ppermute | solution.py:143
  87.9 1.8 %collective-permute-done.10.rest_11_ = bf16[1024,256]{1,0:T(8,128)(2,1)} collective-permute-done((bf16[1024,256]{1,0:T(8,128)(2,1)}, bf16[1024,256]{1,0:T(8,128)(2,1)}, u32[]{:S(2)}, u32[]{:S(2)}) %collective-permute-start.10) | collective-permute-done | bytes 524320 | tf_op jit(solution)/shard_map/ppermute | solution.py:143
  89.7 6.9 %all-gather.2.cloned.1.call-done.left_ref = bf16[288,8192]{1,0:T(8,128)(2,1)} async-done(((bf16[24,8192]{1,0:T(8,128)(2,1)}), bf16[288,8192]{1,0:T(8,128)(2,1)}) %all-gather.2.cloned.1.call-update) | async-done | bytes 4718608 | tf_op jit(solution)/shard_map/all_gather | solution.py:175
  96.7 6.9 %shard_map.57 = bf16[1536,128]{1,0:T(8,128)(2,1)S(1)} custom-call(s32[8,3]{1,0:T(8,128)S(1)} %stack.127.place_ref, s32[1,576]{1,0:T(1,128)S(1)} %broadcast_in_dim.6.source_ref, bf16[288,8192]{1,0:T(8,128)(2,1)} %all-gather.2.cloned.1.call-done.left_ref, bf16[1024,256]{1,0:T(8,128)(2,1)} %bitcast.50, bf16[1024,256]{1,0:T(8,128)(2,1)} %collective-permute-done.1.rest_1_, ...), custom_call_target="tpu_custom_call" | custom-call | flops 2415919104 | bytes 9437184 | tf_op jit(solution)/shard_map/pallas_call | solution.py:189
  103.5 27.5 %all_to_all.21 = bf16[64,24,128]{2,1,0:T(8,128)(2,1)S(1)} all-to-all(bf16[64,24,128]{2,1,0:T(8,128)(2,1)S(1)} %bitcast.43), channel_id=1, replica_groups=mesh['xh'=2,'z'=12,'yq'=4,'yb'=2,'xl'=2,'core'=2] {'xh','yq','yb','xl','..., dimensions={0} | all-to-all | bytes 786432 | tf_op jit(solution)/shard_map/all_to_all | solution.py:206
  131.1 0.2 convert_reduce_fusion
  131.4 0.8 reshape.44
  (47 shorter events, 1.4 us)
Async XLA Ops:
  6.5 44.7 %copy-start.6 = (s32[72]{0:T(128)S(1)}, s32[72]{0:T(128)}, u32[]{:S(2)}) copy-start(s32[72]{0:T(128)} %param.9) | copy-start | bytes 868
  6.5 90.1 %all-gather.2.cloned.1.call-start = ((), (), s32[]{:S(2)}) async-start(), calls=%async_computation.2 | async-start | bytes 5111808 | tf_op jit(solution)/shard_map/all_gather | solution.py:175
  33.0 63.6 %copy-start = (bf16[2,512,256]{2,1,0:T(8,128)(2,1)}, bf16[2,512,256]{2,1,0:T(8,128)(2,1)S(1)}, u32[]{:S(2)}) copy-start(bf16[2,512,256]{2,1,0:T(8,128)(2,1)S(1)} %copy.20) | copy-start | bytes 1572868
  33.0 14.1 %collective-permute-start.2 = (bf16[1024,256]{1,0:T(8,128)(2,1)S(1)}, bf16[1024,256]{1,0:T(8,128)(2,1)S(1)}, u32[]{:S(2)}, u32[]{:S(2)}) collective-permute-start(bf16[1024,256]{1,0:T(8,128)(2,1)S(1)} %bitcast.46), channel_id=1, source_target_pairs={{0,4},{4,0},{1,5},{5,1},{2,6},{6,2},{3,7},{7,3},{8,12},{12,8},{9,1... | collective-permute-start | bytes 1572872 | tf_op jit(solution)/shard_map/ppermute | solution.py:135
  35.7 19.1 %collective-permute-start.7 = (bf16[1024,256]{1,0:T(8,128)(2,1)S(1)}, bf16[1024,256]{1,0:T(8,128)(2,1)S(1)}, u32[]{:S(2)}, u32[]{:S(2)}) collective-permute-start(bf16[1024,256]{1,0:T(8,128)(2,1)S(1)} %bitcast.47), channel_id=1, source_target_pairs={{0,1},{1,0},{2,3},{3,2},{4,5},{5,4},{6,7},{7,6},{8,9},{9,8},{10,11... | collective-permute-start | bytes 1572872 | tf_op jit(solution)/shard_map/ppermute | solution.py:143
  38.0 19.1 %collective-permute-start.5 = (bf16[1024,256]{1,0:T(8,128)(2,1)S(1)}, bf16[1024,256]{1,0:T(8,128)(2,1)S(1)}, u32[]{:S(2)}, u32[]{:S(2)}) collective-permute-start(bf16[1024,256]{1,0:T(8,128)(2,1)S(1)} %bitcast.48), channel_id=1, source_target_pairs={{0,386},{2,0},{384,2},{386,384},{1,387},{3,1},{385,3},{387,385},{4... | collective-permute-start | bytes 1572872 | tf_op jit(solution)/shard_map/ppermute | solution.py:82
  41.1 18.3 %collective-permute-start = (bf16[1024,256]{1,0:T(8,128)(2,1)S(1)}, bf16[1024,256]{1,0:T(8,128)(2,1)S(1)}, u32[]{:S(2)}, u32[]{:S(2)}) collective-permute-start(bf16[1024,256]{1,0:T(8,128)(2,1)S(1)} %bitcast.49), channel_id=1, source_target_pairs={{0,2},{2,384},{384,386},{386,0},{1,3},{3,385},{385,387},{387,1},{4... | collective-permute-start | bytes 1572872 | tf_op jit(solution)/shard_map/ppermute | solution.py:82
  47.2 49.5 %copy-start.1 = (bf16[1024,256]{1,0:T(8,128)(2,1)}, bf16[1024,256]{1,0:T(8,128)(2,1)S(1)}, u32[]{:S(2)}) copy-start(bf16[1024,256]{1,0:T(8,128)(2,1)S(1)} %collective-permute-done.2.rest_2_) | copy-start | bytes 1572868
  47.2 17.6 %collective-permute-start.3 = (bf16[1024,256]{1,0:T(8,128)(2,1)S(1)}, bf16[1024,256]{1,0:T(8,128)(2,1)S(1)}, u32[]{:S(2)}, u32[]{:S(2)}) collective-permute-start(bf16[1024,256]{1,0:T(8,128)(2,1)S(1)} %collective-permute-done.2.rest_2_), channel_id=1, source_target_pairs={{0,386},{2,0},{384,2},{386,384},{1,387},{3,1},{385,3},{387,385},{4... | collective-permute-start | bytes 1572872 | tf_op jit(solution)/shard_map/ppermute | solution.py:82
  51.6 21.0 %collective-permute-start.9 = (bf16[1024,256]{1,0:T(8,128)(2,1)S(1)}, bf16[1024,256]{1,0:T(8,128)(2,1)}, u32[]{:S(2)}, u32[]{:S(2)}) collective-permute-start(bf16[1024,256]{1,0:T(8,128)(2,1)S(1)} %collective-permute-done.2.rest_2_), channel_id=1, source_target_pairs={{0,1},{1,0},{2,3},{3,2},{4,5},{5,4},{6,7},{7,6},{8,9},{9,8},{10,11... | collective-permute-start | bytes 1572872 | tf_op jit(solution)/shard_map/ppermute | solution.py:143
  54.8 41.8 %copy-start.2 = (bf16[1024,256]{1,0:T(8,128)(2,1)}, bf16[1024,256]{1,0:T(8,128)(2,1)S(1)}, u32[]{:S(2)}) copy-start(bf16[1024,256]{1,0:T(8,128)(2,1)S(1)} %collective-permute-done.7.rest_8_) | copy-start | bytes 1572868
  54.8 19.7 %collective-permute-start.6 = (bf16[1024,256]{1,0:T(8,128)(2,1)S(1)}, bf16[1024,256]{1,0:T(8,128)(2,1)}, u32[]{:S(2)}, u32[]{:S(2)}) collective-permute-start(bf16[1024,256]{1,0:T(8,128)(2,1)S(1)} %collective-permute-done.2.rest_2_), channel_id=1, source_target_pairs={{0,2},{2,384},{384,386},{386,0},{1,3},{3,385},{385,387},{387,1},{4... | collective-permute-start | bytes 1572872 | tf_op jit(solution)/shard_map/ppermute | solution.py:82
  57.2 39.4 %copy-start.3 = (bf16[1024,256]{1,0:T(8,128)(2,1)}, bf16[1024,256]{1,0:T(8,128)(2,1)S(1)}, u32[]{:S(2)}) copy-start(bf16[1024,256]{1,0:T(8,128)(2,1)S(1)} %collective-permute-done.5.rest_5_) | copy-start | bytes 1572868
  57.2 12.5 %collective-permute-start.12 = (bf16[1024,256]{1,0:T(8,128)(2,1)S(1)}, bf16[1024,256]{1,0:T(8,128)(2,1)}, u32[]{:S(2)}, u32[]{:S(2)}) collective-permute-start(bf16[1024,256]{1,0:T(8,128)(2,1)S(1)} %collective-permute-done.5.rest_5_), channel_id=1, source_target_pairs={{0,1},{1,0},{2,3},{3,2},{4,5},{5,4},{6,7},{7,6},{8,9},{9,8},{10,11... | collective-permute-start | bytes 1572872 | tf_op jit(solution)/shard_map/ppermute | solution.py:143
  59.4 37.2 %copy-start.4 = (bf16[1024,256]{1,0:T(8,128)(2,1)}, bf16[1024,256]{1,0:T(8,128)(2,1)S(1)}, u32[]{:S(2)}) copy-start(bf16[1024,256]{1,0:T(8,128)(2,1)S(1)} %collective-permute-done.rest_4_) | copy-start | bytes 1572868
  59.4 23.4 %collective-permute-start.1 = (bf16[1024,256]{1,0:T(8,128)(2,1)S(1)}, bf16[1024,256]{1,0:T(8,128)(2,1)}, u32[]{:S(2)}, u32[]{:S(2)}) collective-permute-start(bf16[1024,256]{1,0:T(8,128)(2,1)S(1)} %collective-permute-done.rest_4_), channel_id=1, source_target_pairs={{0,2},{2,384},{384,386},{386,0},{1,3},{3,385},{385,387},{387,1},{4... | collective-permute-start | bytes 1572872 | tf_op jit(solution)/shard_map/ppermute | solution.py:82
  64.8 31.9 %copy-start.5 = (bf16[1024,256]{1,0:T(8,128)(2,1)}, bf16[1024,256]{1,0:T(8,128)(2,1)S(1)}, u32[]{:S(2)}) copy-start(bf16[1024,256]{1,0:T(8,128)(2,1)S(1)} %collective-permute-done.3.rest_7_) | copy-start | bytes 1572868
  64.8 20.8 %collective-permute-start.4 = (bf16[1024,256]{1,0:T(8,128)(2,1)S(1)}, bf16[1024,256]{1,0:T(8,128)(2,1)}, u32[]{:S(2)}, u32[]{:S(2)}) collective-permute-start(bf16[1024,256]{1,0:T(8,128)(2,1)S(1)} %collective-permute-done.3.rest_7_), channel_id=1, source_target_pairs={{0,386},{2,0},{384,2},{386,384},{1,387},{3,1},{385,3},{387,385},{4... | collective-permute-start | bytes 1572872 | tf_op jit(solution)/shard_map/ppermute | solution.py:82
  69.7 18.2 %collective-permute-start.11 = (bf16[1024,256]{1,0:T(8,128)(2,1)S(1)}, bf16[1024,256]{1,0:T(8,128)(2,1)}, u32[]{:S(2)}, u32[]{:S(2)}) collective-permute-start(bf16[1024,256]{1,0:T(8,128)(2,1)S(1)} %collective-permute-done.rest_4_), channel_id=1, source_target_pairs={{0,1},{1,0},{2,3},{3,2},{4,5},{5,4},{6,7},{7,6},{8,9},{9,8},{10,11... | collective-permute-start | bytes 1572872 | tf_op jit(solution)/shard_map/ppermute | solution.py:143
  72.6 15.3 %collective-permute-start.14 = (bf16[1024,256]{1,0:T(8,128)(2,1)S(1)}, bf16[1024,256]{1,0:T(8,128)(2,1)}, u32[]{:S(2)}, u32[]{:S(2)}) collective-permute-start(bf16[1024,256]{1,0:T(8,128)(2,1)S(1)} %collective-permute-done.3.rest_7_), channel_id=1, source_target_pairs={{0,1},{1,0},{2,3},{3,2},{4,5},{5,4},{6,7},{7,6},{8,9},{9,8},{10,11... | collective-permute-start | bytes 1572872 | tf_op jit(solution)/shard_map/ppermute | solution.py:143
  74.6 13.3 %collective-permute-start.13 = (bf16[1024,256]{1,0:T(8,128)(2,1)}, bf16[1024,256]{1,0:T(8,128)(2,1)}, u32[]{:S(2)}, u32[]{:S(2)}) collective-permute-start(bf16[1024,256]{1,0:T(8,128)(2,1)} %collective-permute-done.6.rest_6_), channel_id=1, source_target_pairs={{0,1},{1,0},{2,3},{3,2},{4,5},{5,4},{6,7},{7,6},{8,9},{9,8},{10,11... | collective-permute-start | bytes 1572872 | tf_op jit(solution)/shard_map/ppermute | solution.py:143
  82.8 5.1 %collective-permute-start.8 = (bf16[1024,256]{1,0:T(8,128)(2,1)}, bf16[1024,256]{1,0:T(8,128)(2,1)}, u32[]{:S(2)}, u32[]{:S(2)}) collective-permute-start(bf16[1024,256]{1,0:T(8,128)(2,1)} %collective-permute-done.1.rest_1_), channel_id=1, source_target_pairs={{0,1},{1,0},{2,3},{3,2},{4,5},{5,4},{6,7},{7,6},{8,9},{9,8},{10,11... | collective-permute-start | bytes 1572872 | tf_op jit(solution)/shard_map/ppermute | solution.py:143
  85.5 4.1 %collective-permute-start.10 = (bf16[1024,256]{1,0:T(8,128)(2,1)}, bf16[1024,256]{1,0:T(8,128)(2,1)}, u32[]{:S(2)}, u32[]{:S(2)}) collective-permute-start(bf16[1024,256]{1,0:T(8,128)(2,1)} %collective-permute-done.4.rest_3_), channel_id=1, source_target_pairs={{0,1},{1,0},{2,3},{3,2},{4,5},{5,4},{6,7},{7,6},{8,9},{9,8},{10,11... | collective-permute-start | bytes 1572872 | tf_op jit(solution)/shard_map/ppermute | solution.py:143
Sparse Core Ops, SparseCore 0:
  30.8 65.8 all-gather.1

commit v5 on v4

--- a/solution.py
+++ b/solution.py
@@ -85,41 +85,57 @@
 def contract(place_ref, source_ref, left_ref, *rest):
     pieces, (out_ref, slab_ref, right_ref, total_ref, sems) = rest[:-5], rest[-5:]
     depth = pieces[0].shape[0]
-    copies = []
+    own = place_ref[0, 1]
+
+    def piece_copy(number, side, half):
+        return pltpu.make_async_copy(
+            pieces[2 * number + side], right_ref.at[half, number], sems.at[number, half]
+        )
+
+    def start_piece(number, half):
+        if number % 4 < 2:
+            piece_copy(number, half, half).start()
+        else:
+            first_is_own = place_ref[number, 1] == own
+
+            @pl.when(first_is_own)
+            def _():
+                piece_copy(number, half, half).start()
+
+            @pl.when(jnp.logical_not(first_is_own))
+            def _():
+                piece_copy(number, 1 - half, half).start()
+
+    slab_copies = []
     for number in range(SLICES):
         begin = pl.multiple_of(place_ref[number, 0] * depth, depth)
-        started = [
-            pltpu.make_async_copy(pieces[2 * number], right_ref.at[2 * number], sems.at[number, 0]),
-            pltpu.make_async_copy(
-                left_ref.at[:, pl.ds(begin, depth)], slab_ref.at[number], sems.at[number, 1]
-            ),
-            pltpu.make_async_copy(
-                pieces[2 * number + 1], right_ref.at[2 * number + 1], sems.at[number, 2]
-            ),
-        ]
-        for copy in started:
-            copy.start()
-        copies.append(started)
+        copy = pltpu.make_async_copy(
+            left_ref.at[:, pl.ds(begin, depth)], slab_ref.at[number], sems.at[number, 2]
+        )
+        copy.start()
+        slab_copies.append(copy)
+        start_piece(number, 0)
+    for number in range(SLICES):
+        start_piece(number, 1)
     rows = out_ref.shape[0] // 2
     slot_row = lax.broadcasted_iota(jnp.int32, (rows, source_ref.shape[1]), 0)
     select = (slot_row == source_ref[...]).astype(jnp.bfloat16)
-    for number in range(SLICES):
-        for copy in copies[number]:
-            copy.wait()
-        for side in range(2):
-            term = jnp.dot(
-                slab_ref[number], right_ref[2 * number + side], preferred_element_type=jnp.float32
-            )
-            half = place_ref[number, 1 + side]
+    for half in range(2):
+        for number in range(SLICES):
+            if half == 0:
+                slab_copies[number].wait()
+            piece_copy(number, 0, half).wait()
+            term = jnp.dot(slab_ref[number], right_ref[half, number], preferred_element_type=jnp.float32)
             if number == 0:
                 total_ref[half] = term
             else:
                 total_ref[half] += term
-    for half in range(2):
         rounded = total_ref[half].astype(jnp.bfloat16)
         stacked = jnp.concatenate([rounded[:, :LANES], rounded[:, LANES:]], axis=0)
         placed = jnp.dot(select, stacked, preferred_element_type=jnp.float32)
-        out_ref[half * rows:(half + 1) * rows, :] = placed.astype(jnp.bfloat16)
+        side = own if half == 0 else 1 - own
+        begin = pl.multiple_of(side * rows, rows)
+        out_ref[pl.ds(begin, rows), :] = placed.astype(jnp.bfloat16)
 
 
 def body(amplitudes, integrals, amp_mask, int_mask, owners):
@@ -193,7 +209,7 @@
         out_specs=vmem,
         scratch_shapes=[
             pltpu.VMEM((SLICES, left.shape[0], panels * depth), jnp.bfloat16),
-            pltpu.VMEM((2 * SLICES, panels * depth, width), jnp.bfloat16),
+            pltpu.VMEM((2, SLICES, panels * depth, width), jnp.bfloat16),
             pltpu.VMEM((2, left.shape[0], width), jnp.float32),
             pltpu.SemaphoreType.DMA((SLICES, 3)),
         ],

time: 140 us -> 142 us (1.014)
  Pallas kernels: 9.53 us -> 11.6 us
    pallas_call x1, Pallas kernels: 6.87 us -> 8.94 us  [body(): pl.pallas_call(contract, out_shape=jax.ShapeDtypeStruct((4 * slot_total *...]
where the time goes in v5:
time: 142 us; the launch traced here: 141 us
  blocking collectives  48.9 us (34%)
  starting transfers between devices  40.1 us (28%)
  waiting for transfers between devices  21.8 us (15%)
  between operations  13.9 us (10%)
  Pallas kernels  11.6 us (8%)
  local copies, waits for them, and re-layouts  3.14 us (2%)
  other arithmetic  1.66 us (1%)
    all_to_all x1, blocking collectives, body(): lax.all_to_all(slots, OWNERS, split_axis=0, concat_axis=0, tiled=True)  27.5 us
    all_to_all x1, blocking collectives, body(): lax.all_to_all(parts, GROUP, split_axis=0, concat_axis=0, tiled=True)  21.4 us
    ppermute x8, starting transfers between devices, body(): there = [lax.ppermute(value, 'core', SWAP) for value in here]  19.5 us
    ppermute x6, starting transfers between devices, turn(): return lax.ppermute(value, RING, [(i, (i + step) % 4) for i in range(4)])  17.9 us
    ppermute x6, waiting for transfers between devices, turn(): return lax.ppermute(value, RING, [(i, (i + step) % 4) for i in range(4)])  9.26 us
    pallas_call x1, Pallas kernels, body(): pl.pallas_call(contract, out_shape=jax.ShapeDtypeStruct((4 * slot_total *...  8.94 us
    all_gather x1, waiting for transfers between devices, body(): left = lax.all_gather(traded, 'z', axis=0, tiled=True)  6.94 us
    ppermute x1, waiting for transfers between devices, body(): across = lax.ppermute(own, 'yb', SWAP)  3.8 us
  transfers between devices with their start and end apart: 16, of which 5 were waited for; matrix products, arithmetic and copies ran while one was open for 3% of the time, Pallas kernels for 0%

profile of v5, /device:TPU:1, one launch (start us, length us, event | category | flops | bytes accessed | tf_op | source)
XLA Modules:
  0.0 141.1 jit_solution(214419954335752562)
XLA Ops:
  6.5 1.5 %shard_map.55 = bf16[384,512]{1,0:T(8,128)(2,1)S(1)} custom-call(s32[3,2,8]{2,1,0:T(2,128)} %bitcast.54, bf16[2,192,512]{2,1,0:T(8,128)(2,1)} %amp_hbm_ref.1), custom_call_target="tpu_custom_call" | custom-call | tf_op jit(solution)/shard_map/pallas_call | solution.py:171
  8.1 21.4 %all_to_all.20 = bf16[16,24,512]{2,1,0:T(8,128)(2,1)S(1)} all-to-all(bf16[16,24,512]{2,1,0:T(8,128)(2,1)S(1)} %bitcast.45), channel_id=1, replica_groups=mesh['xh'=2,'z'=12,'yq'=4,'yb'=2,'xl'=2,'core'=2] {'xh','yb','xl','core'}, dimensions={0} | all-to-all | bytes 786432 | tf_op jit(solution)/shard_map/all_to_all | solution.py:183
  29.5 1.1 shard_map.56
  30.6 0.7 convert_element_type.21
  31.5 1.3 copy.19
  32.8 0.2 copy.20
  33.0 2.7 %collective-permute-start.2 = (bf16[1024,256]{1,0:T(8,128)(2,1)S(1)}, bf16[1024,256]{1,0:T(8,128)(2,1)S(1)}, u32[]{:S(2)}, u32[]{:S(2)}) collective-permute-start(bf16[1024,256]{1,0:T(8,128)(2,1)S(1)} %bitcast.46), channel_id=1, source_target_pairs={{0,4},{4,0},{1,5},{5,1},{2,6},{6,2},{3,7},{7,3},{8,12},{12,8},{9,1... | collective-permute-start | bytes 1572872 | tf_op jit(solution)/shard_map/ppermute | solution.py:151
  35.7 2.3 %collective-permute-start.7 = (bf16[1024,256]{1,0:T(8,128)(2,1)S(1)}, bf16[1024,256]{1,0:T(8,128)(2,1)S(1)}, u32[]{:S(2)}, u32[]{:S(2)}) collective-permute-start(bf16[1024,256]{1,0:T(8,128)(2,1)S(1)} %bitcast.47), channel_id=1, source_target_pairs={{0,1},{1,0},{2,3},{3,2},{4,5},{5,4},{6,7},{7,6},{8,9},{9,8},{10,11... | collective-permute-start | bytes 1572872 | tf_op jit(solution)/shard_map/ppermute | solution.py:159
  38.0 3.0 %collective-permute-start.5 = (bf16[1024,256]{1,0:T(8,128)(2,1)S(1)}, bf16[1024,256]{1,0:T(8,128)(2,1)S(1)}, u32[]{:S(2)}, u32[]{:S(2)}) collective-permute-start(bf16[1024,256]{1,0:T(8,128)(2,1)S(1)} %bitcast.48), channel_id=1, source_target_pairs={{0,386},{2,0},{384,2},{386,384},{1,387},{3,1},{385,3},{387,385},{4... | collective-permute-start | bytes 1572872 | tf_op jit(solution)/shard_map/ppermute | solution.py:82
  41.1 2.3 %collective-permute-start = (bf16[1024,256]{1,0:T(8,128)(2,1)S(1)}, bf16[1024,256]{1,0:T(8,128)(2,1)S(1)}, u32[]{:S(2)}, u32[]{:S(2)}) collective-permute-start(bf16[1024,256]{1,0:T(8,128)(2,1)S(1)} %bitcast.49), channel_id=1, source_target_pairs={{0,2},{2,384},{384,386},{386,0},{1,3},{3,385},{385,387},{387,1},{4... | collective-permute-start | bytes 1572872 | tf_op jit(solution)/shard_map/ppermute | solution.py:82
  43.4 3.8 %collective-permute-done.2.rest_2_ = bf16[1024,256]{1,0:T(8,128)(2,1)S(1)} collective-permute-done((bf16[1024,256]{1,0:T(8,128)(2,1)S(1)}, bf16[1024,256]{1,0:T(8,128)(2,1)S(1)}, u32[]{:S(2)}, u32[]{:S(2)}) %collective-permute-start.2) | collective-permute-done | bytes 524320 | tf_op jit(solution)/shard_map/ppermute | solution.py:151
  47.2 4.0 %collective-permute-start.3 = (bf16[1024,256]{1,0:T(8,128)(2,1)S(1)}, bf16[1024,256]{1,0:T(8,128)(2,1)S(1)}, u32[]{:S(2)}, u32[]{:S(2)}) collective-permute-start(bf16[1024,256]{1,0:T(8,128)(2,1)S(1)} %collective-permute-done.2.rest_2_), channel_id=1, source_target_pairs={{0,386},{2,0},{384,2},{386,384},{1,387},{3,1},{385,3},{387,385},{4... | collective-permute-start | bytes 1572872 | tf_op jit(solution)/shard_map/ppermute | solution.py:82
  51.2 0.2 convert_reduce_fusion.1
  51.6 3.2 %collective-permute-start.9 = (bf16[1024,256]{1,0:T(8,128)(2,1)S(1)}, bf16[1024,256]{1,0:T(8,128)(2,1)}, u32[]{:S(2)}, u32[]{:S(2)}) collective-permute-start(bf16[1024,256]{1,0:T(8,128)(2,1)S(1)} %collective-permute-done.2.rest_2_), channel_id=1, source_target_pairs={{0,1},{1,0},{2,3},{3,2},{4,5},{5,4},{6,7},{7,6},{8,9},{9,8},{10,11... | collective-permute-start | bytes 1572872 | tf_op jit(solution)/shard_map/ppermute | solution.py:159
  54.8 2.3 %collective-permute-start.6 = (bf16[1024,256]{1,0:T(8,128)(2,1)S(1)}, bf16[1024,256]{1,0:T(8,128)(2,1)}, u32[]{:S(2)}, u32[]{:S(2)}) collective-permute-start(bf16[1024,256]{1,0:T(8,128)(2,1)S(1)} %collective-permute-done.2.rest_2_), channel_id=1, source_target_pairs={{0,2},{2,384},{384,386},{386,0},{1,3},{3,385},{385,387},{387,1},{4... | collective-permute-start | bytes 1572872 | tf_op jit(solution)/shard_map/ppermute | solution.py:82
  57.2 2.2 %collective-permute-start.12 = (bf16[1024,256]{1,0:T(8,128)(2,1)S(1)}, bf16[1024,256]{1,0:T(8,128)(2,1)}, u32[]{:S(2)}, u32[]{:S(2)}) collective-permute-start(bf16[1024,256]{1,0:T(8,128)(2,1)S(1)} %collective-permute-done.5.rest_5_), channel_id=1, source_target_pairs={{0,1},{1,0},{2,3},{3,2},{4,5},{5,4},{6,7},{7,6},{8,9},{9,8},{10,11... | collective-permute-start | bytes 1572872 | tf_op jit(solution)/shard_map/ppermute | solution.py:159
  59.4 1.9 %collective-permute-start.1 = (bf16[1024,256]{1,0:T(8,128)(2,1)S(1)}, bf16[1024,256]{1,0:T(8,128)(2,1)}, u32[]{:S(2)}, u32[]{:S(2)}) collective-permute-start(bf16[1024,256]{1,0:T(8,128)(2,1)S(1)} %collective-permute-done.rest_4_), channel_id=1, source_target_pairs={{0,2},{2,384},{384,386},{386,0},{1,3},{3,385},{385,387},{387,1},{4... | collective-permute-start | bytes 1572872 | tf_op jit(solution)/shard_map/ppermute | solution.py:82
  61.4 3.4 %collective-permute-done.3.rest_7_ = bf16[1024,256]{1,0:T(8,128)(2,1)S(1)} collective-permute-done((bf16[1024,256]{1,0:T(8,128)(2,1)S(1)}, bf16[1024,256]{1,0:T(8,128)(2,1)S(1)}, u32[]{:S(2)}, u32[]{:S(2)}) %collective-permute-start.3) | collective-permute-done | bytes 524320 | tf_op jit(solution)/shard_map/ppermute | solution.py:82
  64.8 4.3 %collective-permute-start.4 = (bf16[1024,256]{1,0:T(8,128)(2,1)S(1)}, bf16[1024,256]{1,0:T(8,128)(2,1)}, u32[]{:S(2)}, u32[]{:S(2)}) collective-permute-start(bf16[1024,256]{1,0:T(8,128)(2,1)S(1)} %collective-permute-done.3.rest_7_), channel_id=1, source_target_pairs={{0,386},{2,0},{384,2},{386,384},{1,387},{3,1},{385,3},{387,385},{4... | collective-permute-start | bytes 1572872 | tf_op jit(solution)/shard_map/ppermute | solution.py:82
  69.3 0.1 ne.147
  69.7 2.9 %collective-permute-start.11 = (bf16[1024,256]{1,0:T(8,128)(2,1)S(1)}, bf16[1024,256]{1,0:T(8,128)(2,1)}, u32[]{:S(2)}, u32[]{:S(2)}) collective-permute-start(bf16[1024,256]{1,0:T(8,128)(2,1)S(1)} %collective-permute-done.rest_4_), channel_id=1, source_target_pairs={{0,1},{1,0},{2,3},{3,2},{4,5},{5,4},{6,7},{7,6},{8,9},{9,8},{10,11... | collective-permute-start | bytes 1572872 | tf_op jit(solution)/shard_map/ppermute | solution.py:159
  72.6 1.9 %collective-permute-start.14 = (bf16[1024,256]{1,0:T(8,128)(2,1)S(1)}, bf16[1024,256]{1,0:T(8,128)(2,1)}, u32[]{:S(2)}, u32[]{:S(2)}) collective-permute-start(bf16[1024,256]{1,0:T(8,128)(2,1)S(1)} %collective-permute-done.3.rest_7_), channel_id=1, source_target_pairs={{0,1},{1,0},{2,3},{3,2},{4,5},{5,4},{6,7},{7,6},{8,9},{9,8},{10,11... | collective-permute-start | bytes 1572872 | tf_op jit(solution)/shard_map/ppermute | solution.py:159
  74.6 2.4 %collective-permute-start.13 = (bf16[1024,256]{1,0:T(8,128)(2,1)}, bf16[1024,256]{1,0:T(8,128)(2,1)}, u32[]{:S(2)}, u32[]{:S(2)}) collective-permute-start(bf16[1024,256]{1,0:T(8,128)(2,1)} %collective-permute-done.6.rest_6_), channel_id=1, source_target_pairs={{0,1},{1,0},{2,3},{3,2},{4,5},{5,4},{6,7},{7,6},{8,9},{9,8},{10,11... | collective-permute-start | bytes 1572872 | tf_op jit(solution)/shard_map/ppermute | solution.py:159
  77.0 5.8 %collective-permute-done.1.rest_1_ = bf16[1024,256]{1,0:T(8,128)(2,1)} collective-permute-done((bf16[1024,256]{1,0:T(8,128)(2,1)S(1)}, bf16[1024,256]{1,0:T(8,128)(2,1)}, u32[]{:S(2)}, u32[]{:S(2)}) %collective-permute-start.1) | collective-permute-done | bytes 524320 | tf_op jit(solution)/shard_map/ppermute | solution.py:82
  82.8 2.7 %collective-permute-start.8 = (bf16[1024,256]{1,0:T(8,128)(2,1)}, bf16[1024,256]{1,0:T(8,128)(2,1)}, u32[]{:S(2)}, u32[]{:S(2)}) collective-permute-start(bf16[1024,256]{1,0:T(8,128)(2,1)} %collective-permute-done.1.rest_1_), channel_id=1, source_target_pairs={{0,1},{1,0},{2,3},{3,2},{4,5},{5,4},{6,7},{7,6},{8,9},{9,8},{10,11... | collective-permute-start | bytes 1572872 | tf_op jit(solution)/shard_map/ppermute | solution.py:159
  85.5 1.9 %collective-permute-start.10 = (bf16[1024,256]{1,0:T(8,128)(2,1)}, bf16[1024,256]{1,0:T(8,128)(2,1)}, u32[]{:S(2)}, u32[]{:S(2)}) collective-permute-start(bf16[1024,256]{1,0:T(8,128)(2,1)} %collective-permute-done.4.rest_3_), channel_id=1, source_target_pairs={{0,1},{1,0},{2,3},{3,2},{4,5},{5,4},{6,7},{7,6},{8,9},{9,8},{10,11... | collective-permute-start | bytes 1572872 | tf_op jit(solution)/shard_map/ppermute | solution.py:159
  87.9 1.8 %collective-permute-done.10.rest_11_ = bf16[1024,256]{1,0:T(8,128)(2,1)} collective-permute-done((bf16[1024,256]{1,0:T(8,128)(2,1)}, bf16[1024,256]{1,0:T(8,128)(2,1)}, u32[]{:S(2)}, u32[]{:S(2)}) %collective-permute-start.10) | collective-permute-done | bytes 524320 | tf_op jit(solution)/shard_map/ppermute | solution.py:159
  89.7 6.9 %all-gather.2.cloned.1.call-done.left_ref = bf16[288,8192]{1,0:T(8,128)(2,1)} async-done(((bf16[24,8192]{1,0:T(8,128)(2,1)}), bf16[288,8192]{1,0:T(8,128)(2,1)}) %all-gather.2.cloned.1.call-update) | async-done | bytes 4718608 | tf_op jit(solution)/shard_map/all_gather | solution.py:191
  96.7 8.9 %shard_map.57 = bf16[1536,128]{1,0:T(8,128)(2,1)S(1)} custom-call(s32[8,3]{1,0:T(8,128)S(1)} %stack.127.place_ref, s32[1,576]{1,0:T(1,128)S(1)} %broadcast_in_dim.6.source_ref, bf16[288,8192]{1,0:T(8,128)(2,1)} %all-gather.2.cloned.1.call-done.left_ref, bf16[1024,256]{1,0:T(8,128)(2,1)} %bitcast.50, bf16[1024,256]{1,0:T(8,128)(2,1)} %collective-permute-done.1.rest_1_, ...), custom_call_target="tpu_custom_call" | custom-call | flops 2415919104 | bytes 9437184 | tf_op jit(solution)/shard_map/pallas_call | solution.py:205
  105.6 27.5 %all_to_all.21 = bf16[64,24,128]{2,1,0:T(8,128)(2,1)S(1)} all-to-all(bf16[64,24,128]{2,1,0:T(8,128)(2,1)S(1)} %bitcast.43), channel_id=1, replica_groups=mesh['xh'=2,'z'=12,'yq'=4,'yb'=2,'xl'=2,'core'=2] {'xh','yq','yb','xl','..., dimensions={0} | all-to-all | bytes 786432 | tf_op jit(solution)/shard_map/all_to_all | solution.py:222
  133.1 0.2 convert_reduce_fusion
  133.4 0.8 reshape.44
  (47 shorter events, 1.4 us)
Async XLA Ops:
  6.5 44.7 %copy-start.6 = (s32[72]{0:T(128)S(1)}, s32[72]{0:T(128)}, u32[]{:S(2)}) copy-start(s32[72]{0:T(128)} %param.9) | copy-start | bytes 868
  6.5 90.1 %all-gather.2.cloned.1.call-start = ((), (), s32[]{:S(2)}) async-start(), calls=%async_computation.2 | async-start | bytes 5111808 | tf_op jit(solution)/shard_map/all_gather | solution.py:191
  33.0 63.6 %copy-start = (bf16[2,512,256]{2,1,0:T(8,128)(2,1)}, bf16[2,512,256]{2,1,0:T(8,128)(2,1)S(1)}, u32[]{:S(2)}) copy-start(bf16[2,512,256]{2,1,0:T(8,128)(2,1)S(1)} %copy.20) | copy-start | bytes 1572868
  33.0 14.1 %collective-permute-start.2 = (bf16[1024,256]{1,0:T(8,128)(2,1)S(1)}, bf16[1024,256]{1,0:T(8,128)(2,1)S(1)}, u32[]{:S(2)}, u32[]{:S(2)}) collective-permute-start(bf16[1024,256]{1,0:T(8,128)(2,1)S(1)} %bitcast.46), channel_id=1, source_target_pairs={{0,4},{4,0},{1,5},{5,1},{2,6},{6,2},{3,7},{7,3},{8,12},{12,8},{9,1... | collective-permute-start | bytes 1572872 | tf_op jit(solution)/shard_map/ppermute | solution.py:151
  35.7 19.1 %collective-permute-start.7 = (bf16[1024,256]{1,0:T(8,128)(2,1)S(1)}, bf16[1024,256]{1,0:T(8,128)(2,1)S(1)}, u32[]{:S(2)}, u32[]{:S(2)}) collective-permute-start(bf16[1024,256]{1,0:T(8,128)(2,1)S(1)} %bitcast.47), channel_id=1, source_target_pairs={{0,1},{1,0},{2,3},{3,2},{4,5},{5,4},{6,7},{7,6},{8,9},{9,8},{10,11... | collective-permute-start | bytes 1572872 | tf_op jit(solution)/shard_map/ppermute | solution.py:159
  38.0 19.1 %collective-permute-start.5 = (bf16[1024,256]{1,0:T(8,128)(2,1)S(1)}, bf16[1024,256]{1,0:T(8,128)(2,1)S(1)}, u32[]{:S(2)}, u32[]{:S(2)}) collective-permute-start(bf16[1024,256]{1,0:T(8,128)(2,1)S(1)} %bitcast.48), channel_id=1, source_target_pairs={{0,386},{2,0},{384,2},{386,384},{1,387},{3,1},{385,3},{387,385},{4... | collective-permute-start | bytes 1572872 | tf_op jit(solution)/shard_map/ppermute | solution.py:82
  41.1 18.3 %collective-permute-start = (bf16[1024,256]{1,0:T(8,128)(2,1)S(1)}, bf16[1024,256]{1,0:T(8,128)(2,1)S(1)}, u32[]{:S(2)}, u32[]{:S(2)}) collective-permute-start(bf16[1024,256]{1,0:T(8,128)(2,1)S(1)} %bitcast.49), channel_id=1, source_target_pairs={{0,2},{2,384},{384,386},{386,0},{1,3},{3,385},{385,387},{387,1},{4... | collective-permute-start | bytes 1572872 | tf_op jit(solution)/shard_map/ppermute | solution.py:82
  47.2 49.5 %copy-start.1 = (bf16[1024,256]{1,0:T(8,128)(2,1)}, bf16[1024,256]{1,0:T(8,128)(2,1)S(1)}, u32[]{:S(2)}) copy-start(bf16[1024,256]{1,0:T(8,128)(2,1)S(1)} %collective-permute-done.2.rest_2_) | copy-start | bytes 1572868
  47.2 17.6 %collective-permute-start.3 = (bf16[1024,256]{1,0:T(8,128)(2,1)S(1)}, bf16[1024,256]{1,0:T(8,128)(2,1)S(1)}, u32[]{:S(2)}, u32[]{:S(2)}) collective-permute-start(bf16[1024,256]{1,0:T(8,128)(2,1)S(1)} %collective-permute-done.2.rest_2_), channel_id=1, source_target_pairs={{0,386},{2,0},{384,2},{386,384},{1,387},{3,1},{385,3},{387,385},{4... | collective-permute-start | bytes 1572872 | tf_op jit(solution)/shard_map/ppermute | solution.py:82
  51.6 21.0 %collective-permute-start.9 = (bf16[1024,256]{1,0:T(8,128)(2,1)S(1)}, bf16[1024,256]{1,0:T(8,128)(2,1)}, u32[]{:S(2)}, u32[]{:S(2)}) collective-permute-start(bf16[1024,256]{1,0:T(8,128)(2,1)S(1)} %collective-permute-done.2.rest_2_), channel_id=1, source_target_pairs={{0,1},{1,0},{2,3},{3,2},{4,5},{5,4},{6,7},{7,6},{8,9},{9,8},{10,11... | collective-permute-start | bytes 1572872 | tf_op jit(solution)/shard_map/ppermute | solution.py:159
  54.8 41.8 %copy-start.2 = (bf16[1024,256]{1,0:T(8,128)(2,1)}, bf16[1024,256]{1,0:T(8,128)(2,1)S(1)}, u32[]{:S(2)}) copy-start(bf16[1024,256]{1,0:T(8,128)(2,1)S(1)} %collective-permute-done.7.rest_8_) | copy-start | bytes 1572868
  54.8 19.7 %collective-permute-start.6 = (bf16[1024,256]{1,0:T(8,128)(2,1)S(1)}, bf16[1024,256]{1,0:T(8,128)(2,1)}, u32[]{:S(2)}, u32[]{:S(2)}) collective-permute-start(bf16[1024,256]{1,0:T(8,128)(2,1)S(1)} %collective-permute-done.2.rest_2_), channel_id=1, source_target_pairs={{0,2},{2,384},{384,386},{386,0},{1,3},{3,385},{385,387},{387,1},{4... | collective-permute-start | bytes 1572872 | tf_op jit(solution)/shard_map/ppermute | solution.py:82
  57.2 39.4 %copy-start.3 = (bf16[1024,256]{1,0:T(8,128)(2,1)}, bf16[1024,256]{1,0:T(8,128)(2,1)S(1)}, u32[]{:S(2)}) copy-start(bf16[1024,256]{1,0:T(8,128)(2,1)S(1)} %collective-permute-done.5.rest_5_) | copy-start | bytes 1572868
  57.2 12.5 %collective-permute-start.12 = (bf16[1024,256]{1,0:T(8,128)(2,1)S(1)}, bf16[1024,256]{1,0:T(8,128)(2,1)}, u32[]{:S(2)}, u32[]{:S(2)}) collective-permute-start(bf16[1024,256]{1,0:T(8,128)(2,1)S(1)} %collective-permute-done.5.rest_5_), channel_id=1, source_target_pairs={{0,1},{1,0},{2,3},{3,2},{4,5},{5,4},{6,7},{7,6},{8,9},{9,8},{10,11... | collective-permute-start | bytes 1572872 | tf_op jit(solution)/shard_map/ppermute | solution.py:159
  59.4 37.2 %copy-start.4 = (bf16[1024,256]{1,0:T(8,128)(2,1)}, bf16[1024,256]{1,0:T(8,128)(2,1)S(1)}, u32[]{:S(2)}) copy-start(bf16[1024,256]{1,0:T(8,128)(2,1)S(1)} %collective-permute-done.rest_4_) | copy-start | bytes 1572868
  59.4 23.4 %collective-permute-start.1 = (bf16[1024,256]{1,0:T(8,128)(2,1)S(1)}, bf16[1024,256]{1,0:T(8,128)(2,1)}, u32[]{:S(2)}, u32[]{:S(2)}) collective-permute-start(bf16[1024,256]{1,0:T(8,128)(2,1)S(1)} %collective-permute-done.rest_4_), channel_id=1, source_target_pairs={{0,2},{2,384},{384,386},{386,0},{1,3},{3,385},{385,387},{387,1},{4... | collective-permute-start | bytes 1572872 | tf_op jit(solution)/shard_map/ppermute | solution.py:82
  64.8 31.9 %copy-start.5 = (bf16[1024,256]{1,0:T(8,128)(2,1)}, bf16[1024,256]{1,0:T(8,128)(2,1)S(1)}, u32[]{:S(2)}) copy-start(bf16[1024,256]{1,0:T(8,128)(2,1)S(1)} %collective-permute-done.3.rest_7_) | copy-start | bytes 1572868
  64.8 20.8 %collective-permute-start.4 = (bf16[1024,256]{1,0:T(8,128)(2,1)S(1)}, bf16[1024,256]{1,0:T(8,128)(2,1)}, u32[]{:S(2)}, u32[]{:S(2)}) collective-permute-start(bf16[1024,256]{1,0:T(8,128)(2,1)S(1)} %collective-permute-done.3.rest_7_), channel_id=1, source_target_pairs={{0,386},{2,0},{384,2},{386,384},{1,387},{3,1},{385,3},{387,385},{4... | collective-permute-start | bytes 1572872 | tf_op jit(solution)/shard_map/ppermute | solution.py:82
  69.7 18.2 %collective-permute-start.11 = (bf16[1024,256]{1,0:T(8,128)(2,1)S(1)}, bf16[1024,256]{1,0:T(8,128)(2,1)}, u32[]{:S(2)}, u32[]{:S(2)}) collective-permute-start(bf16[1024,256]{1,0:T(8,128)(2,1)S(1)} %collective-permute-done.rest_4_), channel_id=1, source_target_pairs={{0,1},{1,0},{2,3},{3,2},{4,5},{5,4},{6,7},{7,6},{8,9},{9,8},{10,11... | collective-permute-start | bytes 1572872 | tf_op jit(solution)/shard_map/ppermute | solution.py:159
  72.6 15.3 %collective-permute-start.14 = (bf16[1024,256]{1,0:T(8,128)(2,1)S(1)}, bf16[1024,256]{1,0:T(8,128)(2,1)}, u32[]{:S(2)}, u32[]{:S(2)}) collective-permute-start(bf16[1024,256]{1,0:T(8,128)(2,1)S(1)} %collective-permute-done.3.rest_7_), channel_id=1, source_target_pairs={{0,1},{1,0},{2,3},{3,2},{4,5},{5,4},{6,7},{7,6},{8,9},{9,8},{10,11... | collective-permute-start | bytes 1572872 | tf_op jit(solution)/shard_map/ppermute | solution.py:159
  74.6 13.3 %collective-permute-start.13 = (bf16[1024,256]{1,0:T(8,128)(2,1)}, bf16[1024,256]{1,0:T(8,128)(2,1)}, u32[]{:S(2)}, u32[]{:S(2)}) collective-permute-start(bf16[1024,256]{1,0:T(8,128)(2,1)} %collective-permute-done.6.rest_6_), channel_id=1, source_target_pairs={{0,1},{1,0},{2,3},{3,2},{4,5},{5,4},{6,7},{7,6},{8,9},{9,8},{10,11... | collective-permute-start | bytes 1572872 | tf_op jit(solution)/shard_map/ppermute | solution.py:159
  82.8 5.1 %collective-permute-start.8 = (bf16[1024,256]{1,0:T(8,128)(2,1)}, bf16[1024,256]{1,0:T(8,128)(2,1)}, u32[]{:S(2)}, u32[]{:S(2)}) collective-permute-start(bf16[1024,256]{1,0:T(8,128)(2,1)} %collective-permute-done.1.rest_1_), channel_id=1, source_target_pairs={{0,1},{1,0},{2,3},{3,2},{4,5},{5,4},{6,7},{7,6},{8,9},{9,8},{10,11... | collective-permute-start | bytes 1572872 | tf_op jit(solution)/shard_map/ppermute | solution.py:159
  85.5 4.1 %collective-permute-start.10 = (bf16[1024,256]{1,0:T(8,128)(2,1)}, bf16[1024,256]{1,0:T(8,128)(2,1)}, u32[]{:S(2)}, u32[]{:S(2)}) collective-permute-start(bf16[1024,256]{1,0:T(8,128)(2,1)} %collective-permute-done.4.rest_3_), channel_id=1, source_target_pairs={{0,1},{1,0},{2,3},{3,2},{4,5},{5,4},{6,7},{7,6},{8,9},{9,8},{10,11... | collective-permute-start | bytes 1572872 | tf_op jit(solution)/shard_map/ppermute | solution.py:159
Sparse Core Ops, SparseCore 0:
  30.8 65.8 all-gather.1

commit v6 on v4

--- a/solution.py
+++ b/solution.py
@@ -101,8 +101,17 @@
             copy.start()
         copies.append(started)
     rows = out_ref.shape[0] // 2
-    slot_row = lax.broadcasted_iota(jnp.int32, (rows, source_ref.shape[1]), 0)
-    select = (slot_row == source_ref[...]).astype(jnp.bfloat16)
+    tile_rows = source_ref.shape[1]
+    run = CAP * PART_ROWS
+    inverse = -(-(1 << 16) // (2 * run))
+
+    def second_block(lanes):
+        row = lax.broadcasted_iota(jnp.int32, (rows, lanes), 0)
+        return row, row - ((row * inverse) >> 16) * (2 * run) >= run
+
+    row, second = second_block(tile_rows)
+    select = (jnp.where(second, row - run, row) == source_ref[...]).astype(jnp.bfloat16)
+    _, second = second_block(LANES)
     for number in range(SLICES):
         for copy in copies[number]:
             copy.wait()
@@ -117,8 +126,8 @@
                 total_ref[half] += term
     for half in range(2):
         rounded = total_ref[half].astype(jnp.bfloat16)
-        stacked = jnp.concatenate([rounded[:, :LANES], rounded[:, LANES:]], axis=0)
-        placed = jnp.dot(select, stacked, preferred_element_type=jnp.float32)
+        placed = jnp.dot(select, rounded, preferred_element_type=jnp.float32)
+        placed = jnp.where(second, placed[:, LANES:], placed[:, :LANES])
         out_ref[half * rows:(half + 1) * rows, :] = placed.astype(jnp.bfloat16)
 
 
@@ -183,7 +192,6 @@
     source_row = (order[:, None] * PART_ROWS + jnp.arange(PART_ROWS, dtype=jnp.int32)).reshape(-1)
     owner_rows = CAP * PART_ROWS
     source_row = source_row // owner_rows * (2 * owner_rows) + source_row % owner_rows
-    source_row = jnp.concatenate([source_row, source_row + owner_rows])
 
     held = [pltpu.with_memory_space_constraint(value, pltpu.HBM) for value in [left] + here + there]
     slots = pl.pallas_call(

time: 140 us -> 140 us (level)
  no operation moved by 1% of the time
where the time goes in v6:
time: 140 us; the launch traced here: 139 us
  blocking collectives  48.8 us (35%)
  starting transfers between devices  40.1 us (29%)
  waiting for transfers between devices  21.9 us (16%)
  between operations  13.9 us (10%)
  Pallas kernels  9.41 us (7%)
  local copies, waits for them, and re-layouts  3.14 us (2%)
  other arithmetic  1.59 us (1%)
    all_to_all x1, blocking collectives, body(): lax.all_to_all(slots, OWNERS, split_axis=0, concat_axis=0, tiled=True)  27.4 us
    all_to_all x1, blocking collectives, body(): lax.all_to_all(parts, GROUP, split_axis=0, concat_axis=0, tiled=True)  21.4 us
    ppermute x8, starting transfers between devices, body(): there = [lax.ppermute(value, 'core', SWAP) for value in here]  19.5 us
    ppermute x6, starting transfers between devices, turn(): return lax.ppermute(value, RING, [(i, (i + step) % 4) for i in range(4)])  17.9 us
    ppermute x6, waiting for transfers between devices, turn(): return lax.ppermute(value, RING, [(i, (i + step) % 4) for i in range(4)])  9.31 us
    all_gather x1, waiting for transfers between devices, body(): left = lax.all_gather(traded, 'z', axis=0, tiled=True)  6.89 us
    pallas_call x1, Pallas kernels, body(): pl.pallas_call(contract, out_shape=jax.ShapeDtypeStruct((4 * slot_total *...  6.77 us
    ppermute x1, waiting for transfers between devices, body(): across = lax.ppermute(own, 'yb', SWAP)  3.8 us
  transfers between devices with their start and end apart: 16, of which 5 were waited for; matrix products, arithmetic and copies ran while one was open for 3% of the time, Pallas kernels for 0%

profile of v6, /device:TPU:1, one launch (start us, length us, event | category | flops | bytes accessed | tf_op | source)
XLA Modules:
  0.0 138.9 jit_solution(13344476411385479211)
XLA Ops:
  6.5 1.5 %shard_map.55 = bf16[384,512]{1,0:T(8,128)(2,1)S(1)} custom-call(s32[3,2,8]{2,1,0:T(2,128)} %bitcast.54, bf16[2,192,512]{2,1,0:T(8,128)(2,1)} %amp_hbm_ref.1), custom_call_target="tpu_custom_call" | custom-call | tf_op jit(solution)/shard_map/pallas_call | solution.py:164
  8.1 21.4 %all_to_all.20 = bf16[16,24,512]{2,1,0:T(8,128)(2,1)S(1)} all-to-all(bf16[16,24,512]{2,1,0:T(8,128)(2,1)S(1)} %bitcast.45), channel_id=1, replica_groups=mesh['xh'=2,'z'=12,'yq'=4,'yb'=2,'xl'=2,'core'=2] {'xh','yb','xl','core'}, dimensions={0} | all-to-all | bytes 786432 | tf_op jit(solution)/shard_map/all_to_all | solution.py:176
  29.5 1.1 shard_map.56
  30.6 0.7 convert_element_type.21
  31.5 1.3 copy.19
  32.8 0.2 copy.20
  33.0 2.7 %collective-permute-start.2 = (bf16[1024,256]{1,0:T(8,128)(2,1)S(1)}, bf16[1024,256]{1,0:T(8,128)(2,1)S(1)}, u32[]{:S(2)}, u32[]{:S(2)}) collective-permute-start(bf16[1024,256]{1,0:T(8,128)(2,1)S(1)} %bitcast.46), channel_id=1, source_target_pairs={{0,4},{4,0},{1,5},{5,1},{2,6},{6,2},{3,7},{7,3},{8,12},{12,8},{9,1... | collective-permute-start | bytes 1572872 | tf_op jit(solution)/shard_map/ppermute | solution.py:144
  35.7 2.3 %collective-permute-start.7 = (bf16[1024,256]{1,0:T(8,128)(2,1)S(1)}, bf16[1024,256]{1,0:T(8,128)(2,1)S(1)}, u32[]{:S(2)}, u32[]{:S(2)}) collective-permute-start(bf16[1024,256]{1,0:T(8,128)(2,1)S(1)} %bitcast.47), channel_id=1, source_target_pairs={{0,1},{1,0},{2,3},{3,2},{4,5},{5,4},{6,7},{7,6},{8,9},{9,8},{10,11... | collective-permute-start | bytes 1572872 | tf_op jit(solution)/shard_map/ppermute | solution.py:152
  38.0 3.0 %collective-permute-start.5 = (bf16[1024,256]{1,0:T(8,128)(2,1)S(1)}, bf16[1024,256]{1,0:T(8,128)(2,1)S(1)}, u32[]{:S(2)}, u32[]{:S(2)}) collective-permute-start(bf16[1024,256]{1,0:T(8,128)(2,1)S(1)} %bitcast.48), channel_id=1, source_target_pairs={{0,386},{2,0},{384,2},{386,384},{1,387},{3,1},{385,3},{387,385},{4... | collective-permute-start | bytes 1572872 | tf_op jit(solution)/shard_map/ppermute | solution.py:82
  41.1 2.3 %collective-permute-start = (bf16[1024,256]{1,0:T(8,128)(2,1)S(1)}, bf16[1024,256]{1,0:T(8,128)(2,1)S(1)}, u32[]{:S(2)}, u32[]{:S(2)}) collective-permute-start(bf16[1024,256]{1,0:T(8,128)(2,1)S(1)} %bitcast.49), channel_id=1, source_target_pairs={{0,2},{2,384},{384,386},{386,0},{1,3},{3,385},{385,387},{387,1},{4... | collective-permute-start | bytes 1572872 | tf_op jit(solution)/shard_map/ppermute | solution.py:82
  43.4 3.8 %collective-permute-done.2.rest_2_ = bf16[1024,256]{1,0:T(8,128)(2,1)S(1)} collective-permute-done((bf16[1024,256]{1,0:T(8,128)(2,1)S(1)}, bf16[1024,256]{1,0:T(8,128)(2,1)S(1)}, u32[]{:S(2)}, u32[]{:S(2)}) %collective-permute-start.2) | collective-permute-done | bytes 524320 | tf_op jit(solution)/shard_map/ppermute | solution.py:144
  47.2 4.0 %collective-permute-start.3 = (bf16[1024,256]{1,0:T(8,128)(2,1)S(1)}, bf16[1024,256]{1,0:T(8,128)(2,1)S(1)}, u32[]{:S(2)}, u32[]{:S(2)}) collective-permute-start(bf16[1024,256]{1,0:T(8,128)(2,1)S(1)} %collective-permute-done.2.rest_2_), channel_id=1, source_target_pairs={{0,386},{2,0},{384,2},{386,384},{1,387},{3,1},{385,3},{387,385},{4... | collective-permute-start | bytes 1572872 | tf_op jit(solution)/shard_map/ppermute | solution.py:82
  51.3 0.2 convert_reduce_fusion.1
  51.7 3.2 %collective-permute-start.9 = (bf16[1024,256]{1,0:T(8,128)(2,1)S(1)}, bf16[1024,256]{1,0:T(8,128)(2,1)}, u32[]{:S(2)}, u32[]{:S(2)}) collective-permute-start(bf16[1024,256]{1,0:T(8,128)(2,1)S(1)} %collective-permute-done.2.rest_2_), channel_id=1, source_target_pairs={{0,1},{1,0},{2,3},{3,2},{4,5},{5,4},{6,7},{7,6},{8,9},{9,8},{10,11... | collective-permute-start | bytes 1572872 | tf_op jit(solution)/shard_map/ppermute | solution.py:152
  55.0 2.3 %collective-permute-start.6 = (bf16[1024,256]{1,0:T(8,128)(2,1)S(1)}, bf16[1024,256]{1,0:T(8,128)(2,1)}, u32[]{:S(2)}, u32[]{:S(2)}) collective-permute-start(bf16[1024,256]{1,0:T(8,128)(2,1)S(1)} %collective-permute-done.2.rest_2_), channel_id=1, source_target_pairs={{0,2},{2,384},{384,386},{386,0},{1,3},{3,385},{385,387},{387,1},{4... | collective-permute-start | bytes 1572872 | tf_op jit(solution)/shard_map/ppermute | solution.py:82
  57.3 2.2 %collective-permute-start.12 = (bf16[1024,256]{1,0:T(8,128)(2,1)S(1)}, bf16[1024,256]{1,0:T(8,128)(2,1)}, u32[]{:S(2)}, u32[]{:S(2)}) collective-permute-start(bf16[1024,256]{1,0:T(8,128)(2,1)S(1)} %collective-permute-done.5.rest_5_), channel_id=1, source_target_pairs={{0,1},{1,0},{2,3},{3,2},{4,5},{5,4},{6,7},{7,6},{8,9},{9,8},{10,11... | collective-permute-start | bytes 1572872 | tf_op jit(solution)/shard_map/ppermute | solution.py:152
  59.6 1.9 %collective-permute-start.1 = (bf16[1024,256]{1,0:T(8,128)(2,1)S(1)}, bf16[1024,256]{1,0:T(8,128)(2,1)}, u32[]{:S(2)}, u32[]{:S(2)}) collective-permute-start(bf16[1024,256]{1,0:T(8,128)(2,1)S(1)} %collective-permute-done.rest_4_), channel_id=1, source_target_pairs={{0,2},{2,384},{384,386},{386,0},{1,3},{3,385},{385,387},{387,1},{4... | collective-permute-start | bytes 1572872 | tf_op jit(solution)/shard_map/ppermute | solution.py:82
  61.5 3.3 %collective-permute-done.3.rest_7_ = bf16[1024,256]{1,0:T(8,128)(2,1)S(1)} collective-permute-done((bf16[1024,256]{1,0:T(8,128)(2,1)S(1)}, bf16[1024,256]{1,0:T(8,128)(2,1)S(1)}, u32[]{:S(2)}, u32[]{:S(2)}) %collective-permute-start.3) | collective-permute-done | bytes 524320 | tf_op jit(solution)/shard_map/ppermute | solution.py:82
  64.8 4.3 %collective-permute-start.4 = (bf16[1024,256]{1,0:T(8,128)(2,1)S(1)}, bf16[1024,256]{1,0:T(8,128)(2,1)}, u32[]{:S(2)}, u32[]{:S(2)}) collective-permute-start(bf16[1024,256]{1,0:T(8,128)(2,1)S(1)} %collective-permute-done.3.rest_7_), channel_id=1, source_target_pairs={{0,386},{2,0},{384,2},{386,384},{1,387},{3,1},{385,3},{387,385},{4... | collective-permute-start | bytes 1572872 | tf_op jit(solution)/shard_map/ppermute | solution.py:82
  69.1 0.1 ne.169
  69.7 2.9 %collective-permute-start.11 = (bf16[1024,256]{1,0:T(8,128)(2,1)S(1)}, bf16[1024,256]{1,0:T(8,128)(2,1)}, u32[]{:S(2)}, u32[]{:S(2)}) collective-permute-start(bf16[1024,256]{1,0:T(8,128)(2,1)S(1)} %collective-permute-done.rest_4_), channel_id=1, source_target_pairs={{0,1},{1,0},{2,3},{3,2},{4,5},{5,4},{6,7},{7,6},{8,9},{9,8},{10,11... | collective-permute-start | bytes 1572872 | tf_op jit(solution)/shard_map/ppermute | solution.py:152
  72.6 1.9 %collective-permute-start.14 = (bf16[1024,256]{1,0:T(8,128)(2,1)S(1)}, bf16[1024,256]{1,0:T(8,128)(2,1)}, u32[]{:S(2)}, u32[]{:S(2)}) collective-permute-start(bf16[1024,256]{1,0:T(8,128)(2,1)S(1)} %collective-permute-done.3.rest_7_), channel_id=1, source_target_pairs={{0,1},{1,0},{2,3},{3,2},{4,5},{5,4},{6,7},{7,6},{8,9},{9,8},{10,11... | collective-permute-start | bytes 1572872 | tf_op jit(solution)/shard_map/ppermute | solution.py:152
  74.5 2.4 %collective-permute-start.13 = (bf16[1024,256]{1,0:T(8,128)(2,1)}, bf16[1024,256]{1,0:T(8,128)(2,1)}, u32[]{:S(2)}, u32[]{:S(2)}) collective-permute-start(bf16[1024,256]{1,0:T(8,128)(2,1)} %collective-permute-done.6.rest_6_), channel_id=1, source_target_pairs={{0,1},{1,0},{2,3},{3,2},{4,5},{5,4},{6,7},{7,6},{8,9},{9,8},{10,11... | collective-permute-start | bytes 1572872 | tf_op jit(solution)/shard_map/ppermute | solution.py:152
  76.9 6.0 %collective-permute-done.1.rest_1_ = bf16[1024,256]{1,0:T(8,128)(2,1)} collective-permute-done((bf16[1024,256]{1,0:T(8,128)(2,1)S(1)}, bf16[1024,256]{1,0:T(8,128)(2,1)}, u32[]{:S(2)}, u32[]{:S(2)}) %collective-permute-start.1) | collective-permute-done | bytes 524320 | tf_op jit(solution)/shard_map/ppermute | solution.py:82
  83.0 2.7 %collective-permute-start.8 = (bf16[1024,256]{1,0:T(8,128)(2,1)}, bf16[1024,256]{1,0:T(8,128)(2,1)}, u32[]{:S(2)}, u32[]{:S(2)}) collective-permute-start(bf16[1024,256]{1,0:T(8,128)(2,1)} %collective-permute-done.1.rest_1_), channel_id=1, source_target_pairs={{0,1},{1,0},{2,3},{3,2},{4,5},{5,4},{6,7},{7,6},{8,9},{9,8},{10,11... | collective-permute-start | bytes 1572872 | tf_op jit(solution)/shard_map/ppermute | solution.py:152
  85.7 1.9 %collective-permute-start.10 = (bf16[1024,256]{1,0:T(8,128)(2,1)}, bf16[1024,256]{1,0:T(8,128)(2,1)}, u32[]{:S(2)}, u32[]{:S(2)}) collective-permute-start(bf16[1024,256]{1,0:T(8,128)(2,1)} %collective-permute-done.4.rest_3_), channel_id=1, source_target_pairs={{0,1},{1,0},{2,3},{3,2},{4,5},{5,4},{6,7},{7,6},{8,9},{9,8},{10,11... | collective-permute-start | bytes 1572872 | tf_op jit(solution)/shard_map/ppermute | solution.py:152
  87.9 1.9 %collective-permute-done.10.rest_11_ = bf16[1024,256]{1,0:T(8,128)(2,1)} collective-permute-done((bf16[1024,256]{1,0:T(8,128)(2,1)}, bf16[1024,256]{1,0:T(8,128)(2,1)}, u32[]{:S(2)}, u32[]{:S(2)}) %collective-permute-start.10) | collective-permute-done | bytes 524320 | tf_op jit(solution)/shard_map/ppermute | solution.py:152
  89.8 6.9 %all-gather.2.cloned.1.call-done.left_ref = bf16[288,8192]{1,0:T(8,128)(2,1)} async-done(((bf16[24,8192]{1,0:T(8,128)(2,1)}), bf16[288,8192]{1,0:T(8,128)(2,1)}) %all-gather.2.cloned.1.call-update) | async-done | bytes 4718608 | tf_op jit(solution)/shard_map/all_gather | solution.py:184
  96.7 6.8 %shard_map.57 = bf16[1536,128]{1,0:T(8,128)(2,1)S(1)} custom-call(s32[8,3]{1,0:T(8,128)S(1)} %stack.127.place_ref, s32[1,288]{1,0:T(1,128)S(1)} %fusion.3.source_ref, bf16[288,8192]{1,0:T(8,128)(2,1)} %all-gather.2.cloned.1.call-done.left_ref, bf16[1024,256]{1,0:T(8,128)(2,1)} %bitcast.50, bf16[1024,256]{1,0:T(8,128)(2,1)} %collective-permute-done.1.rest_1_, ...), custom_call_target="tpu_custom_call" | custom-call | flops 2415919104 | bytes 9437184 | tf_op jit(solution)/shard_map/pallas_call | solution.py:197
  103.5 27.4 %all_to_all.21 = bf16[64,24,128]{2,1,0:T(8,128)(2,1)S(1)} all-to-all(bf16[64,24,128]{2,1,0:T(8,128)(2,1)S(1)} %bitcast.43), channel_id=1, replica_groups=mesh['xh'=2,'z'=12,'yq'=4,'yb'=2,'xl'=2,'core'=2] {'xh','yq','yb','xl','..., dimensions={0} | all-to-all | bytes 786432 | tf_op jit(solution)/shard_map/all_to_all | solution.py:214
  130.9 0.2 convert_reduce_fusion
  131.2 0.8 reshape.103
  (45 shorter events, 1.3 us)
Async XLA Ops:
  6.5 44.8 %copy-start.6 = (s32[72]{0:T(128)S(1)}, s32[72]{0:T(128)}, u32[]{:S(2)}) copy-start(s32[72]{0:T(128)} %param.9) | copy-start | bytes 868
  6.5 90.2 %all-gather.2.cloned.1.call-start = ((), (), s32[]{:S(2)}) async-start(), calls=%async_computation.2 | async-start | bytes 5111808 | tf_op jit(solution)/shard_map/all_gather | solution.py:184
  33.0 63.7 %copy-start = (bf16[2,512,256]{2,1,0:T(8,128)(2,1)}, bf16[2,512,256]{2,1,0:T(8,128)(2,1)S(1)}, u32[]{:S(2)}) copy-start(bf16[2,512,256]{2,1,0:T(8,128)(2,1)S(1)} %copy.20) | copy-start | bytes 1572868
  33.0 14.1 %collective-permute-start.2 = (bf16[1024,256]{1,0:T(8,128)(2,1)S(1)}, bf16[1024,256]{1,0:T(8,128)(2,1)S(1)}, u32[]{:S(2)}, u32[]{:S(2)}) collective-permute-start(bf16[1024,256]{1,0:T(8,128)(2,1)S(1)} %bitcast.46), channel_id=1, source_target_pairs={{0,4},{4,0},{1,5},{5,1},{2,6},{6,2},{3,7},{7,3},{8,12},{12,8},{9,1... | collective-permute-start | bytes 1572872 | tf_op jit(solution)/shard_map/ppermute | solution.py:144
  35.7 19.2 %collective-permute-start.7 = (bf16[1024,256]{1,0:T(8,128)(2,1)S(1)}, bf16[1024,256]{1,0:T(8,128)(2,1)S(1)}, u32[]{:S(2)}, u32[]{:S(2)}) collective-permute-start(bf16[1024,256]{1,0:T(8,128)(2,1)S(1)} %bitcast.47), channel_id=1, source_target_pairs={{0,1},{1,0},{2,3},{3,2},{4,5},{5,4},{6,7},{7,6},{8,9},{9,8},{10,11... | collective-permute-start | bytes 1572872 | tf_op jit(solution)/shard_map/ppermute | solution.py:152
  38.0 19.3 %collective-permute-start.5 = (bf16[1024,256]{1,0:T(8,128)(2,1)S(1)}, bf16[1024,256]{1,0:T(8,128)(2,1)S(1)}, u32[]{:S(2)}, u32[]{:S(2)}) collective-permute-start(bf16[1024,256]{1,0:T(8,128)(2,1)S(1)} %bitcast.48), channel_id=1, source_target_pairs={{0,386},{2,0},{384,2},{386,384},{1,387},{3,1},{385,3},{387,385},{4... | collective-permute-start | bytes 1572872 | tf_op jit(solution)/shard_map/ppermute | solution.py:82
  41.1 18.5 %collective-permute-start = (bf16[1024,256]{1,0:T(8,128)(2,1)S(1)}, bf16[1024,256]{1,0:T(8,128)(2,1)S(1)}, u32[]{:S(2)}, u32[]{:S(2)}) collective-permute-start(bf16[1024,256]{1,0:T(8,128)(2,1)S(1)} %bitcast.49), channel_id=1, source_target_pairs={{0,2},{2,384},{384,386},{386,0},{1,3},{3,385},{385,387},{387,1},{4... | collective-permute-start | bytes 1572872 | tf_op jit(solution)/shard_map/ppermute | solution.py:82
  47.2 49.6 %copy-start.1 = (bf16[1024,256]{1,0:T(8,128)(2,1)}, bf16[1024,256]{1,0:T(8,128)(2,1)S(1)}, u32[]{:S(2)}) copy-start(bf16[1024,256]{1,0:T(8,128)(2,1)S(1)} %collective-permute-done.2.rest_2_) | copy-start | bytes 1572868
  47.2 17.6 %collective-permute-start.3 = (bf16[1024,256]{1,0:T(8,128)(2,1)S(1)}, bf16[1024,256]{1,0:T(8,128)(2,1)S(1)}, u32[]{:S(2)}, u32[]{:S(2)}) collective-permute-start(bf16[1024,256]{1,0:T(8,128)(2,1)S(1)} %collective-permute-done.2.rest_2_), channel_id=1, source_target_pairs={{0,386},{2,0},{384,2},{386,384},{1,387},{3,1},{385,3},{387,385},{4... | collective-permute-start | bytes 1572872 | tf_op jit(solution)/shard_map/ppermute | solution.py:82
  51.7 20.8 %collective-permute-start.9 = (bf16[1024,256]{1,0:T(8,128)(2,1)S(1)}, bf16[1024,256]{1,0:T(8,128)(2,1)}, u32[]{:S(2)}, u32[]{:S(2)}) collective-permute-start(bf16[1024,256]{1,0:T(8,128)(2,1)S(1)} %collective-permute-done.2.rest_2_), channel_id=1, source_target_pairs={{0,1},{1,0},{2,3},{3,2},{4,5},{5,4},{6,7},{7,6},{8,9},{9,8},{10,11... | collective-permute-start | bytes 1572872 | tf_op jit(solution)/shard_map/ppermute | solution.py:152
  55.0 41.8 %copy-start.2 = (bf16[1024,256]{1,0:T(8,128)(2,1)}, bf16[1024,256]{1,0:T(8,128)(2,1)S(1)}, u32[]{:S(2)}) copy-start(bf16[1024,256]{1,0:T(8,128)(2,1)S(1)} %collective-permute-done.7.rest_8_) | copy-start | bytes 1572868
  55.0 19.5 %collective-permute-start.6 = (bf16[1024,256]{1,0:T(8,128)(2,1)S(1)}, bf16[1024,256]{1,0:T(8,128)(2,1)}, u32[]{:S(2)}, u32[]{:S(2)}) collective-permute-start(bf16[1024,256]{1,0:T(8,128)(2,1)S(1)} %collective-permute-done.2.rest_2_), channel_id=1, source_target_pairs={{0,2},{2,384},{384,386},{386,0},{1,3},{3,385},{385,387},{387,1},{4... | collective-permute-start | bytes 1572872 | tf_op jit(solution)/shard_map/ppermute | solution.py:82
  57.3 39.4 %copy-start.3 = (bf16[1024,256]{1,0:T(8,128)(2,1)}, bf16[1024,256]{1,0:T(8,128)(2,1)S(1)}, u32[]{:S(2)}) copy-start(bf16[1024,256]{1,0:T(8,128)(2,1)S(1)} %collective-permute-done.5.rest_5_) | copy-start | bytes 1572868
  57.3 12.3 %collective-permute-start.12 = (bf16[1024,256]{1,0:T(8,128)(2,1)S(1)}, bf16[1024,256]{1,0:T(8,128)(2,1)}, u32[]{:S(2)}, u32[]{:S(2)}) collective-permute-start(bf16[1024,256]{1,0:T(8,128)(2,1)S(1)} %collective-permute-done.5.rest_5_), channel_id=1, source_target_pairs={{0,1},{1,0},{2,3},{3,2},{4,5},{5,4},{6,7},{7,6},{8,9},{9,8},{10,11... | collective-permute-start | bytes 1572872 | tf_op jit(solution)/shard_map/ppermute | solution.py:152
  59.6 37.2 %copy-start.4 = (bf16[1024,256]{1,0:T(8,128)(2,1)}, bf16[1024,256]{1,0:T(8,128)(2,1)S(1)}, u32[]{:S(2)}) copy-start(bf16[1024,256]{1,0:T(8,128)(2,1)S(1)} %collective-permute-done.rest_4_) | copy-start | bytes 1572868
  59.6 23.4 %collective-permute-start.1 = (bf16[1024,256]{1,0:T(8,128)(2,1)S(1)}, bf16[1024,256]{1,0:T(8,128)(2,1)}, u32[]{:S(2)}, u32[]{:S(2)}) collective-permute-start(bf16[1024,256]{1,0:T(8,128)(2,1)S(1)} %collective-permute-done.rest_4_), channel_id=1, source_target_pairs={{0,2},{2,384},{384,386},{386,0},{1,3},{3,385},{385,387},{387,1},{4... | collective-permute-start | bytes 1572872 | tf_op jit(solution)/shard_map/ppermute | solution.py:82
  64.8 32.0 %copy-start.5 = (bf16[1024,256]{1,0:T(8,128)(2,1)}, bf16[1024,256]{1,0:T(8,128)(2,1)S(1)}, u32[]{:S(2)}) copy-start(bf16[1024,256]{1,0:T(8,128)(2,1)S(1)} %collective-permute-done.3.rest_7_) | copy-start | bytes 1572868
  64.8 20.9 %collective-permute-start.4 = (bf16[1024,256]{1,0:T(8,128)(2,1)S(1)}, bf16[1024,256]{1,0:T(8,128)(2,1)}, u32[]{:S(2)}, u32[]{:S(2)}) collective-permute-start(bf16[1024,256]{1,0:T(8,128)(2,1)S(1)} %collective-permute-done.3.rest_7_), channel_id=1, source_target_pairs={{0,386},{2,0},{384,2},{386,384},{1,387},{3,1},{385,3},{387,385},{4... | collective-permute-start | bytes 1572872 | tf_op jit(solution)/shard_map/ppermute | solution.py:82
  69.7 18.2 %collective-permute-start.11 = (bf16[1024,256]{1,0:T(8,128)(2,1)S(1)}, bf16[1024,256]{1,0:T(8,128)(2,1)}, u32[]{:S(2)}, u32[]{:S(2)}) collective-permute-start(bf16[1024,256]{1,0:T(8,128)(2,1)S(1)} %collective-permute-done.rest_4_), channel_id=1, source_target_pairs={{0,1},{1,0},{2,3},{3,2},{4,5},{5,4},{6,7},{7,6},{8,9},{9,8},{10,11... | collective-permute-start | bytes 1572872 | tf_op jit(solution)/shard_map/ppermute | solution.py:152
  72.6 15.3 %collective-permute-start.14 = (bf16[1024,256]{1,0:T(8,128)(2,1)S(1)}, bf16[1024,256]{1,0:T(8,128)(2,1)}, u32[]{:S(2)}, u32[]{:S(2)}) collective-permute-start(bf16[1024,256]{1,0:T(8,128)(2,1)S(1)} %collective-permute-done.3.rest_7_), channel_id=1, source_target_pairs={{0,1},{1,0},{2,3},{3,2},{4,5},{5,4},{6,7},{7,6},{8,9},{9,8},{10,11... | collective-permute-start | bytes 1572872 | tf_op jit(solution)/shard_map/ppermute | solution.py:152
  74.5 13.4 %collective-permute-start.13 = (bf16[1024,256]{1,0:T(8,128)(2,1)}, bf16[1024,256]{1,0:T(8,128)(2,1)}, u32[]{:S(2)}, u32[]{:S(2)}) collective-permute-start(bf16[1024,256]{1,0:T(8,128)(2,1)} %collective-permute-done.6.rest_6_), channel_id=1, source_target_pairs={{0,1},{1,0},{2,3},{3,2},{4,5},{5,4},{6,7},{7,6},{8,9},{9,8},{10,11... | collective-permute-start | bytes 1572872 | tf_op jit(solution)/shard_map/ppermute | solution.py:152
  83.0 5.0 %collective-permute-start.8 = (bf16[1024,256]{1,0:T(8,128)(2,1)}, bf16[1024,256]{1,0:T(8,128)(2,1)}, u32[]{:S(2)}, u32[]{:S(2)}) collective-permute-start(bf16[1024,256]{1,0:T(8,128)(2,1)} %collective-permute-done.1.rest_1_), channel_id=1, source_target_pairs={{0,1},{1,0},{2,3},{3,2},{4,5},{5,4},{6,7},{7,6},{8,9},{9,8},{10,11... | collective-permute-start | bytes 1572872 | tf_op jit(solution)/shard_map/ppermute | solution.py:152
  85.7 4.1 %collective-permute-start.10 = (bf16[1024,256]{1,0:T(8,128)(2,1)}, bf16[1024,256]{1,0:T(8,128)(2,1)}, u32[]{:S(2)}, u32[]{:S(2)}) collective-permute-start(bf16[1024,256]{1,0:T(8,128)(2,1)} %collective-permute-done.4.rest_3_), channel_id=1, source_target_pairs={{0,1},{1,0},{2,3},{3,2},{4,5},{5,4},{6,7},{7,6},{8,9},{9,8},{10,11... | collective-permute-start | bytes 1572872 | tf_op jit(solution)/shard_map/ppermute | solution.py:152
Sparse Core Ops, SparseCore 0:
  30.8 65.9 all-gather.1

commit v7 on v6

--- a/solution.py
+++ b/solution.py
@@ -84,19 +84,20 @@
 
 def contract(place_ref, source_ref, left_ref, *rest):
     pieces, (out_ref, slab_ref, right_ref, total_ref, sems) = rest[:-5], rest[-5:]
-    depth = pieces[0].shape[0]
+    depth, width = pieces[0].shape
     copies = []
     for number in range(SLICES):
         begin = pl.multiple_of(place_ref[number, 0] * depth, depth)
         started = [
-            pltpu.make_async_copy(pieces[2 * number], right_ref.at[2 * number], sems.at[number, 0]),
             pltpu.make_async_copy(
-                left_ref.at[:, pl.ds(begin, depth)], slab_ref.at[number], sems.at[number, 1]
-            ),
-            pltpu.make_async_copy(
-                pieces[2 * number + 1], right_ref.at[2 * number + 1], sems.at[number, 2]
-            ),
+                left_ref.at[:, pl.ds(begin, depth)], slab_ref.at[number], sems.at[number, 2]
+            )
         ]
+        for side in range(2):
+            lane = pl.multiple_of(place_ref[number, 1 + side] * width, width)
+            started.append(pltpu.make_async_copy(
+                pieces[2 * number + side], right_ref.at[number, :, pl.ds(lane, width)], sems.at[number, side]
+            ))
         for copy in started:
             copy.start()
         copies.append(started)
@@ -115,17 +116,13 @@
     for number in range(SLICES):
         for copy in copies[number]:
             copy.wait()
-        for side in range(2):
-            term = jnp.dot(
-                slab_ref[number], right_ref[2 * number + side], preferred_element_type=jnp.float32
-            )
-            half = place_ref[number, 1 + side]
-            if number == 0:
-                total_ref[half] = term
-            else:
-                total_ref[half] += term
+        term = jnp.dot(slab_ref[number], right_ref[number], preferred_element_type=jnp.float32)
+        if number == 0:
+            total_ref[...] = term
+        else:
+            total_ref[...] += term
     for half in range(2):
-        rounded = total_ref[half].astype(jnp.bfloat16)
+        rounded = total_ref[:, half * width:(half + 1) * width].astype(jnp.bfloat16)
         placed = jnp.dot(select, rounded, preferred_element_type=jnp.float32)
         placed = jnp.where(second, placed[:, LANES:], placed[:, :LANES])
         out_ref[half * rows:(half + 1) * rows, :] = placed.astype(jnp.bfloat16)
@@ -201,8 +198,8 @@
         out_specs=vmem,
         scratch_shapes=[
             pltpu.VMEM((SLICES, left.shape[0], panels * depth), jnp.bfloat16),
-            pltpu.VMEM((2 * SLICES, panels * depth, width), jnp.bfloat16),
-            pltpu.VMEM((2, left.shape[0], width), jnp.float32),
+            pltpu.VMEM((SLICES, panels * depth, 2 * width), jnp.bfloat16),
+            pltpu.VMEM((left.shape[0], 2 * width), jnp.float32),
             pltpu.SemaphoreType.DMA((SLICES, 3)),
         ],
         compiler_params=pltpu.CompilerParams(vmem_limit_bytes=GRANT),

time: 140 us -> 139 us (level)
  no operation moved by 1% of the time
where the time goes in v7:
time: 139 us
  blocking collectives  48.8 us (35%)
  starting transfers between devices  40.1 us (29%)
  waiting for transfers between devices  21.9 us (16%)
  between operations  13.9 us (10%)
  Pallas kernels  9.22 us (7%)
  local copies, waits for them, and re-layouts  3.14 us (2%)
  other arithmetic  1.59 us (1%)
    all_to_all x1, blocking collectives, body(): lax.all_to_all(slots, OWNERS, split_axis=0, concat_axis=0, tiled=True)  27.4 us
    all_to_all x1, blocking collectives, body(): lax.all_to_all(parts, GROUP, split_axis=0, concat_axis=0, tiled=True)  21.4 us
    ppermute x8, starting transfers between devices, body(): there = [lax.ppermute(value, 'core', SWAP) for value in here]  19.5 us
    ppermute x6, starting transfers between devices, turn(): return lax.ppermute(value, RING, [(i, (i + step) % 4) for i in range(4)])  17.9 us
    ppermute x6, waiting for transfers between devices, turn(): return lax.ppermute(value, RING, [(i, (i + step) % 4) for i in range(4)])  9.31 us
    all_gather x1, waiting for transfers between devices, body(): left = lax.all_gather(traded, 'z', axis=0, tiled=True)  6.89 us
    pallas_call x1, Pallas kernels, body(): pl.pallas_call(contract, out_shape=jax.ShapeDtypeStruct((4 * slot_total *...  6.57 us
    ppermute x1, waiting for transfers between devices, body(): across = lax.ppermute(own, 'yb', SWAP)  3.8 us
  transfers between devices with their start and end apart: 16, of which 5 were waited for; matrix products, arithmetic and copies ran while one was open for 3% of the time, Pallas kernels for 0%

profile of v7, /device:TPU:1, one launch (start us, length us, event | category | flops | bytes accessed | tf_op | source)
XLA Modules:
  0.0 138.7 jit_solution(3202257472437557847)
XLA Ops:
  6.5 1.5 %shard_map.55 = bf16[384,512]{1,0:T(8,128)(2,1)S(1)} custom-call(s32[3,2,8]{2,1,0:T(2,128)} %bitcast.54, bf16[2,192,512]{2,1,0:T(8,128)(2,1)} %amp_hbm_ref.1), custom_call_target="tpu_custom_call" | custom-call | tf_op jit(solution)/shard_map/pallas_call | solution.py:161
  8.1 21.4 %all_to_all.20 = bf16[16,24,512]{2,1,0:T(8,128)(2,1)S(1)} all-to-all(bf16[16,24,512]{2,1,0:T(8,128)(2,1)S(1)} %bitcast.45), channel_id=1, replica_groups=mesh['xh'=2,'z'=12,'yq'=4,'yb'=2,'xl'=2,'core'=2] {'xh','yb','xl','core'}, dimensions={0} | all-to-all | bytes 786432 | tf_op jit(solution)/shard_map/all_to_all | solution.py:173
  29.5 1.1 shard_map.56
  30.6 0.7 convert_element_type.21
  31.5 1.3 copy.19
  32.8 0.2 copy.20
  33.0 2.7 %collective-permute-start.2 = (bf16[1024,256]{1,0:T(8,128)(2,1)S(1)}, bf16[1024,256]{1,0:T(8,128)(2,1)S(1)}, u32[]{:S(2)}, u32[]{:S(2)}) collective-permute-start(bf16[1024,256]{1,0:T(8,128)(2,1)S(1)} %bitcast.46), channel_id=1, source_target_pairs={{0,4},{4,0},{1,5},{5,1},{2,6},{6,2},{3,7},{7,3},{8,12},{12,8},{9,1... | collective-permute-start | bytes 1572872 | tf_op jit(solution)/shard_map/ppermute | solution.py:141
  35.7 2.3 %collective-permute-start.7 = (bf16[1024,256]{1,0:T(8,128)(2,1)S(1)}, bf16[1024,256]{1,0:T(8,128)(2,1)S(1)}, u32[]{:S(2)}, u32[]{:S(2)}) collective-permute-start(bf16[1024,256]{1,0:T(8,128)(2,1)S(1)} %bitcast.47), channel_id=1, source_target_pairs={{0,1},{1,0},{2,3},{3,2},{4,5},{5,4},{6,7},{7,6},{8,9},{9,8},{10,11... | collective-permute-start | bytes 1572872 | tf_op jit(solution)/shard_map/ppermute | solution.py:149
  38.0 3.0 %collective-permute-start.5 = (bf16[1024,256]{1,0:T(8,128)(2,1)S(1)}, bf16[1024,256]{1,0:T(8,128)(2,1)S(1)}, u32[]{:S(2)}, u32[]{:S(2)}) collective-permute-start(bf16[1024,256]{1,0:T(8,128)(2,1)S(1)} %bitcast.48), channel_id=1, source_target_pairs={{0,386},{2,0},{384,2},{386,384},{1,387},{3,1},{385,3},{387,385},{4... | collective-permute-start | bytes 1572872 | tf_op jit(solution)/shard_map/ppermute | solution.py:82
  41.1 2.3 %collective-permute-start = (bf16[1024,256]{1,0:T(8,128)(2,1)S(1)}, bf16[1024,256]{1,0:T(8,128)(2,1)S(1)}, u32[]{:S(2)}, u32[]{:S(2)}) collective-permute-start(bf16[1024,256]{1,0:T(8,128)(2,1)S(1)} %bitcast.49), channel_id=1, source_target_pairs={{0,2},{2,384},{384,386},{386,0},{1,3},{3,385},{385,387},{387,1},{4... | collective-permute-start | bytes 1572872 | tf_op jit(solution)/shard_map/ppermute | solution.py:82
  43.4 3.8 %collective-permute-done.2.rest_2_ = bf16[1024,256]{1,0:T(8,128)(2,1)S(1)} collective-permute-done((bf16[1024,256]{1,0:T(8,128)(2,1)S(1)}, bf16[1024,256]{1,0:T(8,128)(2,1)S(1)}, u32[]{:S(2)}, u32[]{:S(2)}) %collective-permute-start.2) | collective-permute-done | bytes 524320 | tf_op jit(solution)/shard_map/ppermute | solution.py:141
  47.2 4.0 %collective-permute-start.3 = (bf16[1024,256]{1,0:T(8,128)(2,1)S(1)}, bf16[1024,256]{1,0:T(8,128)(2,1)S(1)}, u32[]{:S(2)}, u32[]{:S(2)}) collective-permute-start(bf16[1024,256]{1,0:T(8,128)(2,1)S(1)} %collective-permute-done.2.rest_2_), channel_id=1, source_target_pairs={{0,386},{2,0},{384,2},{386,384},{1,387},{3,1},{385,3},{387,385},{4... | collective-permute-start | bytes 1572872 | tf_op jit(solution)/shard_map/ppermute | solution.py:82
  51.3 0.2 convert_reduce_fusion.1
  51.7 3.2 %collective-permute-start.9 = (bf16[1024,256]{1,0:T(8,128)(2,1)S(1)}, bf16[1024,256]{1,0:T(8,128)(2,1)}, u32[]{:S(2)}, u32[]{:S(2)}) collective-permute-start(bf16[1024,256]{1,0:T(8,128)(2,1)S(1)} %collective-permute-done.2.rest_2_), channel_id=1, source_target_pairs={{0,1},{1,0},{2,3},{3,2},{4,5},{5,4},{6,7},{7,6},{8,9},{9,8},{10,11... | collective-permute-start | bytes 1572872 | tf_op jit(solution)/shard_map/ppermute | solution.py:149
  55.0 2.3 %collective-permute-start.6 = (bf16[1024,256]{1,0:T(8,128)(2,1)S(1)}, bf16[1024,256]{1,0:T(8,128)(2,1)}, u32[]{:S(2)}, u32[]{:S(2)}) collective-permute-start(bf16[1024,256]{1,0:T(8,128)(2,1)S(1)} %collective-permute-done.2.rest_2_), channel_id=1, source_target_pairs={{0,2},{2,384},{384,386},{386,0},{1,3},{3,385},{385,387},{387,1},{4... | collective-permute-start | bytes 1572872 | tf_op jit(solution)/shard_map/ppermute | solution.py:82
  57.3 2.2 %collective-permute-start.12 = (bf16[1024,256]{1,0:T(8,128)(2,1)S(1)}, bf16[1024,256]{1,0:T(8,128)(2,1)}, u32[]{:S(2)}, u32[]{:S(2)}) collective-permute-start(bf16[1024,256]{1,0:T(8,128)(2,1)S(1)} %collective-permute-done.5.rest_5_), channel_id=1, source_target_pairs={{0,1},{1,0},{2,3},{3,2},{4,5},{5,4},{6,7},{7,6},{8,9},{9,8},{10,11... | collective-permute-start | bytes 1572872 | tf_op jit(solution)/shard_map/ppermute | solution.py:149
  59.6 1.9 %collective-permute-start.1 = (bf16[1024,256]{1,0:T(8,128)(2,1)S(1)}, bf16[1024,256]{1,0:T(8,128)(2,1)}, u32[]{:S(2)}, u32[]{:S(2)}) collective-permute-start(bf16[1024,256]{1,0:T(8,128)(2,1)S(1)} %collective-permute-done.rest_4_), channel_id=1, source_target_pairs={{0,2},{2,384},{384,386},{386,0},{1,3},{3,385},{385,387},{387,1},{4... | collective-permute-start | bytes 1572872 | tf_op jit(solution)/shard_map/ppermute | solution.py:82
  61.5 3.3 %collective-permute-done.3.rest_7_ = bf16[1024,256]{1,0:T(8,128)(2,1)S(1)} collective-permute-done((bf16[1024,256]{1,0:T(8,128)(2,1)S(1)}, bf16[1024,256]{1,0:T(8,128)(2,1)S(1)}, u32[]{:S(2)}, u32[]{:S(2)}) %collective-permute-start.3) | collective-permute-done | bytes 524320 | tf_op jit(solution)/shard_map/ppermute | solution.py:82
  64.8 4.3 %collective-permute-start.4 = (bf16[1024,256]{1,0:T(8,128)(2,1)S(1)}, bf16[1024,256]{1,0:T(8,128)(2,1)}, u32[]{:S(2)}, u32[]{:S(2)}) collective-permute-start(bf16[1024,256]{1,0:T(8,128)(2,1)S(1)} %collective-permute-done.3.rest_7_), channel_id=1, source_target_pairs={{0,386},{2,0},{384,2},{386,384},{1,387},{3,1},{385,3},{387,385},{4... | collective-permute-start | bytes 1572872 | tf_op jit(solution)/shard_map/ppermute | solution.py:82
  69.1 0.1 ne.169
  69.7 2.9 %collective-permute-start.11 = (bf16[1024,256]{1,0:T(8,128)(2,1)S(1)}, bf16[1024,256]{1,0:T(8,128)(2,1)}, u32[]{:S(2)}, u32[]{:S(2)}) collective-permute-start(bf16[1024,256]{1,0:T(8,128)(2,1)S(1)} %collective-permute-done.rest_4_), channel_id=1, source_target_pairs={{0,1},{1,0},{2,3},{3,2},{4,5},{5,4},{6,7},{7,6},{8,9},{9,8},{10,11... | collective-permute-start | bytes 1572872 | tf_op jit(solution)/shard_map/ppermute | solution.py:149
  72.6 1.9 %collective-permute-start.14 = (bf16[1024,256]{1,0:T(8,128)(2,1)S(1)}, bf16[1024,256]{1,0:T(8,128)(2,1)}, u32[]{:S(2)}, u32[]{:S(2)}) collective-permute-start(bf16[1024,256]{1,0:T(8,128)(2,1)S(1)} %collective-permute-done.3.rest_7_), channel_id=1, source_target_pairs={{0,1},{1,0},{2,3},{3,2},{4,5},{5,4},{6,7},{7,6},{8,9},{9,8},{10,11... | collective-permute-start | bytes 1572872 | tf_op jit(solution)/shard_map/ppermute | solution.py:149
  74.5 2.4 %collective-permute-start.13 = (bf16[1024,256]{1,0:T(8,128)(2,1)}, bf16[1024,256]{1,0:T(8,128)(2,1)}, u32[]{:S(2)}, u32[]{:S(2)}) collective-permute-start(bf16[1024,256]{1,0:T(8,128)(2,1)} %collective-permute-done.6.rest_6_), channel_id=1, source_target_pairs={{0,1},{1,0},{2,3},{3,2},{4,5},{5,4},{6,7},{7,6},{8,9},{9,8},{10,11... | collective-permute-start | bytes 1572872 | tf_op jit(solution)/shard_map/ppermute | solution.py:149
  76.9 6.0 %collective-permute-done.1.rest_1_ = bf16[1024,256]{1,0:T(8,128)(2,1)} collective-permute-done((bf16[1024,256]{1,0:T(8,128)(2,1)S(1)}, bf16[1024,256]{1,0:T(8,128)(2,1)}, u32[]{:S(2)}, u32[]{:S(2)}) %collective-permute-start.1) | collective-permute-done | bytes 524320 | tf_op jit(solution)/shard_map/ppermute | solution.py:82
  83.0 2.7 %collective-permute-start.8 = (bf16[1024,256]{1,0:T(8,128)(2,1)}, bf16[1024,256]{1,0:T(8,128)(2,1)}, u32[]{:S(2)}, u32[]{:S(2)}) collective-permute-start(bf16[1024,256]{1,0:T(8,128)(2,1)} %collective-permute-done.1.rest_1_), channel_id=1, source_target_pairs={{0,1},{1,0},{2,3},{3,2},{4,5},{5,4},{6,7},{7,6},{8,9},{9,8},{10,11... | collective-permute-start | bytes 1572872 | tf_op jit(solution)/shard_map/ppermute | solution.py:149
  85.7 1.9 %collective-permute-start.10 = (bf16[1024,256]{1,0:T(8,128)(2,1)}, bf16[1024,256]{1,0:T(8,128)(2,1)}, u32[]{:S(2)}, u32[]{:S(2)}) collective-permute-start(bf16[1024,256]{1,0:T(8,128)(2,1)} %collective-permute-done.4.rest_3_), channel_id=1, source_target_pairs={{0,1},{1,0},{2,3},{3,2},{4,5},{5,4},{6,7},{7,6},{8,9},{9,8},{10,11... | collective-permute-start | bytes 1572872 | tf_op jit(solution)/shard_map/ppermute | solution.py:149
  87.9 1.9 %collective-permute-done.10.rest_11_ = bf16[1024,256]{1,0:T(8,128)(2,1)} collective-permute-done((bf16[1024,256]{1,0:T(8,128)(2,1)}, bf16[1024,256]{1,0:T(8,128)(2,1)}, u32[]{:S(2)}, u32[]{:S(2)}) %collective-permute-start.10) | collective-permute-done | bytes 524320 | tf_op jit(solution)/shard_map/ppermute | solution.py:149
  89.8 6.9 %all-gather.2.cloned.1.call-done.left_ref = bf16[288,8192]{1,0:T(8,128)(2,1)} async-done(((bf16[24,8192]{1,0:T(8,128)(2,1)}), bf16[288,8192]{1,0:T(8,128)(2,1)}) %all-gather.2.cloned.1.call-update) | async-done | bytes 4718608 | tf_op jit(solution)/shard_map/all_gather | solution.py:181
  96.7 6.6 %shard_map.57 = bf16[1536,128]{1,0:T(8,128)(2,1)S(1)} custom-call(s32[8,3]{1,0:T(8,128)S(1)} %stack.127.place_ref, s32[1,288]{1,0:T(1,128)S(1)} %fusion.3.source_ref, bf16[288,8192]{1,0:T(8,128)(2,1)} %all-gather.2.cloned.1.call-done.left_ref, bf16[1024,256]{1,0:T(8,128)(2,1)} %bitcast.50, bf16[1024,256]{1,0:T(8,128)(2,1)} %collective-permute-done.1.rest_1_, ...), custom_call_target="tpu_custom_call" | custom-call | flops 2415919104 | bytes 9437184 | tf_op jit(solution)/shard_map/pallas_call | solution.py:194
  103.3 27.4 %all_to_all.21 = bf16[64,24,128]{2,1,0:T(8,128)(2,1)S(1)} all-to-all(bf16[64,24,128]{2,1,0:T(8,128)(2,1)S(1)} %bitcast.43), channel_id=1, replica_groups=mesh['xh'=2,'z'=12,'yq'=4,'yb'=2,'xl'=2,'core'=2] {'xh','yq','yb','xl','..., dimensions={0} | all-to-all | bytes 786432 | tf_op jit(solution)/shard_map/all_to_all | solution.py:211
  130.7 0.2 convert_reduce_fusion
  131.0 0.8 reshape.103
  (45 shorter events, 1.3 us)
Async XLA Ops:
  6.5 44.8 %copy-start.6 = (s32[72]{0:T(128)S(1)}, s32[72]{0:T(128)}, u32[]{:S(2)}) copy-start(s32[72]{0:T(128)} %param.9) | copy-start | bytes 868
  6.5 90.2 %all-gather.2.cloned.1.call-start = ((), (), s32[]{:S(2)}) async-start(), calls=%async_computation.2 | async-start | bytes 5111808 | tf_op jit(solution)/shard_map/all_gather | solution.py:181
  33.0 63.7 %copy-start = (bf16[2,512,256]{2,1,0:T(8,128)(2,1)}, bf16[2,512,256]{2,1,0:T(8,128)(2,1)S(1)}, u32[]{:S(2)}) copy-start(bf16[2,512,256]{2,1,0:T(8,128)(2,1)S(1)} %copy.20) | copy-start | bytes 1572868
  33.0 14.1 %collective-permute-start.2 = (bf16[1024,256]{1,0:T(8,128)(2,1)S(1)}, bf16[1024,256]{1,0:T(8,128)(2,1)S(1)}, u32[]{:S(2)}, u32[]{:S(2)}) collective-permute-start(bf16[1024,256]{1,0:T(8,128)(2,1)S(1)} %bitcast.46), channel_id=1, source_target_pairs={{0,4},{4,0},{1,5},{5,1},{2,6},{6,2},{3,7},{7,3},{8,12},{12,8},{9,1... | collective-permute-start | bytes 1572872 | tf_op jit(solution)/shard_map/ppermute | solution.py:141
  35.7 19.2 %collective-permute-start.7 = (bf16[1024,256]{1,0:T(8,128)(2,1)S(1)}, bf16[1024,256]{1,0:T(8,128)(2,1)S(1)}, u32[]{:S(2)}, u32[]{:S(2)}) collective-permute-start(bf16[1024,256]{1,0:T(8,128)(2,1)S(1)} %bitcast.47), channel_id=1, source_target_pairs={{0,1},{1,0},{2,3},{3,2},{4,5},{5,4},{6,7},{7,6},{8,9},{9,8},{10,11... | collective-permute-start | bytes 1572872 | tf_op jit(solution)/shard_map/ppermute | solution.py:149
  38.0 19.3 %collective-permute-start.5 = (bf16[1024,256]{1,0:T(8,128)(2,1)S(1)}, bf16[1024,256]{1,0:T(8,128)(2,1)S(1)}, u32[]{:S(2)}, u32[]{:S(2)}) collective-permute-start(bf16[1024,256]{1,0:T(8,128)(2,1)S(1)} %bitcast.48), channel_id=1, source_target_pairs={{0,386},{2,0},{384,2},{386,384},{1,387},{3,1},{385,3},{387,385},{4... | collective-permute-start | bytes 1572872 | tf_op jit(solution)/shard_map/ppermute | solution.py:82
  41.1 18.5 %collective-permute-start = (bf16[1024,256]{1,0:T(8,128)(2,1)S(1)}, bf16[1024,256]{1,0:T(8,128)(2,1)S(1)}, u32[]{:S(2)}, u32[]{:S(2)}) collective-permute-start(bf16[1024,256]{1,0:T(8,128)(2,1)S(1)} %bitcast.49), channel_id=1, source_target_pairs={{0,2},{2,384},{384,386},{386,0},{1,3},{3,385},{385,387},{387,1},{4... | collective-permute-start | bytes 1572872 | tf_op jit(solution)/shard_map/ppermute | solution.py:82
  47.2 49.6 %copy-start.1 = (bf16[1024,256]{1,0:T(8,128)(2,1)}, bf16[1024,256]{1,0:T(8,128)(2,1)S(1)}, u32[]{:S(2)}) copy-start(bf16[1024,256]{1,0:T(8,128)(2,1)S(1)} %collective-permute-done.2.rest_2_) | copy-start | bytes 1572868
  47.2 17.6 %collective-permute-start.3 = (bf16[1024,256]{1,0:T(8,128)(2,1)S(1)}, bf16[1024,256]{1,0:T(8,128)(2,1)S(1)}, u32[]{:S(2)}, u32[]{:S(2)}) collective-permute-start(bf16[1024,256]{1,0:T(8,128)(2,1)S(1)} %collective-permute-done.2.rest_2_), channel_id=1, source_target_pairs={{0,386},{2,0},{384,2},{386,384},{1,387},{3,1},{385,3},{387,385},{4... | collective-permute-start | bytes 1572872 | tf_op jit(solution)/shard_map/ppermute | solution.py:82
  51.7 20.8 %collective-permute-start.9 = (bf16[1024,256]{1,0:T(8,128)(2,1)S(1)}, bf16[1024,256]{1,0:T(8,128)(2,1)}, u32[]{:S(2)}, u32[]{:S(2)}) collective-permute-start(bf16[1024,256]{1,0:T(8,128)(2,1)S(1)} %collective-permute-done.2.rest_2_), channel_id=1, source_target_pairs={{0,1},{1,0},{2,3},{3,2},{4,5},{5,4},{6,7},{7,6},{8,9},{9,8},{10,11... | collective-permute-start | bytes 1572872 | tf_op jit(solution)/shard_map/ppermute | solution.py:149
  55.0 41.8 %copy-start.2 = (bf16[1024,256]{1,0:T(8,128)(2,1)}, bf16[1024,256]{1,0:T(8,128)(2,1)S(1)}, u32[]{:S(2)}) copy-start(bf16[1024,256]{1,0:T(8,128)(2,1)S(1)} %collective-permute-done.7.rest_8_) | copy-start | bytes 1572868
  55.0 19.5 %collective-permute-start.6 = (bf16[1024,256]{1,0:T(8,128)(2,1)S(1)}, bf16[1024,256]{1,0:T(8,128)(2,1)}, u32[]{:S(2)}, u32[]{:S(2)}) collective-permute-start(bf16[1024,256]{1,0:T(8,128)(2,1)S(1)} %collective-permute-done.2.rest_2_), channel_id=1, source_target_pairs={{0,2},{2,384},{384,386},{386,0},{1,3},{3,385},{385,387},{387,1},{4... | collective-permute-start | bytes 1572872 | tf_op jit(solution)/shard_map/ppermute | solution.py:82
  57.3 39.4 %copy-start.3 = (bf16[1024,256]{1,0:T(8,128)(2,1)}, bf16[1024,256]{1,0:T(8,128)(2,1)S(1)}, u32[]{:S(2)}) copy-start(bf16[1024,256]{1,0:T(8,128)(2,1)S(1)} %collective-permute-done.5.rest_5_) | copy-start | bytes 1572868
  57.3 12.3 %collective-permute-start.12 = (bf16[1024,256]{1,0:T(8,128)(2,1)S(1)}, bf16[1024,256]{1,0:T(8,128)(2,1)}, u32[]{:S(2)}, u32[]{:S(2)}) collective-permute-start(bf16[1024,256]{1,0:T(8,128)(2,1)S(1)} %collective-permute-done.5.rest_5_), channel_id=1, source_target_pairs={{0,1},{1,0},{2,3},{3,2},{4,5},{5,4},{6,7},{7,6},{8,9},{9,8},{10,11... | collective-permute-start | bytes 1572872 | tf_op jit(solution)/shard_map/ppermute | solution.py:149
  59.6 37.2 %copy-start.4 = (bf16[1024,256]{1,0:T(8,128)(2,1)}, bf16[1024,256]{1,0:T(8,128)(2,1)S(1)}, u32[]{:S(2)}) copy-start(bf16[1024,256]{1,0:T(8,128)(2,1)S(1)} %collective-permute-done.rest_4_) | copy-start | bytes 1572868
  59.6 23.4 %collective-permute-start.1 = (bf16[1024,256]{1,0:T(8,128)(2,1)S(1)}, bf16[1024,256]{1,0:T(8,128)(2,1)}, u32[]{:S(2)}, u32[]{:S(2)}) collective-permute-start(bf16[1024,256]{1,0:T(8,128)(2,1)S(1)} %collective-permute-done.rest_4_), channel_id=1, source_target_pairs={{0,2},{2,384},{384,386},{386,0},{1,3},{3,385},{385,387},{387,1},{4... | collective-permute-start | bytes 1572872 | tf_op jit(solution)/shard_map/ppermute | solution.py:82
  64.8 32.0 %copy-start.5 = (bf16[1024,256]{1,0:T(8,128)(2,1)}, bf16[1024,256]{1,0:T(8,128)(2,1)S(1)}, u32[]{:S(2)}) copy-start(bf16[1024,256]{1,0:T(8,128)(2,1)S(1)} %collective-permute-done.3.rest_7_) | copy-start | bytes 1572868
  64.8 20.9 %collective-permute-start.4 = (bf16[1024,256]{1,0:T(8,128)(2,1)S(1)}, bf16[1024,256]{1,0:T(8,128)(2,1)}, u32[]{:S(2)}, u32[]{:S(2)}) collective-permute-start(bf16[1024,256]{1,0:T(8,128)(2,1)S(1)} %collective-permute-done.3.rest_7_), channel_id=1, source_target_pairs={{0,386},{2,0},{384,2},{386,384},{1,387},{3,1},{385,3},{387,385},{4... | collective-permute-start | bytes 1572872 | tf_op jit(solution)/shard_map/ppermute | solution.py:82
  69.7 18.2 %collective-permute-start.11 = (bf16[1024,256]{1,0:T(8,128)(2,1)S(1)}, bf16[1024,256]{1,0:T(8,128)(2,1)}, u32[]{:S(2)}, u32[]{:S(2)}) collective-permute-start(bf16[1024,256]{1,0:T(8,128)(2,1)S(1)} %collective-permute-done.rest_4_), channel_id=1, source_target_pairs={{0,1},{1,0},{2,3},{3,2},{4,5},{5,4},{6,7},{7,6},{8,9},{9,8},{10,11... | collective-permute-start | bytes 1572872 | tf_op jit(solution)/shard_map/ppermute | solution.py:149
  72.6 15.3 %collective-permute-start.14 = (bf16[1024,256]{1,0:T(8,128)(2,1)S(1)}, bf16[1024,256]{1,0:T(8,128)(2,1)}, u32[]{:S(2)}, u32[]{:S(2)}) collective-permute-start(bf16[1024,256]{1,0:T(8,128)(2,1)S(1)} %collective-permute-done.3.rest_7_), channel_id=1, source_target_pairs={{0,1},{1,0},{2,3},{3,2},{4,5},{5,4},{6,7},{7,6},{8,9},{9,8},{10,11... | collective-permute-start | bytes 1572872 | tf_op jit(solution)/shard_map/ppermute | solution.py:149
  74.5 13.4 %collective-permute-start.13 = (bf16[1024,256]{1,0:T(8,128)(2,1)}, bf16[1024,256]{1,0:T(8,128)(2,1)}, u32[]{:S(2)}, u32[]{:S(2)}) collective-permute-start(bf16[1024,256]{1,0:T(8,128)(2,1)} %collective-permute-done.6.rest_6_), channel_id=1, source_target_pairs={{0,1},{1,0},{2,3},{3,2},{4,5},{5,4},{6,7},{7,6},{8,9},{9,8},{10,11... | collective-permute-start | bytes 1572872 | tf_op jit(solution)/shard_map/ppermute | solution.py:149
  83.0 5.0 %collective-permute-start.8 = (bf16[1024,256]{1,0:T(8,128)(2,1)}, bf16[1024,256]{1,0:T(8,128)(2,1)}, u32[]{:S(2)}, u32[]{:S(2)}) collective-permute-start(bf16[1024,256]{1,0:T(8,128)(2,1)} %collective-permute-done.1.rest_1_), channel_id=1, source_target_pairs={{0,1},{1,0},{2,3},{3,2},{4,5},{5,4},{6,7},{7,6},{8,9},{9,8},{10,11... | collective-permute-start | bytes 1572872 | tf_op jit(solution)/shard_map/ppermute | solution.py:149
  85.7 4.1 %collective-permute-start.10 = (bf16[1024,256]{1,0:T(8,128)(2,1)}, bf16[1024,256]{1,0:T(8,128)(2,1)}, u32[]{:S(2)}, u32[]{:S(2)}) collective-permute-start(bf16[1024,256]{1,0:T(8,128)(2,1)} %collective-permute-done.4.rest_3_), channel_id=1, source_target_pairs={{0,1},{1,0},{2,3},{3,2},{4,5},{5,4},{6,7},{7,6},{8,9},{9,8},{10,11... | collective-permute-start | bytes 1572872 | tf_op jit(solution)/shard_map/ppermute | solution.py:149
Sparse Core Ops, SparseCore 0:
  30.8 65.9 all-gather.1
